TPU v7x, 512 devices: a whole 4x4x16 slice. The times are simulated.
512 devices in a mesh: cube: 8 (over x, core), front: 64 (over z, y).
Axes of the slice: x: 4, y: 4, z: 16, core: 2. Of those that a mesh axis runs over, the one named last changes fastest.
Arguments:
- leaf_blocks: float32 [8, 3840, 3840], P('cube', 'front'), may hold values from -8 to 11, as said below
- front_entries: float32 [7, 4096, 256], P(None, 'front'), may hold values from -0.001 to 3
- child_maps: int32 [7, 2, 60], replicated, may hold values from 0 to 63, as said below
Outputs:
- factor_columns: float32 [8, 3, 4096, 256], P('cube', None, 'front')
- top_block: float32 [3840, 3840], P('front')
Inputs may be any that keep to these rules, and one draw needn't show every extreme that they name: `child_maps`: for each node, each of the two rows lists distinct offsets, and the two rows together name every offset from 0 to 63. `leaf_blocks`: each leaf block is symmetric positive definite.
All inputs are finite; a program needn't handle non-finite values.
Results may differ from a plain program's by a relative error of at most 0.00033.
Values may be sent and summed in bfloat16 or wider, within the bound.
No kernel may reach another device: no remote copies, remote signals or barrier semaphores. Data moves between devices by JAX's collectives and lax.ppermute only.
A program may use at most 128 MiB of HBM per device.

v0:
```python
import jax
import jax.numpy as jnp
from jax import lax
from jax.sharding import PartitionSpec as P

PANEL = 256


HIGH = lax.Precision.HIGHEST


def swapped(value, axis, apart):
    mask = 2**apart
    pairs = [(source, source ^ mask) for source in range(lax.axis_size(axis))]
    return lax.ppermute(value, axis, pairs)


def onehot_table(mapping, width):
    return (mapping[:, None] == jnp.arange(width, dtype=jnp.int32)[None, :]).astype(jnp.float32)


def scatter_rows(block, mapping, devices, width):
    block_rows = block.shape[0]
    table = onehot_table(mapping, width)
    grid = block.reshape(block_rows, devices, block_rows)
    widened = jnp.einsum("ubv,vs->usb", grid, table, precision=HIGH)
    placed = jnp.einsum("usb,ut->tsb", widened, table, precision=HIGH)
    return placed.reshape(width, width * devices)


def cholesky_lower(pivot):
    symmetric = jnp.tril(pivot) + jnp.tril(pivot, -1).T
    return jnp.linalg.cholesky(symmetric)


def factor_front(matrix, devices, position, width, panel_rows):
    panel = panel_rows * devices
    trailing = width - panel_rows
    last_col = panel_rows * devices
    local_pivot = matrix[0:panel_rows, 0:last_col]
    gathered = lax.all_gather(local_pivot, "front", axis=0, tiled=True)
    pivot = jnp.transpose(gathered.reshape(devices, panel_rows, panel), (1, 0, 2)).reshape(
        panel, panel
    )
    factor = cholesky_lower(pivot)
    lhs_rows = matrix[panel_rows:, 0:last_col]
    solved = jax.scipy.linalg.solve_triangular(factor, lhs_rows.T, lower=True).T
    rounded = solved.astype(jnp.bfloat16)
    update = jnp.einsum(
        "ip,jp->ij",
        rounded,
        lax.all_gather(rounded, "front", axis=0, tiled=True),
        preferred_element_type=jnp.float32,
    )
    reordered = jnp.transpose(update.reshape(trailing, devices, trailing), (0, 2, 1)).reshape(
        trailing, trailing * devices
    )
    matrix = matrix.at[panel_rows:, last_col:].add(-reordered)
    upper = jnp.zeros((0, panel), jnp.float32)
    middle = lax.dynamic_index_in_dim(
        factor.reshape(panel_rows, devices, panel), position, 1, keepdims=False
    )
    columns = jnp.concatenate([upper, middle, solved], axis=0)
    return (columns, matrix)


def on_device(leaf_blocks, front_entries, child_maps):
    devices = lax.axis_size("front")
    position = lax.axis_index("front")
    subcube = lax.axis_index("cube")
    cube_count = lax.axis_size("cube")
    heights = cube_count.bit_length() - 1
    width = front_entries.shape[1]
    sep_rows = front_entries.shape[2] // devices
    panel_rows = PANEL // devices
    block_rows = leaf_blocks.shape[1]
    current = leaf_blocks[0]
    factors = []
    for height in range(heights):
        sibling = swapped(current, "cube", height)
        side_bit = jnp.right_shift(subcube, height) & 1
        left_block = jnp.where(side_bit == 0, current, sibling)
        right_block = jnp.where(side_bit == 0, sibling, current)
        node = jnp.right_shift(subcube + cube_count, height + 1)
        entries = lax.dynamic_index_in_dim(front_entries, node - 1, 0, keepdims=False)
        mappings = lax.dynamic_index_in_dim(child_maps, node - 1, 0, keepdims=False)
        placed_entries = jnp.transpose(
            entries.reshape(width, devices, sep_rows), (0, 2, 1)
        ).reshape(width, sep_rows * devices)
        zeros_rest = jnp.zeros((width, (width - sep_rows) * devices), jnp.float32)
        matrix = jnp.concatenate([placed_entries, zeros_rest], axis=1)
        matrix = matrix + scatter_rows(left_block, mappings[0], devices, width)
        matrix = matrix + scatter_rows(right_block, mappings[1], devices, width)
        factor_part, matrix = factor_front(matrix, devices, position, width, panel_rows)
        factors.append(factor_part)
        remain = matrix[sep_rows:, sep_rows * devices :].reshape(block_rows, block_rows, devices)
        current = jnp.transpose(remain, (0, 2, 1)).reshape(block_rows, devices * block_rows)
    return (jnp.stack(factors)[None], current)


def solution(mesh):
    in_specs = (P("cube", "front", None), P(None, "front", None), P())
    out_specs = (P("cube", None, "front", None), P("front", None))
    return jax.shard_map(
        on_device, mesh=mesh, in_specs=in_specs, out_specs=out_specs, check_vma=False
    )
```

profile of v0, /device:TPU:1, one launch (start us, length us, event | category | flops | bytes accessed | tf_op | source)
XLA Modules:
  0.0 1033.8 jit_solution(18427782496393358375)
XLA Ops:
  8.5 8.8 collective-permute-start
  21.7 4.3 reshape.238
  26.0 2.9 convolution_bitcast_fusion.5
  28.9 2.4 fusion.10
  34.2 2.9 reshape.240
  37.2 2.9 convolution_bitcast_fusion.4
  40.1 2.9 fusion.8
  47.5 64.5 %all-gather = f32[64,4,256]{2,1,0:T(4,128)S(1)} all-gather(f32[1,4,256]{2,1,0:T(4,128)S(1)} %slice_bitcast_fusion.17), channel_id=1, replica_groups=mesh['cube'=8,'front'=64] {'front'}, dimensions={0}, use_global_device_ids=true | all-gather | bytes 266240 | tf_op jit(solution)/shard_map/all_gather | solution.py:41
  112.5 11.7 %cholesky.172 = f32[128,128]{1,0:T(8,128)S(1)} custom-call(f32[128,128]{1,0:T(8,128)S(1)} %copy.109), custom_call_target="Cholesky" | custom-call | tf_op jit(solution)/shard_map/jit(cholesky)/cholesky | solution.py:33
  124.3 9.8 custom-call.15
  134.8 11.7 %cholesky.189 = f32[128,128]{1,0:T(8,128)S(1)} custom-call(f32[128,128]{1,0:T(8,128)S(1)} %copy.111), custom_call_target="Cholesky" | custom-call | tf_op jit(solution)/shard_map/jit(cholesky)/cholesky | solution.py:33
  148.5 4.0 while.9
  152.6 19.7 %custom-call.16 = f32[2,128,128]{1,2,0:T(8,128)S(1)} custom-call(f32[2,128,128]{2,1,0:T(8,128)S(1)} %get-tuple-element.60), custom_call_target="InvertDiagBlocksLowerTriangular" | custom-call | tf_op jit(solution)/shard_map/jit(_solve_triangular)/triangular_solve | solution.py:47
  173.6 146.1 %all-gather.10.cloned.1.call-done = bf16[64,60,256]{2,1,0:T(8,128)(2,1)} async-done(((bf16[1,60,256]{2,1,0:T(8,128)(2,1)}), bf16[64,60,256]{2,1,0:T(8,128)(2,1)}) %all-gather.10.cloned.1.call-update) | async-done | bytes 1966096 | tf_op jit(solution)/shard_map/all_gather | solution.py:52
  319.7 2.5 reshape.297
  323.8 4.1 neg.37
  327.9 1.9 copy.114
  329.8 2.1 neg.39
  333.0 2.0 reshape.247
  335.0 1.9 copy.115
  336.9 2.8 reshape.248
  339.7 3.1 collective-permute-start.1
  343.2 12.1 %collective-permute-done.1 = f32[60,3840]{1,0:T(8,128)S(1)} collective-permute-done((f32[60,3840]{1,0:T(8,128)S(1)}, f32[60,3840]{1,0:T(8,128)S(1)}, u32[]{:S(2)}, u32[]{:S(2)}) %collective-permute-start.1) | collective-permute-done | bytes 921632 | tf_op jit(solution)/shard_map/ppermute | solution.py:15
  356.4 4.5 reshape.249
  360.9 2.9 convolution_bitcast_fusion.3
  363.8 2.4 fusion.6
  369.1 2.9 reshape.251
  372.0 2.9 convolution_bitcast_fusion.2
  375.0 2.6 fusion.4
  382.1 62.1 %all-gather.2 = f32[64,4,256]{2,1,0:T(4,128)S(1)} all-gather(f32[1,4,256]{2,1,0:T(4,128)S(1)} %slice_bitcast_fusion.16), channel_id=1, replica_groups=mesh['cube'=8,'front'=64] {'front'}, dimensions={0}, use_global_device_ids=true | all-gather | bytes 266240 | tf_op jit(solution)/shard_map/all_gather | solution.py:41
  444.7 11.7 %cholesky.206 = f32[128,128]{1,0:T(8,128)S(1)} custom-call(f32[128,128]{1,0:T(8,128)S(1)} %copy.124), custom_call_target="Cholesky" | custom-call | tf_op jit(solution)/shard_map/jit(cholesky)/cholesky | solution.py:33
  457.1 9.8 custom-call.17
  467.6 11.7 %cholesky.223 = f32[128,128]{1,0:T(8,128)S(1)} custom-call(f32[128,128]{1,0:T(8,128)S(1)} %copy.126), custom_call_target="Cholesky" | custom-call | tf_op jit(solution)/shard_map/jit(cholesky)/cholesky | solution.py:33
  482.0 4.2 while.10
  486.2 19.7 %custom-call.18 = f32[2,128,128]{1,2,0:T(8,128)S(1)} custom-call(f32[2,128,128]{2,1,0:T(8,128)S(1)} %get-tuple-element.61), custom_call_target="InvertDiagBlocksLowerTriangular" | custom-call | tf_op jit(solution)/shard_map/jit(_solve_triangular)/triangular_solve | solution.py:47
  507.2 155.4 %all-gather.12.cloned.1.call-done = bf16[64,60,256]{2,1,0:T(8,128)(2,1)} async-done(((bf16[1,60,256]{2,1,0:T(8,128)(2,1)}), bf16[64,60,256]{2,1,0:T(8,128)(2,1)}) %all-gather.12.cloned.1.call-update) | async-done | bytes 1966096 | tf_op jit(solution)/shard_map/all_gather | solution.py:52
  662.6 2.5 reshape.301
  666.8 4.1 neg.41
  670.9 1.9 copy.129
  672.8 2.1 neg.43
  675.9 2.0 reshape.258
  677.9 1.9 copy.130
  679.8 2.9 reshape.259
  682.7 4.6 collective-permute-start.2
  688.5 11.3 %collective-permute-done.2 = f32[60,3840]{1,0:T(8,128)S(1)} collective-permute-done((f32[60,3840]{1,0:T(8,128)S(1)}, f32[60,3840]{1,0:T(8,128)S(1)}, u32[]{:S(2)}, u32[]{:S(2)}) %collective-permute-start.2) | collective-permute-done | bytes 921632 | tf_op jit(solution)/shard_map/ppermute | solution.py:15
  700.9 4.2 reshape.260
  705.1 2.9 convolution_bitcast_fusion.1
  708.1 2.4 fusion.2
  713.4 2.9 reshape.262
  716.3 2.9 convolution_bitcast_fusion
  719.2 2.6 fusion
  726.4 62.1 %all-gather.4 = f32[64,4,256]{2,1,0:T(4,128)S(1)} all-gather(f32[1,4,256]{2,1,0:T(4,128)S(1)} %slice_bitcast_fusion.15), channel_id=1, replica_groups=mesh['cube'=8,'front'=64] {'front'}, dimensions={0}, use_global_device_ids=true | all-gather | bytes 266240 | tf_op jit(solution)/shard_map/all_gather | solution.py:41
  789.0 11.7 %cholesky.240 = f32[128,128]{1,0:T(8,128)S(1)} custom-call(f32[128,128]{1,0:T(8,128)S(1)} %cholesky.276), custom_call_target="Cholesky" | custom-call | tf_op jit(solution)/shard_map/jit(cholesky)/cholesky | solution.py:33
  801.4 9.8 custom-call.19
  811.7 11.7 %cholesky.257 = f32[128,128]{1,0:T(8,128)S(1)} custom-call(f32[128,128]{1,0:T(8,128)S(1)} %convolution_subtract_fusion), custom_call_target="Cholesky" | custom-call | tf_op jit(solution)/shard_map/jit(cholesky)/cholesky | solution.py:33
  825.5 4.3 while.11
  829.7 19.7 %custom-call.20 = f32[2,128,128]{1,2,0:T(8,128)S(1)} custom-call(f32[2,128,128]{2,1,0:T(8,128)S(1)} %get-tuple-element.62), custom_call_target="InvertDiagBlocksLowerTriangular" | custom-call | tf_op jit(solution)/shard_map/jit(_solve_triangular)/triangular_solve | solution.py:47
  852.3 153.8 %all-gather.14.cloned.1.call-done = bf16[64,60,256]{2,1,0:T(8,128)(2,1)} async-done(((bf16[1,60,256]{2,1,0:T(8,128)(2,1)}), bf16[64,60,256]{2,1,0:T(8,128)(2,1)}) %all-gather.14.cloned.1.call-update) | async-done | bytes 1966096 | tf_op jit(solution)/shard_map/all_gather | solution.py:52
  1006.1 2.5 reshape.305
  1010.3 4.1 neg.45
  1014.4 1.9 copy.139
  1016.3 2.1 neg.47
  1019.4 2.0 reshape.267
  1023.3 3.5 reshape.268
  (158 shorter events, 66.0 us)
Async XLA Ops:
  7.2 13.4 %copy-start = (f32[1,60,3840]{2,0,1:T(1,128)S(1)}, f32[1,60,3840]{2,0,1:T(1,128)}, u32[]{:S(2)}) copy-start(f32[1,60,3840]{2,0,1:T(1,128)} %param.12) | copy-start | bytes 2764804
  7.2 312.5 %all-gather.10.cloned.1.call-start = ((), (), s32[]{:S(2)}) async-start(), calls=%async_computation | async-start | bytes 2129920 | tf_op jit(solution)/shard_map/all_gather | solution.py:52
  8.5 12.0 %collective-permute-start = (f32[60,3840]{1,0:T(8,128)S(1)}, f32[60,3840]{1,0:T(8,128)S(1)}, u32[]{:S(2)}, u32[]{:S(2)}) collective-permute-start(f32[60,3840]{1,0:T(8,128)S(1)} %bitcast.260), channel_id=1, source_target_pairs={{0,64},{64,0},{128,192},{192,128},{256,320},{320,256},{384,448},{4... | collective-permute-start | bytes 2764808 | tf_op jit(solution)/shard_map/ppermute | solution.py:15
  112.2 36.2 %copy-start.3 = (s32[2]{0:T(128)S(1)}, s32[2]{0:T(128)}, u32[]{:S(2)}) copy-start(s32[2]{0:T(128)} %iota_multiply_fusion) | copy-start | bytes 28
  173.5 489.1 %all-gather.12.cloned.1.call-start = ((), (), s32[]{:S(2)}) async-start(), calls=%async_computation.1 | async-start | bytes 2129920 | tf_op jit(solution)/shard_map/all_gather | solution.py:52
  339.7 15.6 %collective-permute-start.1 = (f32[60,3840]{1,0:T(8,128)S(1)}, f32[60,3840]{1,0:T(8,128)S(1)}, u32[]{:S(2)}, u32[]{:S(2)}) collective-permute-start(f32[60,3840]{1,0:T(8,128)S(1)} %reshape.248), channel_id=1, source_target_pairs={{0,128},{64,192},{128,0},{192,64},{256,384},{320,448},{384,256},{4... | collective-permute-start | bytes 2764808 | tf_op jit(solution)/shard_map/ppermute | solution.py:15
  507.2 499.0 %all-gather.14.cloned.1.call-start = ((), (), s32[]{:S(2)}) async-start(), calls=%async_computation.2 | async-start | bytes 2129920 | tf_op jit(solution)/shard_map/all_gather | solution.py:52
  679.8 8.3 copy-start.1
  682.7 17.1 %collective-permute-start.2 = (f32[60,3840]{1,0:T(8,128)S(1)}, f32[60,3840]{1,0:T(8,128)S(1)}, u32[]{:S(2)}, u32[]{:S(2)}) collective-permute-start(f32[60,3840]{1,0:T(8,128)S(1)} %reshape.259), channel_id=1, source_target_pairs={{0,256},{64,320},{128,384},{192,448},{256,0},{320,64},{384,128},{4... | collective-permute-start | bytes 2764808 | tf_op jit(solution)/shard_map/ppermute | solution.py:15
  724.7 64.0 %copy-start.2 = (pred[256,256]{1,0:T(8,128)(4,1)S(1)}, pred[256,256]{1,0:T(8,128)(4,1)}, u32[]{:S(2)}) copy-start(pred[256,256]{1,0:T(8,128)(4,1)} %copy.136) | copy-start | bytes 196612
Sparse Core Ops, SparseCore 0:
  173.6 146.0 all-gather.9
  507.3 155.3 all-gather.11
  850.8 155.3 all-gather.13
where the time goes:
time: 1050 us; the launch traced here: 1030 us
  waiting for transfers between devices  479 us (46%)
  blocking collectives  189 us (18%)
  other arithmetic  178 us (17%)
  local copies, waits for them, and re-layouts  111 us (11%)
  matrix products  41.4 us (4%)
  between operations  18.8 us (2%)
  starting transfers between devices  16.6 us (2%)
    all_gather x3, waiting for transfers between devices, factor_front(): lax.all_gather(rounded, 'front', axis=0, tiled=True)  455 us
    all_gather x3, blocking collectives, factor_front(): gathered = lax.all_gather(local_pivot, 'front', axis=0, tiled=True)  189 us
    another operation x20, other arithmetic, cholesky_lower(): return jnp.linalg.cholesky(symmetric)  103 us
    another operation x7, other arithmetic, factor_front(): solved = jax.scipy.linalg.solve_triangular(factor, lhs_rows.T, lower=True).T  60.4 us
    neg x9, local copies, waits for them, and re-layouts, factor_front(): matrix = matrix.at[panel_rows:, last_col:].add(-reordered)  24.2 us
    ppermute x3, waiting for transfers between devices, swapped(): return lax.ppermute(value, axis, pairs)  23.4 us
    reshape x6, local copies, waits for them, and re-layouts, scatter_rows(): grid = block.reshape(block_rows, devices, block_rows)  21.7 us
  transfers between devices with their start and end apart: 6, of which 5 were waited for; matrix products, arithmetic and copies ran while one was open for 1% of the time, Pallas kernels for 0%

commit v1 on v0

v1 whole, which is shorter than its diff:
```python
import functools

import jax
import jax.numpy as jnp
from jax import lax
from jax.experimental import pallas as pl
from jax.experimental.pallas import tpu as pltpu
from jax.sharding import PartitionSpec as P

F32 = jnp.float32
BF16 = jnp.bfloat16
HIGH = lax.Precision.HIGHEST

N = 64
Z, Y = 16, 4
WIDTH = 64
KEEP = 60
PAN = 256
BLK = 32

Z_GROUPS = [[Y * z + y for z in range(Z)] for y in range(Y)]
Y_GROUPS = [[Y * z + y for y in range(Y)] for z in range(Z)]
CORE_GROUPS = [[0, 1], [2, 3], [4, 5], [6, 7]]
X_GROUPS = [[0, 2, 4, 6], [1, 3, 5, 7]]

VMEM = pl.BlockSpec(memory_space=pltpu.VMEM)
SMEM = pl.BlockSpec(memory_space=pltpu.SMEM)


def iota(shape, dim):
    return lax.broadcasted_iota(jnp.int32, shape, dim)


def split3(x):
    high = x.astype(BF16)
    rest = x - high.astype(F32)
    mid = rest.astype(BF16)
    low = (rest - mid.astype(F32)).astype(BF16)
    return high, mid, low


def dot(a, b, dims):
    return lax.dot_general(a, b, (dims, ((), ())), preferred_element_type=F32)


NN = ((1,), (0,))
NT = ((1,), (1,))
TN = ((0,), (0,))


def onehot_rows(row):
    return (iota((WIDTH, WIDTH), 0) == row).astype(BF16)


def compose(a, b):
    return dot(a, b, NN).astype(BF16)


def tail_table():
    return (iota((WIDTH, WIDTH), 0) + 4 == iota((WIDTH, WIDTH), 1)).astype(BF16)


def unpack(packed):
    full = jnp.concatenate([packed, pltpu.roll(packed, 64, 1)], axis=0)
    return jnp.where(iota(full.shape, 1) < WIDTH, full, 0.0)


def factor(a_ref, width):
    for b in range(PAN // BLK):
        j0 = b * BLK
        lo = j0 // 128 * 128
        rows = a_ref[j0 : j0 + BLK, lo:width]
        rid = iota((BLK, 1), 0)
        for i in range(BLK):
            jl = j0 - lo + i
            col = rows[:, jl : jl + 1]
            inv = 1.0 / rows[i : i + 1, jl : jl + 1]
            scale = jnp.where(rid > i, col * inv, 0.0)
            rows = rows - scale * rows[i : i + 1, :]
        head = rows[:, 0:128]
        diag = jnp.sum(
            jnp.where(iota(head.shape, 1) == iota(head.shape, 0) + (j0 - lo), head, 0.0),
            axis=1,
            keepdims=True,
        )
        root = lax.rsqrt(diag)
        root = root * (1.5 - 0.5 * diag * root * root)
        rows = rows * root
        a_ref[j0 : j0 + BLK, lo:width] = rows
        r0 = j0 + BLK
        if r0 < PAN:
            nlo = r0 // 128 * 128
            h, m, l = split3(rows[:, nlo - lo :])
            n = PAN - nlo
            left = jnp.concatenate([h, h, m, h, l, m], axis=0)[:, :n]
            right = jnp.concatenate([h, m, h, l, h, m], axis=0)
            done = dot(left, right, TN)
            a_ref[r0:PAN, nlo:width] -= done[r0 - nlo :, :]


def own_columns(own, position):
    p = iota(own.shape, 0)
    t = iota(own.shape, 1)
    kept = jnp.where((t < 4) & (p > t * N + position), 0.0, own)
    return jnp.transpose(kept)[:WIDTH, :]


def rows_of(g_ref, part, first, count, out_ref):
    for r in range(count):
        for y in range(Y):
            for half in range(2):
                out_ref[half, pl.ds(r * N + y, Z, stride=Y), :] = g_ref[
                    part, y, pl.ds(half * 12 + first + r, Z, stride=24), :
                ]


def joined(r, first, last):
    return jnp.concatenate([r[0, first:last, :], r[1, first:last, :]], axis=1)


def symmetric(g):
    return jnp.where(iota(g.shape, 1) >= iota(g.shape, 0), jnp.transpose(g), g)


def leaf_kernel(sc, maps_s, maps_v, leaf, entries, e_ref, ent_ref, ta_ref, tb_ref, big, inv):
    cube = sc[3]

    @pl.loop(0, 72)
    def _(k):
        inv[k] = -1

    @pl.loop(0, KEEP)
    def _(v):
        a0 = maps_s[0, v]
        a1 = maps_s[1, a0]
        a2 = maps_s[2, jnp.maximum(a1, 0)]
        code = jnp.where(a0 < 4, a0, jnp.where(a1 < 4, 4 + a1, 8 + a2))
        inv[code] = v

    t0 = onehot_rows(maps_v[0:1, :])
    t1 = compose(onehot_rows(maps_v[1:2, :]), t0)
    t2 = compose(onehot_rows(maps_v[2:3, :]), t1)
    tt = compose(tail_table(), t2)
    table = jnp.concatenate([tt, tt, t0, t0, t1, t1, t2, t2], axis=0).astype(F32)
    table = jnp.transpose(table).astype(BF16)
    table = jnp.concatenate([table, table, table], axis=0)

    pad = jnp.zeros((WIDTH - KEEP, 256), F32)
    for j in range(3840 // 256):
        block = leaf[0, :, j * 256 : (j + 1) * 256]
        block = jnp.concatenate([block, pad], axis=0)
        parts = jnp.concatenate(split3(block), axis=0)
        turned = dot(parts, table, TN)
        for f in range(4):
            big[f, j * 256 : (j + 1) * 256, :] = turned[:, f * 128 : (f + 1) * 128]

    lane = iota((N, 128), 1)
    for h in range(3):
        for k in range(2):
            pieces = []
            for side in range(2):
                v = inv[h * 4 + side * 2 + k]
                got = big[1 + h, pl.ds(jnp.maximum(v, 0), N, stride=KEEP), :]
                pieces.append(jnp.where(v >= 0, got, 0.0))
            e_ref[h, k * N : (k + 1) * N, :] = jnp.where(lane < WIDTH, pieces[0], pieces[1])

    half_lane = iota((N // 2, 128), 1)
    for s in range(8):
        r = jnp.bitwise_xor(s, cube)
        slot = jnp.bitwise_and(r, 2) + jnp.right_shift(r, 2)
        for i in range(8):
            dst = pl.ds(slot * 256 + i, N // 2, stride=8)
            if s * 8 + i < KEEP:
                v = inv[12 + s * 8 + i]
                start = jnp.maximum(v, 0)
                low = big[0, pl.ds(start, N // 2, stride=KEEP), :]
                high = big[0, pl.ds(start + KEEP * N // 2, N // 2, stride=KEEP), :]
                got = jnp.where(v >= 0, jnp.where(half_lane < WIDTH, low, high), 0.0)
            else:
                got = jnp.zeros((N // 2, 128), F32)

            @pl.when(jnp.bitwise_and(r, 1) == 0)
            def _():
                ta_ref[dst, :] = got

            @pl.when(jnp.bitwise_and(r, 1) == 1)
            def _():
                tb_ref[dst, :] = got

    p = iota((PAN, PAN), 0)
    order = (iota((PAN, PAN), 1) == (p % N) * 4 + p // N).astype(BF16)
    for h in range(3):
        e = entries[sc[h]]
        e3 = split3(e)
        placed = dot(order, e3[0], NT) + dot(order, e3[1], NT) + dot(order, e3[2], NT)
        ent_ref[h] = jnp.concatenate([placed[:128], placed[128:]], axis=1)


def pick_kernel(sc, maps_v, e0, e12, ent, x_ref, send_ref):
    core = sc[5]
    pair = sc[6]
    x0 = e0[0, 0] + e0[1, 0] + ent[0]
    q = [e12[x] for x in range(4)]
    low, high = q[0] + q[1], q[2] + q[3]
    x1 = jnp.where(pair == 0, low[0], high[0]) + ent[1]
    x2 = low[1] + high[1] + ent[2]
    x_ref[0], x_ref[1], x_ref[2] = x0, x1, x2
    m1 = onehot_rows(maps_v[1:2, :])
    m2 = onehot_rows(maps_v[2:3, :])
    m21 = compose(m2, m1)
    eye = (iota((WIDTH, WIDTH), 0) == iota((WIDTH, WIDTH), 1)).astype(BF16)

    def first4(tables):
        four = [x.astype(F32)[:8] for x in tables]
        while len(four) < 3:
            four.append(jnp.zeros_like(four[0]))
        return jnp.concatenate(four, axis=0)

    zero = jnp.zeros((8, WIDTH), F32)
    s0 = jnp.where(core == 0, first4([eye, m1, m21]), 0.0)
    s1 = jnp.where(core == 1, first4([eye, m2]), 0.0)
    s2 = jnp.where(
        core == 1, jnp.concatenate([zero, zero, eye.astype(F32)[:8]], axis=0), 0.0
    )
    z = jnp.zeros((24, PAN), F32)
    for s, x in ((s0, x0), (s1, x1), (s2, x2)):
        full = jnp.concatenate([x, pltpu.roll(x, 64, 1)], axis=0)[:, :WIDTH]
        table = s.astype(BF16)
        h, m, l = split3(full)
        z = z + (dot(table, h, NT) + dot(table, m, NT) + dot(table, l, NT))
    rows = jnp.concatenate([z[0:4], z[8:12], z[16:20]], axis=0)
    rows = jnp.concatenate([rows[:, :128], rows[:, 128:]], axis=0)
    for k in range(Z):
        send_ref[k] = rows


def level0_kernel(sc, maps_v, g, x, f_ref, v_ref, a, r):
    rows_of(g, 0, 0, 12, r)
    a[:, 0:256] = symmetric(joined(r, 0, 256))
    a[:, 256:768] = jnp.transpose(joined(r, 256, 768))
    a[:, 768:896] = unpack(x[0])
    factor(a, 896)
    own = a[:, 768:896]
    f_ref[...] = own_columns(own, sc[4])
    m1 = onehot_rows(maps_v[1:2, :])
    v_ref[:, 0:512] = a[:, 256:768].astype(BF16)
    moved = dot(own[:, :WIDTH].astype(BF16), m1, NT)
    v_ref[:, 512:640] = jnp.concatenate([moved, jnp.zeros_like(moved)], axis=1).astype(BF16)


def level1_kernel(sc, maps_v, g, x, v0, v0s, f_ref, d_ref, w_ref, dh_ref, wh_ref, a, r):
    rows_of(g, 1, 0, 8, r)
    a[:, 0:256] = symmetric(joined(r, 0, 256))
    a[:, 256:512] = jnp.transpose(joined(r, 256, 512))
    a[:, 512:640] = unpack(x[1])
    mine, other = v0[...], v0s[...]
    a[...] -= dot(mine[:, 0:256], mine, TN) + dot(other[:, 0:256], other, TN)
    factor(a, 640)
    own = a[:, 512:640]
    f_ref[...] = own_columns(own, sc[4])
    m2 = onehot_rows(maps_v[2:3, :])
    moved = [
        dot(mine[:, 512 : 512 + WIDTH], m2, NT).astype(BF16),
        dot(other[:, 512 : 512 + WIDTH], m2, NT).astype(BF16),
        dot(own[:, :WIDTH].astype(BF16), m2, NT).astype(BF16),
    ]
    cols = [mine[:, 256:512], other[:, 256:512], a[:, 256:512].astype(BF16)]
    zero = jnp.zeros((PAN, WIDTH), F32)
    w = jnp.concatenate([m.astype(F32) for m in moved] + [zero], axis=1).astype(BF16)
    w_ref[...] = w
    total = jnp.zeros((PAN, 384), F32)
    for c, m in zip(cols, moved):
        right = jnp.concatenate(
            [c.astype(F32), m.astype(F32), zero], axis=1
        ).astype(BF16)
        total = total + dot(c, right, TN)
    d_ref[...] = total
    first = pl.multiple_of(sc[5] * 128, 128)
    dh_ref[...] = d_ref[pl.ds(first, 128), :]
    wh_ref[...] = w_ref[pl.ds(first, 128), :]


def level2_kernel(sc, g, x, d, ds, w, ws, f_ref, send_ref, vw_ref, a, r):
    rows_of(g, 1, 8, 4, r)
    sib = jnp.concatenate([ds[0], ds[1]], axis=0)
    sub = d[...] + sib
    a[:, 0:256] = symmetric(joined(r, 0, 256)) - sub[:, 0:256]
    a[:, 256:384] = unpack(x[2]) - sub[:, 256:384]
    factor(a, 384)
    own = a[:, 256:384]
    f_ref[...] = own_columns(own, sc[4])
    wsib = jnp.concatenate([ws[0], ws[1]], axis=0)
    mine = w[...]
    pieces = [mine[:, n * WIDTH : (n + 1) * WIDTH] for n in range(3)]
    pieces += [wsib[:, n * WIDTH : (n + 1) * WIDTH] for n in range(3)]
    pieces.append(own[:, :WIDTH].astype(BF16))
    first = 4 + 8 * sc[3]
    pick = (iota((8, WIDTH), 0) + first == iota((8, WIDTH), 1)).astype(BF16)
    thick = jnp.concatenate([dot(pick, v, NT) for v in pieces], axis=0)
    thick = jnp.concatenate([thick[:, :128], thick[:, 128:]], axis=0).astype(BF16)
    for k in range(Z):
        send_ref[k] = thick
    src = iota((WIDTH, 128), 0)
    dst = iota((WIDTH, 128), 1)
    low = (src == dst + 4).astype(BF16)
    low = jnp.where(dst < KEEP, low, jnp.zeros_like(low))
    high = ((src == dst - 60) & (dst >= WIDTH)).astype(BF16)
    for n, v in enumerate(pieces):
        vw_ref[0, n * PAN : (n + 1) * PAN, :] = dot(v, low, NN).astype(BF16)
        vw_ref[1, n * PAN : (n + 1) * PAN, :] = dot(v, high, NN).astype(BF16)


def top_kernel(t_raw, got, vw, out, big):
    for y in range(Y):
        for z in range(Z):
            block = got[y, z].astype(F32)
            d = z * Y + y
            for n in range(7):
                for half in range(2):
                    first = half * 56 + n * 8
                    big[d * 8 : d * 8 + 8, (n * 2 + half) * 128 : (n * 2 + half + 1) * 128] = (
                        block[first : first + 8, :]
                    )
    low = dot(big[0:256, :].astype(BF16), vw[0], NN)
    high = dot(big[256:512, :].astype(BF16), vw[1], NN)
    out[...] = t_raw[...] - (low + high)


def last_kernel(t, out):
    for d in range(N // 2):
        block = jnp.concatenate([t[s, d * 8 : d * 8 + 8, :] for s in range(8)], axis=0)
        turned = jnp.transpose(block)
        out[:, d * KEEP : (d + 1) * KEEP] = turned[0:KEEP, 0:KEEP]
        d2 = d + N // 2
        out[:, d2 * KEEP : (d2 + 1) * KEEP] = turned[WIDTH : WIDTH + KEEP, 0:KEEP]


def call(kernel, specs, outs, scratch=(), flops=10**8, name=None):
    return pl.pallas_call(
        kernel,
        in_specs=specs,
        out_specs=[VMEM] * len(outs),
        out_shape=[jax.ShapeDtypeStruct(s, t) for s, t in outs],
        scratch_shapes=list(scratch),
        compiler_params=pltpu.CompilerParams(vmem_limit_bytes=48 * 2**20),
        cost_estimate=pl.CostEstimate(flops=flops, bytes_accessed=4 * 10**6, transcendentals=0),
        name=name,
    )


def crossed(value, mask):
    return lax.ppermute(value, "cube", [(c, c ^ mask) for c in range(8)])


def spread(value, axis_groups):
    return lax.all_to_all(value, "front", 0, 0, axis_index_groups=axis_groups, tiled=True)


def gather_front(sent, rows):
    lanes = sent.shape[-1]
    got = spread(sent.reshape(Z * rows, lanes), Z_GROUPS)
    copies = jnp.broadcast_to(got[None], (Y, Z * rows, lanes)).reshape(Y * Z * rows, lanes)
    return spread(copies, Y_GROUPS).reshape(Y, Z * rows, lanes)


def on_device(leaf_blocks, front_entries, child_maps):
    position = lax.axis_index("front")
    cube = lax.axis_index("cube")
    core = cube & 1
    nodes = [jnp.right_shift(cube + 8, h + 1) for h in range(3)]
    sides = [jnp.right_shift(cube, h) & 1 for h in range(3)]
    sc = jnp.stack(
        [n - 1 for n in nodes] + [cube, position, core, jnp.right_shift(cube, 2), cube * 0]
    ).astype(jnp.int32)
    flat = child_maps.reshape(14, KEEP)
    picked = [
        lax.dynamic_index_in_dim(flat, 2 * (n - 1) + s, 0, keepdims=False)
        for n, s in zip(nodes, sides)
    ]
    none = jnp.full((4,), -1, jnp.int32)
    maps = jnp.stack(
        [
            jnp.concatenate([picked[0], none]),
            jnp.concatenate([none, picked[1]]),
            jnp.concatenate([none, picked[2]]),
        ]
    )

    e, ent, ta, tb = call(
        leaf_kernel,
        [SMEM, SMEM, VMEM, VMEM, VMEM],
        [((3, 128, 128), F32), ((3, 128, 128), F32), ((1024, 128), F32), ((1024, 128), F32)],
        [pltpu.VMEM((4, 3840, 128), F32), pltpu.SMEM((128,), jnp.int32)],
        name="leaf",
    )(sc, maps, maps, leaf_blocks, front_entries)

    both = lax.all_gather(e, "cube", axis_index_groups=CORE_GROUPS, axis=0)
    pair = both[0, 1:] + both[1, 1:]
    quad = lax.all_gather(pair, "cube", axis_index_groups=X_GROUPS, axis=0)
    x, sent = call(
        pick_kernel,
        [SMEM] + [VMEM] * 4,
        [((3, 128, 128), F32), ((Z, 24, 128), F32)],
        name="pick",
    )(sc, maps, both, quad, ent)
    g = gather_front(sent, 24)
    g = lax.all_gather(g, "cube", axis_index_groups=CORE_GROUPS, axis=0)

    t_raw = ta + crossed(tb, 1)
    t_raw = t_raw[:512] + crossed(t_raw[512:], 2)
    t_raw = t_raw[:256] + crossed(t_raw[256:], 4)

    f0, v0 = call(
        level0_kernel,
        [SMEM] + [VMEM] * 3,
        [((WIDTH, PAN), F32), ((PAN, 640), BF16)],
        [pltpu.VMEM((PAN, 896), F32), pltpu.VMEM((2, 768, 128), F32)],
        flops=10**9,
        name="level0",
    )(sc, maps, g, x)
    v0s = crossed(v0, 2)
    f1, d1, w1, dh, wh = call(
        level1_kernel,
        [SMEM] + [VMEM] * 5,
        [
            ((WIDTH, PAN), F32),
            ((PAN, 384), F32),
            ((PAN, 256), BF16),
            ((128, 384), F32),
            ((128, 256), BF16),
        ],
        [pltpu.VMEM((PAN, 640), F32), pltpu.VMEM((2, 512, 128), F32)],
        flops=10**9,
        name="level1",
    )(sc, maps, g, x, v0, v0s)
    dh = lax.all_gather(crossed(dh, 4), "cube", axis_index_groups=CORE_GROUPS, axis=0)
    wh = lax.all_gather(crossed(wh, 4), "cube", axis_index_groups=CORE_GROUPS, axis=0)
    f2, thick, vw = call(
        level2_kernel,
        [SMEM] + [VMEM] * 6,
        [((WIDTH, PAN), F32), ((Z, 112, 128), BF16), ((2, 7 * PAN, 128), BF16)],
        [pltpu.VMEM((PAN, 384), F32), pltpu.VMEM((2, 256, 128), F32)],
        flops=10**9,
        name="level2",
    )(sc, g, x, d1, dh, w1, wh)
    thick = gather_front(thick, 112).reshape(Y, Z, 112, 128)
    (piece,) = call(
        top_kernel,
        [VMEM] * 3,
        [((256, 128), F32)],
        [pltpu.VMEM((512, 7 * PAN), F32)],
        name="top",
    )(t_raw, thick, vw)
    pieces = lax.all_gather(piece, "cube", axis=0)
    (top,) = call(last_kernel, [VMEM], [((KEEP, KEEP * N), F32)], name="last")(pieces)
    return jnp.stack([f0, f1, f2])[None], top


def solution(mesh):
    in_specs = (P("cube", "front", None), P(None, "front", None), P())
    out_specs = (P("cube", None, "front", None), P("front", None))
    return jax.shard_map(
        on_device, mesh=mesh, in_specs=in_specs, out_specs=out_specs, check_vma=False
    )
```

time: 1050 us -> 293 us (0.28); the launches traced: 1030 us -> 292 us
  waiting for transfers between devices: 479 us -> 96.1 us
  other arithmetic: 178 us -> 1.86 us
  blocking collectives: 189 us -> 59.3 us
  local copies, waits for them, and re-layouts: 111 us -> 6.39 us
  Pallas kernels: 0 us -> 81.3 us
  matrix products: 41.4 us -> 0 us
  starting transfers between devices: 16.6 us -> 33.1 us
    all_gather x3 -> x2, waiting for transfers between devices: 455 us -> 54.8 us  [the longest x1 36 us: on_device(): pieces = lax.all_gather(piece, 'cube', axis=0)]
    all_gather x3 -> x4, blocking collectives: 189 us -> 23.8 us  [the longest x1 9.9 us: on_device(): quad = lax.all_gather(pair, 'cube', axis_index_groups=X_GROUPS, axis=0)]
    another operation x30 -> x1, other arithmetic: 164 us -> 0.01 us  [on_device(): jnp.stack([jnp.concatenate([picked[0], none]), jnp.concatenate([none, pic...]
    pallas_call x0 -> x7, Pallas kernels: none -> 81.3 us  [the longest x1 24 us: on_device(): call(level2_kernel, [SMEM] + [VMEM] * 6, [((WIDTH, PAN), F32), ((Z, 112,...]
    reshape x25 -> x1, local copies, waits for them, and re-layouts: 51.3 us -> 0.74 us  [on_device(): flat = child_maps.reshape(14, KEEP)]
    dot_general x15 -> x0, matrix products: 38 us -> none  [the longest x6 17.6 us: scatter_rows(): widened = jnp.einsum('ubv,vs->usb', grid, table, precision=HIGH)]
    all_to_all x0 -> x2, blocking collectives: none -> 35.4 us  [spread(): lax.all_to_all(value, 'front', 0, 0, axis_index_groups=axis_groups, tiled...]
    neg x9 -> x0, local copies, waits for them, and re-layouts: 24.2 us -> none  [factor_front(): matrix = matrix.at[panel_rows:, last_col:].add(-reordered)]
  transfers between devices with their start and end apart: 6 -> 10, of which waited for: 5 -> 7; matrix products, arithmetic and copies ran while one was open for 1% -> 1% of each run, Pallas kernels for 0% -> 0%
where the time goes in v1:
time: 293 us; the launch traced here: 292 us
  waiting for transfers between devices  96.1 us (33%)
  Pallas kernels  81.3 us (28%)
  blocking collectives  59.3 us (20%)
  starting transfers between devices  33.1 us (11%)
  between operations  14.2 us (5%)
  local copies, waits for them, and re-layouts  6.39 us (2%)
    all_gather x1, waiting for transfers between devices, on_device(): pieces = lax.all_gather(piece, 'cube', axis=0)  36 us
    all_to_all x2, blocking collectives, spread(): lax.all_to_all(value, 'front', 0, 0, axis_index_groups=axis_groups, tiled...  35.4 us
    pallas_call x1, Pallas kernels, on_device(): call(level2_kernel, [SMEM] + [VMEM] * 6, [((WIDTH, PAN), F32), ((Z, 112,...  24 us
    pallas_call x1, Pallas kernels, on_device(): call(level1_kernel, [SMEM] + [VMEM] * 5, [((WIDTH, PAN), F32), ((PAN, 384...  23.7 us
    pallas_call x1, Pallas kernels, on_device(): call(level0_kernel, [SMEM] + [VMEM] * 3, [((WIDTH, PAN), F32), ((PAN, 640...  23.4 us
    ppermute x6, waiting for transfers between devices, crossed(): return lax.ppermute(value, 'cube', [(c, c ^ mask) for c in range(8)])  23.1 us
    all_gather x1, waiting for transfers between devices, on_device(): g = lax.all_gather(g, 'cube', axis_index_groups=CORE_GROUPS, axis=0)  18.8 us
    all_to_all x2, waiting for transfers between devices, spread(): lax.all_to_all(value, 'front', 0, 0, axis_index_groups=axis_groups, tiled...  18.1 us
  transfers between devices with their start and end apart: 10, of which 7 were waited for; matrix products, arithmetic and copies ran while one was open for 1% of the time, Pallas kernels for 0%

profile of v1, /device:TPU:1, one launch (start us, length us, event | category | flops | bytes accessed | tf_op | source)
XLA Modules:
  0.0 292.2 jit_solution(7367264898022458579)
XLA Ops:
  7.2 0.0 copy-start.1
  7.2 0.0 all-gather.8.cloned.1.call-start
  7.2 0.7 reshape.29
  8.0 1.3 copy.6.leaf
  9.3 0.1 pad_bitcast_fusion
  9.4 0.1 stack.55.sc
  9.4 0.0 copy-done.1
  9.4 5.9 %leaf.2 = (f32[3,128,128]{2,1,0:T(8,128)S(1)}, f32[3,128,128]{2,1,0:T(8,128)S(1)}, f32[1024,128]{1,0:T(8,128)S(1)}, f32[1024,128]{1,0:T(8,128)}) custom-call(s32[8]{0:T(128)S(1)} %stack.55.sc, s32[3,64]{1,0:T(4,128)S(1)} %pad_add_fusion.maps_s.maps_v, s32[3,64]{1,0:T(4,128)S(1)} %pad_add_fusion.maps_s.maps_v, f32[1,60,3840]{2,1,0:T(8,128)S(1)} %copy.6.leaf, ...), custom_call_target="tpu_custom_call" | custom-call | flops 100000000 | bytes 4000000 | tf_op jit(solution)/shard_map/leaf/pallas_call | solution.py:389
  15.3 8.6 %all-gather = f32[6,128,128]{2,1,0:T(8,128)S(1)} all-gather(f32[3,128,128]{2,1,0:T(8,128)S(1)} %get-tuple-element.18), channel_id=2, replica_groups={{0,64},{128,192},{256,320},{384,448},{1,65},{129,193},{257,321},{385,44..., dimensions={0}, use_global_device_ids=true | all-gather | bytes 589824 | tf_op jit(solution)/shard_map/all_gather | solution.py:397
  24.0 9.9 %all_gather.33.e12 = f32[4,2,128,128]{3,2,1,0:T(8,128)S(1)} all-gather(f32[1,2,128,128]{3,2,1,0:T(8,128)S(1)} %slice_add_fusion.2), channel_id=1, replica_groups={{0,128,256,384},{64,192,320,448},{1,129,257,385},{65,193,321,449},{2,13..., dimensions={0}, use_global_device_ids=true | all-gather | bytes 655360 | tf_op jit(solution)/shard_map/all_gather | solution.py:399
  33.9 0.9 pick.1
  34.8 23.0 %all_to_all.24 = f32[16,24,128]{2,1,0:T(8,128)S(1)} all-to-all(f32[16,24,128]{2,1,0:T(8,128)S(1)} %get-tuple-element.20), channel_id=1, replica_groups={{0,4,8,12,16,20,24,28,32,36,40,44,48,52,56,60},{1,5,9,13,17,21,25,29,33..., dimensions={0} | all-to-all | bytes 393216 | tf_op jit(solution)/shard_map/all_to_all | solution.py:356
  57.8 0.1 broadcast_in_dim.20
  57.8 12.4 %all_to_all.25 = f32[4,384,128]{2,1,0:T(8,128)} all-to-all(f32[4,384,128]{2,1,0:T(8,128)S(1)} %broadcast_in_dim.20), channel_id=1, replica_groups={{0,1,2,3},{4,5,6,7},{8,9,10,11},{12,13,14,15},{16,17,18,19},{20,21,22,2..., dimensions={0} | all-to-all | bytes 1572864 | tf_op jit(solution)/shard_map/all_to_all | solution.py:356
  70.3 0.0 all-gather.8.cloned.1.call-update
  70.3 18.8 %all-gather.8.cloned.1.call-done = f32[8,384,128]{2,1,0:T(8,128)} async-done(((f32[4,384,128]{2,1,0:T(8,128)}), f32[8,384,128]{2,1,0:T(8,128)}) %all-gather.8.cloned.1.call-update) | async-done | bytes 1572880 | tf_op jit(solution)/shard_map/all_gather | solution.py:407
  89.1 0.0 copy-start.2
  89.1 1.4 copy-done.2
  90.5 23.4 %level0.1 = (f32[64,256]{1,0:T(8,128)S(1)}, bf16[256,640]{1,0:T(8,128)(2,1)S(1)}) custom-call(s32[8]{0:T(128)S(1)} %stack.55.sc, s32[3,64]{1,0:T(4,128)S(1)} %pad_add_fusion.maps_s.maps_v, f32[2,4,384,128]{3,2,1,0:T(8,128)S(1)} %bitcast.41, f32[3,128,128]{2,1,0:T(8,128)S(1)} %get-tuple-element.21.x), custom_call_target="tpu_custom_call" | custom-call | flops 1000000000 | bytes 4000000 | tf_op jit(solution)/shard_map/level0/pallas_call | solution.py:413
  113.9 0.0 copy-start.3
  113.9 2.4 collective-permute-start
  116.3 8.7 %collective-permute-done.v0s = bf16[256,640]{1,0:T(8,128)(2,1)S(1)} collective-permute-done((bf16[256,640]{1,0:T(8,128)(2,1)S(1)}, bf16[256,640]{1,0:T(8,128)(2,1)S(1)}, u32[]{:S(2)}, u32[]{:S(2)}) %collective-permute-start) | collective-permute-done | bytes 327712 | tf_op jit(solution)/shard_map/ppermute | solution.py:352
  125.0 23.7 %level1.1 = (f32[64,256]{1,0:T(8,128)S(1)}, f32[256,384]{1,0:T(8,128)S(1)}, bf16[256,256]{1,0:T(8,128)(2,1)S(1)}, f32[128,384]{1,0:T(8,128)S(1)}, bf16[128,256]{1,0:T(8,128)(2,1)S(1)}) custom-call(s32[8]{0:T(128)S(1)} %stack.55.sc, s32[3,64]{1,0:T(4,128)S(1)} %pad_add_fusion.maps_s.maps_v, f32[2,4,384,128]{3,2,1,0:T(8,128)S(1)} %bitcast.42, ...), custom_call_target="tpu_custom_call" | custom-call | flops 1000000000 | bytes 4000000 | tf_op jit(solution)/shard_map/level1/pallas_call | solution.py:422
  148.7 3.6 %collective-permute-start.1 = (f32[128,384]{1,0:T(8,128)S(1)}, f32[128,384]{1,0:T(8,128)S(1)}, u32[]{:S(2)}, u32[]{:S(2)}) collective-permute-start(f32[128,384]{1,0:T(8,128)S(1)} %get-tuple-element.26), channel_id=1, source_target_pairs={{0,256},{64,320},{128,384},{192,448},{256,0},{320,64},{384,128},{4... | collective-permute-start | bytes 589832 | tf_op jit(solution)/shard_map/ppermute | solution.py:352
  152.3 3.2 %collective-permute-start.2 = (bf16[128,256]{1,0:T(8,128)(2,1)S(1)}, bf16[128,256]{1,0:T(8,128)(2,1)S(1)}, u32[]{:S(2)}, u32[]{:S(2)}) collective-permute-start(bf16[128,256]{1,0:T(8,128)(2,1)S(1)} %get-tuple-element.28), channel_id=1, source_target_pairs={{0,256},{64,320},{128,384},{192,448},{256,0},{320,64},{384,128},{4... | collective-permute-start | bytes 196616 | tf_op jit(solution)/shard_map/ppermute | solution.py:352
  155.5 4.0 %collective-permute-done.2 = bf16[128,256]{1,0:T(8,128)(2,1)S(1)} collective-permute-done((bf16[128,256]{1,0:T(8,128)(2,1)S(1)}, bf16[128,256]{1,0:T(8,128)(2,1)S(1)}, u32[]{:S(2)}, u32[]{:S(2)}) %collective-permute-start.2) | collective-permute-done | bytes 65568 | tf_op jit(solution)/shard_map/ppermute | solution.py:352
  159.5 3.3 %all-gather.3 = bf16[256,256]{1,0:T(8,128)(2,1)S(1)} all-gather(bf16[128,256]{1,0:T(8,128)(2,1)S(1)} %collective-permute-done.2), channel_id=5, replica_groups={{0,64},{128,192},{256,320},{384,448},{1,65},{129,193},{257,321},{385,44..., dimensions={0}, use_global_device_ids=true | all-gather | bytes 196608 | tf_op jit(solution)/shard_map/all_gather | solution.py:437
  162.8 0.0 collective-permute-done.1
  162.8 2.1 all-gather.2
  164.9 0.0 copy-done.3
  164.9 24.0 %level2.1 = (f32[64,256]{1,0:T(8,128)S(1)}, bf16[16,112,128]{2,1,0:T(8,128)(2,1)}, bf16[2,1792,128]{2,1,0:T(8,128)(2,1)S(1)}) custom-call(s32[8]{0:T(128)S(1)} %stack.55.sc, f32[2,4,384,128]{3,2,1,0:T(8,128)S(1)} %bitcast.43, f32[3,128,128]{2,1,0:T(8,128)S(1)} %get-tuple-element.21.x, f32[256,384]{1,0:T(8,128)S(1)} %get-tuple-element.25.d, ...), custom_call_target="tpu_custom_call" | custom-call | flops 1000000000 | bytes 4000000 | tf_op jit(solution)/shard_map/level2/pallas_call | solution.py:438
  188.9 12.0 %all-to-all-start.2 = ((bf16[16,112,128]{2,1,0:T(8,128)(2,1)}), bf16[16,112,128]{2,1,0:T(8,128)(2,1)S(1)}, u32[]{:S(2)}, u32[]{:S(2)}) async-start(bf16[16,112,128]{2,1,0:T(8,128)(2,1)} %get-tuple-element.32), calls=%async_computation.2 | async-start | bytes 917504 | tf_op jit(solution)/shard_map/all_to_all | solution.py:356
  201.0 2.5 collective-permute-start.3
  203.5 18.1 %all-to-all-done.2 = bf16[16,112,128]{2,1,0:T(8,128)(2,1)S(1)} async-done(((bf16[16,112,128]{2,1,0:T(8,128)(2,1)}), bf16[16,112,128]{2,1,0:T(8,128)(2,1)S(1)}, u32[]{:S(2)}, u32[]{:S(2)}) %all-to-all-start.2) | async-done | bytes 458784 | tf_op jit(solution)/shard_map/all_to_all | solution.py:356
  221.6 1.5 broadcast_in_dim.23
  223.1 4.0 %all-to-all-start.3 = ((bf16[4,1792,128]{2,1,0:T(8,128)(2,1)}), bf16[4,1792,128]{2,1,0:T(8,128)(2,1)S(1)}, u32[]{:S(2)}, u32[]{:S(2)}) async-start(bf16[4,1792,128]{2,1,0:T(8,128)(2,1)} %broadcast_in_dim.23), calls=%async_computation.3 | async-start | bytes 3670016 | tf_op jit(solution)/shard_map/all_to_all | solution.py:356
  227.1 0.0 all-gather.10.cloned.1.call-start
  227.1 0.0 collective-permute-done.3
  227.2 1.1 add.54
  228.3 2.2 collective-permute-start.4
  230.5 4.9 %collective-permute-done.4 = f32[512,128]{1,0:T(8,128)S(1)} collective-permute-done((f32[512,128]{1,0:T(8,128)S(1)}, f32[512,128]{1,0:T(8,128)S(1)}, u32[]{:S(2)}, u32[]{:S(2)}) %collective-permute-start.4) | collective-permute-done | bytes 262176 | tf_op jit(solution)/shard_map/ppermute | solution.py:352
  235.4 3.1 %collective-permute-start.5 = (f32[256,128]{1,0:T(8,128)S(1)}, f32[256,128]{1,0:T(8,128)S(1)}, u32[]{:S(2)}, u32[]{:S(2)}) collective-permute-start(f32[256,128]{1,0:T(8,128)S(1)} %slice.29), channel_id=1, source_target_pairs={{0,256},{64,320},{128,384},{192,448},{256,0},{320,64},{384,128},{4... | collective-permute-start | bytes 393224 | tf_op jit(solution)/shard_map/ppermute | solution.py:352
  238.6 5.5 %collective-permute-done.5 = f32[256,128]{1,0:T(8,128)S(1)} collective-permute-done((f32[256,128]{1,0:T(8,128)S(1)}, f32[256,128]{1,0:T(8,128)S(1)}, u32[]{:S(2)}, u32[]{:S(2)}) %collective-permute-start.5) | collective-permute-done | bytes 131104 | tf_op jit(solution)/shard_map/ppermute | solution.py:352
  244.1 0.0 all-to-all-done.3
  244.1 1.3 top.1
  245.4 0.0 all-gather.10.cloned.1.call-update
  245.4 0.7 maximum_bitcast_fusion
  246.1 36.0 %all-gather.10.cloned.1.call-done = f32[2048,128]{1,0:T(8,128)} async-done(((f32[256,128]{1,0:T(8,128)}), f32[2048,128]{1,0:T(8,128)}) %all-gather.10.cloned.1.call-update) | async-done | bytes 1048592 | tf_op jit(solution)/shard_map/all_gather | solution.py:454
  282.1 0.0 copy-start
  282.1 1.2 copy-done
  283.3 2.1 last.1
  (8 shorter events, 0.1 us)
Async XLA Ops:
  7.2 2.3 copy-start.1
  7.2 81.9 %all-gather.8.cloned.1.call-start = ((), (), s32[]{:S(2)}) async-start(), calls=%async_computation.4 | async-start | bytes 2359296 | tf_op jit(solution)/shard_map/all_gather | solution.py:407
  89.1 1.4 copy-start.2
  113.9 51.0 %copy-start.3 = (f32[8,384,128]{2,1,0:T(8,128)S(1)}, f32[8,384,128]{2,1,0:T(8,128)}, u32[]{:S(2)}) copy-start(f32[8,384,128]{2,1,0:T(8,128)} %all-gather.8.cloned.1.call-done) | copy-start | bytes 4718596
  113.9 11.1 %collective-permute-start = (bf16[256,640]{1,0:T(8,128)(2,1)S(1)}, bf16[256,640]{1,0:T(8,128)(2,1)S(1)}, u32[]{:S(2)}, u32[]{:S(2)}) collective-permute-start(bf16[256,640]{1,0:T(8,128)(2,1)S(1)} %get-tuple-element.23.v0), channel_id=1, source_target_pairs={{0,128},{64,192},{128,0},{192,64},{256,384},{320,448},{384,256},{4... | collective-permute-start | bytes 983048 | tf_op jit(solution)/shard_map/ppermute | solution.py:352
  148.7 14.1 %collective-permute-start.1 = (f32[128,384]{1,0:T(8,128)S(1)}, f32[128,384]{1,0:T(8,128)S(1)}, u32[]{:S(2)}, u32[]{:S(2)}) collective-permute-start(f32[128,384]{1,0:T(8,128)S(1)} %get-tuple-element.26), channel_id=1, source_target_pairs={{0,256},{64,320},{128,384},{192,448},{256,0},{320,64},{384,128},{4... | collective-permute-start | bytes 589832 | tf_op jit(solution)/shard_map/ppermute | solution.py:352
  152.3 7.2 %collective-permute-start.2 = (bf16[128,256]{1,0:T(8,128)(2,1)S(1)}, bf16[128,256]{1,0:T(8,128)(2,1)S(1)}, u32[]{:S(2)}, u32[]{:S(2)}) collective-permute-start(bf16[128,256]{1,0:T(8,128)(2,1)S(1)} %get-tuple-element.28), channel_id=1, source_target_pairs={{0,256},{64,320},{128,384},{192,448},{256,0},{320,64},{384,128},{4... | collective-permute-start | bytes 196616 | tf_op jit(solution)/shard_map/ppermute | solution.py:352
  188.9 32.7 %all-to-all-start.2 = ((bf16[16,112,128]{2,1,0:T(8,128)(2,1)}), bf16[16,112,128]{2,1,0:T(8,128)(2,1)S(1)}, u32[]{:S(2)}, u32[]{:S(2)}) async-start(bf16[16,112,128]{2,1,0:T(8,128)(2,1)} %get-tuple-element.32), calls=%async_computation.2 | async-start | bytes 917504 | tf_op jit(solution)/shard_map/all_to_all | solution.py:356
  201.0 26.2 %collective-permute-start.3 = (f32[1024,128]{1,0:T(8,128)}, f32[1024,128]{1,0:T(8,128)}, u32[]{:S(2)}, u32[]{:S(2)}) collective-permute-start(f32[1024,128]{1,0:T(8,128)} %get-tuple-element.31), channel_id=1, source_target_pairs={{0,64},{64,0},{128,192},{192,128},{256,320},{320,256},{384,448},{4... | collective-permute-start | bytes 1572872 | tf_op jit(solution)/shard_map/ppermute | solution.py:352
  223.1 20.9 %all-to-all-start.3 = ((bf16[4,1792,128]{2,1,0:T(8,128)(2,1)}), bf16[4,1792,128]{2,1,0:T(8,128)(2,1)S(1)}, u32[]{:S(2)}, u32[]{:S(2)}) async-start(bf16[4,1792,128]{2,1,0:T(8,128)(2,1)} %broadcast_in_dim.23), calls=%async_computation.3 | async-start | bytes 3670016 | tf_op jit(solution)/shard_map/all_to_all | solution.py:356
  227.1 55.0 %all-gather.10.cloned.1.call-start = ((), (), s32[]{:S(2)}) async-start(), calls=%async_computation.5 | async-start | bytes 1179648 | tf_op jit(solution)/shard_map/all_gather | solution.py:454
  228.3 7.1 %collective-permute-start.4 = (f32[512,128]{1,0:T(8,128)S(1)}, f32[512,128]{1,0:T(8,128)S(1)}, u32[]{:S(2)}, u32[]{:S(2)}) collective-permute-start(f32[512,128]{1,0:T(8,128)S(1)} %slice.27), channel_id=1, source_target_pairs={{0,128},{64,192},{128,0},{192,64},{256,384},{320,448},{384,256},{4... | collective-permute-start | bytes 786440 | tf_op jit(solution)/shard_map/ppermute | solution.py:352
  235.4 8.6 %collective-permute-start.5 = (f32[256,128]{1,0:T(8,128)S(1)}, f32[256,128]{1,0:T(8,128)S(1)}, u32[]{:S(2)}, u32[]{:S(2)}) collective-permute-start(f32[256,128]{1,0:T(8,128)S(1)} %slice.29), channel_id=1, source_target_pairs={{0,256},{64,320},{128,384},{192,448},{256,0},{320,64},{384,128},{4... | collective-permute-start | bytes 393224 | tf_op jit(solution)/shard_map/ppermute | solution.py:352
  282.1 1.2 copy-start
Sparse Core Ops, SparseCore 0:
  70.4 18.6 all-gather.7
  245.5 36.5 all-gather.9

commit v2 on v1

--- a/solution.py
+++ b/solution.py
@@ -65,18 +65,43 @@
     return jnp.where(iota(full.shape, 1) < WIDTH, full, 0.0)
 
 
+def spread_over(x, shape):
+    return jnp.broadcast_to(x, shape)
+
+
 def factor(a_ref, width):
+    tile = (8, 128)
+    rid = iota(tile, 0)
+    count = BLK // 8
     for b in range(PAN // BLK):
         j0 = b * BLK
         lo = j0 // 128 * 128
-        rows = a_ref[j0 : j0 + BLK, lo:width]
-        rid = iota((BLK, 1), 0)
-        for i in range(BLK):
-            jl = j0 - lo + i
-            col = rows[:, jl : jl + 1]
-            inv = 1.0 / rows[i : i + 1, jl : jl + 1]
-            scale = jnp.where(rid > i, col * inv, 0.0)
-            rows = rows - scale * rows[i : i + 1, :]
+        wide = width - lo
+        tiles = [a_ref[j0 + 8 * t : j0 + 8 * t + 8, lo:width] for t in range(count)]
+        for g in range(count):
+            c0 = j0 - lo + 8 * g
+            cols = [
+                [spread_over(tiles[t][:, c0 + k : c0 + k + 1], tile) for t in range(g, count)]
+                for k in range(8)
+            ]
+            for i in range(8):
+                inv = 1.0 / spread_over(cols[i][0][i : i + 1, :], tile)
+                scale = [c * inv for c in cols[i]]
+                scale[0] = jnp.where(rid > i, scale[0], 0.0)
+                for k in range(i + 1, 8):
+                    s = spread_over(cols[i][0][k : k + 1, :], tile)
+                    cols[k] = [c - f * s for c, f in zip(cols[k], scale)]
+                row = spread_over(tiles[g][i : i + 1, :], (8, wide))
+                for t in range(g, count):
+                    f = scale[t - g]
+                    tiles[t] = jnp.concatenate(
+                        [
+                            tiles[t][:, q : q + 128] - f * row[:, q : q + 128]
+                            for q in range(0, wide, 128)
+                        ],
+                        axis=1,
+                    )
+        rows = jnp.concatenate(tiles, axis=0)
         head = rows[:, 0:128]
         diag = jnp.sum(
             jnp.where(iota(head.shape, 1) == iota(head.shape, 0) + (j0 - lo), head, 0.0),
@@ -109,8 +134,8 @@
     for r in range(count):
         for y in range(Y):
             for half in range(2):
-                out_ref[half, pl.ds(r * N + y, Z, stride=Y), :] = g_ref[
-                    part, y, pl.ds(half * 12 + first + r, Z, stride=24), :
+                out_ref[half, pl.ds(r * N + y, Z, stride=Y), :] = g_ref[y // 2][
+                    part, y % 2, pl.ds(half * 12 + first + r, Z, stride=24), :
                 ]
 
 
@@ -234,8 +259,8 @@
         send_ref[k] = rows
 
 
-def level0_kernel(sc, maps_v, g, x, f_ref, v_ref, a, r):
-    rows_of(g, 0, 0, 12, r)
+def level0_kernel(sc, maps_v, ga, gb, x, f_ref, v_ref, a, r):
+    rows_of((ga, gb), 0, 0, 12, r)
     a[:, 0:256] = symmetric(joined(r, 0, 256))
     a[:, 256:768] = jnp.transpose(joined(r, 256, 768))
     a[:, 768:896] = unpack(x[0])
@@ -248,8 +273,8 @@
     v_ref[:, 512:640] = jnp.concatenate([moved, jnp.zeros_like(moved)], axis=1).astype(BF16)
 
 
-def level1_kernel(sc, maps_v, g, x, v0, v0s, f_ref, d_ref, w_ref, dh_ref, wh_ref, a, r):
-    rows_of(g, 1, 0, 8, r)
+def level1_kernel(sc, maps_v, ga, gb, x, v0, v0s, f_ref, d_ref, half_ref, a, r):
+    rows_of((ga, gb), 1, 0, 8, r)
     a[:, 0:256] = symmetric(joined(r, 0, 256))
     a[:, 256:512] = jnp.transpose(joined(r, 256, 512))
     a[:, 512:640] = unpack(x[1])
@@ -266,40 +291,46 @@
     ]
     cols = [mine[:, 256:512], other[:, 256:512], a[:, 256:512].astype(BF16)]
     zero = jnp.zeros((PAN, WIDTH), F32)
-    w = jnp.concatenate([m.astype(F32) for m in moved] + [zero], axis=1).astype(BF16)
-    w_ref[...] = w
+    right0 = [jnp.concatenate([c.astype(F32), m.astype(F32), zero], axis=1) for c, m in zip(cols, moved)]
     total = jnp.zeros((PAN, 384), F32)
-    for c, m in zip(cols, moved):
-        right = jnp.concatenate(
-            [c.astype(F32), m.astype(F32), zero], axis=1
-        ).astype(BF16)
-        total = total + dot(c, right, TN)
-    d_ref[...] = total
+    for c, right in zip(cols, right0):
+        total = total + dot(c, right.astype(BF16), TN)
+    d_ref[:, 0:256] = total[:, 0:256]
+    d_ref[:, 256:384] = jnp.concatenate(
+        [total[:, 256 : 256 + WIDTH], moved[0].astype(F32)], axis=1
+    )
+    d_ref[:, 384:512] = jnp.concatenate(
+        [moved[1].astype(F32), moved[2].astype(F32)], axis=1
+    )
     first = pl.multiple_of(sc[5] * 128, 128)
-    dh_ref[...] = d_ref[pl.ds(first, 128), :]
-    wh_ref[...] = w_ref[pl.ds(first, 128), :]
-
-
-def level2_kernel(sc, g, x, d, ds, w, ws, f_ref, send_ref, vw_ref, a, r):
-    rows_of(g, 1, 8, 4, r)
+    half_ref[...] = d_ref[pl.ds(first, 128), :]
+
+
+def level2_kernel(sc, ga, gb, x, d, ds, f0, f1, f_ref, send_ref, vw_ref, a, r):
+    rows_of((ga, gb), 1, 8, 4, r)
     sib = jnp.concatenate([ds[0], ds[1]], axis=0)
-    sub = d[...] + sib
+    mine = d[...]
+    sub = mine[:, 0:384] + sib[:, 0:384]
     a[:, 0:256] = symmetric(joined(r, 0, 256)) - sub[:, 0:256]
-    a[:, 256:384] = unpack(x[2]) - sub[:, 256:384]
+    a[:, 256:384] = jnp.where(
+        iota((PAN, 128), 1) < WIDTH, unpack(x[2]) - sub[:, 256:384], 0.0
+    )
     factor(a, 384)
     own = a[:, 256:384]
-    f_ref[...] = own_columns(own, sc[4])
-    wsib = jnp.concatenate([ws[0], ws[1]], axis=0)
-    mine = w[...]
-    pieces = [mine[:, n * WIDTH : (n + 1) * WIDTH] for n in range(3)]
-    pieces += [wsib[:, n * WIDTH : (n + 1) * WIDTH] for n in range(3)]
+    f_ref[0] = f0[...]
+    f_ref[1] = f1[...]
+    f_ref[2] = own_columns(own, sc[4])
+    pieces = [
+        m[:, first : first + WIDTH].astype(BF16)
+        for m in (mine, sib)
+        for first in (320, 384, 448)
+    ]
     pieces.append(own[:, :WIDTH].astype(BF16))
     first = 4 + 8 * sc[3]
     pick = (iota((8, WIDTH), 0) + first == iota((8, WIDTH), 1)).astype(BF16)
     thick = jnp.concatenate([dot(pick, v, NT) for v in pieces], axis=0)
     thick = jnp.concatenate([thick[:, :128], thick[:, 128:]], axis=0).astype(BF16)
-    for k in range(Z):
-        send_ref[k] = thick
+    send_ref[...] = thick
     src = iota((WIDTH, 128), 0)
     dst = iota((WIDTH, 128), 1)
     low = (src == dst + 4).astype(BF16)
@@ -323,12 +354,36 @@
                     )
     low = dot(big[0:256, :].astype(BF16), vw[0], NN)
     high = dot(big[256:512, :].astype(BF16), vw[1], NN)
-    out[...] = t_raw[...] - (low + high)
+    piece = t_raw[...] - (low + high)
+    last = piece[248:256, :]
+    lane = iota((8, 128), 1)
+    for t in range(31):
+        rows = piece[8 * t : 8 * t + 8, :]
+        if t < 16:
+            one = pltpu.roll(last, (60 - 8 * t) % 128, 1)
+            two = pltpu.roll(last, (120 - 8 * t) % 128, 1)
+            rows = jnp.where(
+                lane >= 124, two, jnp.where((lane >= 60) & (lane < 64), one, rows)
+            )
+        out[8 * t : 8 * t + 8, :] = rows
 
 
 def last_kernel(t, out):
+    lane = iota((8, 128), 1)
+    ends = []
+    for s in range(8):
+        end = jnp.zeros((8, 128), F32)
+        for k in range(16):
+            rows = t[s, 8 * k : 8 * k + 8, :]
+            one = pltpu.roll(rows, (8 * k - 60) % 128, 1)
+            two = pltpu.roll(rows, (8 * k - 120) % 128, 1)
+            end = jnp.where(lane // 4 == 2 * k, one, jnp.where(lane // 4 == 2 * k + 1, two, end))
+        ends.append(end)
     for d in range(N // 2):
-        block = jnp.concatenate([t[s, d * 8 : d * 8 + 8, :] for s in range(8)], axis=0)
+        if d < N // 2 - 1:
+            block = jnp.concatenate([t[s, d * 8 : d * 8 + 8, :] for s in range(8)], axis=0)
+        else:
+            block = jnp.concatenate(ends, axis=0)
         turned = jnp.transpose(block)
         out[:, d * KEEP : (d + 1) * KEEP] = turned[0:KEEP, 0:KEEP]
         d2 = d + N // 2
@@ -404,7 +459,10 @@
         name="pick",
     )(sc, maps, both, quad, ent)
     g = gather_front(sent, 24)
-    g = lax.all_gather(g, "cube", axis_index_groups=CORE_GROUPS, axis=0)
+    ga, gb = [
+        lax.all_gather(part, "cube", axis_index_groups=CORE_GROUPS, axis=0)
+        for part in (g[:2], g[2:])
+    ]
 
     t_raw = ta + crossed(tb, 1)
     t_raw = t_raw[:512] + crossed(t_raw[512:], 2)
@@ -412,48 +470,43 @@
 
     f0, v0 = call(
         level0_kernel,
-        [SMEM] + [VMEM] * 3,
+        [SMEM] + [VMEM] * 4,
         [((WIDTH, PAN), F32), ((PAN, 640), BF16)],
         [pltpu.VMEM((PAN, 896), F32), pltpu.VMEM((2, 768, 128), F32)],
         flops=10**9,
         name="level0",
-    )(sc, maps, g, x)
+    )(sc, maps, ga, gb, x)
     v0s = crossed(v0, 2)
-    f1, d1, w1, dh, wh = call(
+    f1, d1, half = call(
         level1_kernel,
-        [SMEM] + [VMEM] * 5,
-        [
-            ((WIDTH, PAN), F32),
-            ((PAN, 384), F32),
-            ((PAN, 256), BF16),
-            ((128, 384), F32),
-            ((128, 256), BF16),
-        ],
+        [SMEM] + [VMEM] * 6,
+        [((WIDTH, PAN), F32), ((PAN, 512), F32), ((128, 512), F32)],
         [pltpu.VMEM((PAN, 640), F32), pltpu.VMEM((2, 512, 128), F32)],
         flops=10**9,
         name="level1",
-    )(sc, maps, g, x, v0, v0s)
-    dh = lax.all_gather(crossed(dh, 4), "cube", axis_index_groups=CORE_GROUPS, axis=0)
-    wh = lax.all_gather(crossed(wh, 4), "cube", axis_index_groups=CORE_GROUPS, axis=0)
-    f2, thick, vw = call(
+    )(sc, maps, ga, gb, x, v0, v0s)
+    d1s = lax.all_gather(crossed(half, 4), "cube", axis_index_groups=CORE_GROUPS, axis=0)
+    factors, thick, vw = call(
         level2_kernel,
-        [SMEM] + [VMEM] * 6,
-        [((WIDTH, PAN), F32), ((Z, 112, 128), BF16), ((2, 7 * PAN, 128), BF16)],
+        [SMEM] + [VMEM] * 7,
+        [((3, WIDTH, PAN), F32), ((112, 128), BF16), ((2, 7 * PAN, 128), BF16)],
         [pltpu.VMEM((PAN, 384), F32), pltpu.VMEM((2, 256, 128), F32)],
         flops=10**9,
         name="level2",
-    )(sc, g, x, d1, dh, w1, wh)
-    thick = gather_front(thick, 112).reshape(Y, Z, 112, 128)
+    )(sc, ga, gb, x, d1, d1s, f0, f1)
+    thick = lax.all_gather(thick, "front", axis_index_groups=Z_GROUPS, axis=0, tiled=True)
+    copies = jnp.broadcast_to(thick[None], (Y, Z * 112, 128)).reshape(Y * Z * 112, 128)
+    thick = spread(copies, Y_GROUPS).reshape(Y, Z, 112, 128)
     (piece,) = call(
         top_kernel,
         [VMEM] * 3,
-        [((256, 128), F32)],
+        [((248, 128), F32)],
         [pltpu.VMEM((512, 7 * PAN), F32)],
         name="top",
     )(t_raw, thick, vw)
     pieces = lax.all_gather(piece, "cube", axis=0)
     (top,) = call(last_kernel, [VMEM], [((KEEP, KEEP * N), F32)], name="last")(pieces)
-    return jnp.stack([f0, f1, f2])[None], top
+    return factors[None], top
 
 
 def solution(mesh):

time: 293 us -> 201 us (0.69)
  waiting for transfers between devices: 96.1 us -> 22.4 us
  blocking collectives: 59.3 us -> 116 us
  Pallas kernels: 81.3 us -> 38.9 us
  starting transfers between devices: 33.1 us -> 17.7 us
  between operations: 14.2 us -> 0.81 us
    all_gather x2 -> x5, blocking collectives: 5.36 us -> 61.9 us  [the longest x1 24.6 us: on_device(): lax.all_gather(thick, 'front', axis_index_groups=Z_GROUPS, axis=0, tiled=...]
    all_gather x2 -> x0, waiting for transfers between devices: 54.8 us -> none  [the longest x1 36 us: on_device(): pieces = lax.all_gather(piece, 'cube', axis=0)]
    pallas_call x4, Pallas kernels: 72.4 us -> 29.6 us  [the longest x1 9.93 us: on_device(): call(level2_kernel, [SMEM] + [VMEM] * 7, [((3, WIDTH, PAN), F32), ((112,...]
    all_to_all x2 -> x1, waiting for transfers between devices: 18.1 us -> 0.01 us  [spread(): lax.all_to_all(value, 'front', 0, 0, axis_index_groups=axis_groups, tiled...]
    all_to_all x2 -> x1, starting transfers between devices: 16 us -> 3.58 us  [spread(): lax.all_to_all(value, 'front', 0, 0, axis_index_groups=axis_groups, tiled...]
    ppermute x6 -> x5, starting transfers between devices: 17.1 us -> 14.1 us  [crossed(): return lax.ppermute(value, 'cube', [(c, c ^ mask) for c in range(8)])]
    ppermute x6 -> x5, waiting for transfers between devices: 23.1 us -> 22.4 us  [crossed(): return lax.ppermute(value, 'cube', [(c, c ^ mask) for c in range(8)])]
  transfers between devices with their start and end apart: 10 -> 6, of which waited for: 7 -> 4; matrix products, arithmetic and copies ran while one was open for 1% -> 1% of each run, Pallas kernels for 0% -> 5%
where the time goes in v2:
time: 201 us
  blocking collectives  116 us (58%)
  Pallas kernels  38.9 us (19%)
  waiting for transfers between devices  22.4 us (11%)
  starting transfers between devices  17.7 us (9%)
  local copies, waits for them, and re-layouts  3.83 us (2%)
    all_to_all x2, blocking collectives, spread(): lax.all_to_all(value, 'front', 0, 0, axis_index_groups=axis_groups, tiled...  35.3 us
    all_gather x1, blocking collectives, on_device(): lax.all_gather(thick, 'front', axis_index_groups=Z_GROUPS, axis=0, tiled=...  24.6 us
    ppermute x5, waiting for transfers between devices, crossed(): return lax.ppermute(value, 'cube', [(c, c ^ mask) for c in range(8)])  22.4 us
    all_gather x1, blocking collectives, on_device(): pieces = lax.all_gather(piece, 'cube', axis=0)  22.1 us
    ppermute x5, starting transfers between devices, crossed(): return lax.ppermute(value, 'cube', [(c, c ^ mask) for c in range(8)])  14.1 us
    all_gather x2, blocking collectives, on_device(): lax.all_gather(part, 'cube', axis_index_groups=CORE_GROUPS, axis=0)  11.3 us
    pallas_call x1, Pallas kernels, on_device(): call(level2_kernel, [SMEM] + [VMEM] * 7, [((3, WIDTH, PAN), F32), ((112,...  9.93 us
    all_gather x1, blocking collectives, on_device(): quad = lax.all_gather(pair, 'cube', axis_index_groups=X_GROUPS, axis=0)  9.9 us
  transfers between devices with their start and end apart: 6, of which 4 were waited for; matrix products, arithmetic and copies ran while one was open for 1% of the time, Pallas kernels for 5%

profile of v2, /device:TPU:1, one launch (start us, length us, event | category | flops | bytes accessed | tf_op | source)
XLA Modules:
  0.0 200.5 jit_solution(7691722174411940603)
XLA Ops:
  0.6 0.0 copy-start
  0.7 0.8 reshape.35
  1.4 1.3 copy.6.leaf
  2.7 0.1 pad_bitcast_fusion
  2.8 0.1 stack.43.sc
  2.9 0.0 copy-done
  2.9 5.9 %leaf.2 = (f32[3,128,128]{2,1,0:T(8,128)S(1)}, f32[3,128,128]{2,1,0:T(8,128)S(1)}, f32[1024,128]{1,0:T(8,128)S(1)}, f32[1024,128]{1,0:T(8,128)}) custom-call(s32[8]{0:T(128)S(1)} %stack.43.sc, s32[3,64]{1,0:T(4,128)S(1)} %pad_add_fusion.maps_s.maps_v, s32[3,64]{1,0:T(4,128)S(1)} %pad_add_fusion.maps_s.maps_v, f32[1,60,3840]{2,1,0:T(8,128)S(1)} %copy.6.leaf, ...), custom_call_target="tpu_custom_call" | custom-call | flops 100000000 | bytes 4000000 | tf_op jit(solution)/shard_map/leaf/pallas_call | solution.py:444
  8.8 8.6 %all-gather = f32[6,128,128]{2,1,0:T(8,128)S(1)} all-gather(f32[3,128,128]{2,1,0:T(8,128)S(1)} %get-tuple-element.16), channel_id=2, replica_groups={{0,64},{128,192},{256,320},{384,448},{1,65},{129,193},{257,321},{385,44..., dimensions={0}, use_global_device_ids=true | all-gather | bytes 589824 | tf_op jit(solution)/shard_map/all_gather | solution.py:452
  17.4 9.9 %all_gather.39.e12 = f32[4,2,128,128]{3,2,1,0:T(8,128)S(1)} all-gather(f32[1,2,128,128]{3,2,1,0:T(8,128)S(1)} %slice_add_fusion.2), channel_id=1, replica_groups={{0,128,256,384},{64,192,320,448},{1,129,257,385},{65,193,321,449},{2,13..., dimensions={0}, use_global_device_ids=true | all-gather | bytes 655360 | tf_op jit(solution)/shard_map/all_gather | solution.py:454
  27.3 0.9 pick.1
  28.2 23.0 %all_to_all.18 = f32[16,24,128]{2,1,0:T(8,128)S(1)} all-to-all(f32[16,24,128]{2,1,0:T(8,128)S(1)} %get-tuple-element.18), channel_id=1, replica_groups={{0,4,8,12,16,20,24,28,32,36,40,44,48,52,56,60},{1,5,9,13,17,21,25,29,33..., dimensions={0} | all-to-all | bytes 393216 | tf_op jit(solution)/shard_map/all_to_all | solution.py:411
  51.2 0.1 broadcast_in_dim.18
  51.3 12.3 %all_to_all.19 = f32[4,384,128]{2,1,0:T(8,128)S(1)} all-to-all(f32[4,384,128]{2,1,0:T(8,128)S(1)} %broadcast_in_dim.18), channel_id=1, replica_groups={{0,1,2,3},{4,5,6,7},{8,9,10,11},{12,13,14,15},{16,17,18,19},{20,21,22,2..., dimensions={0} | all-to-all | bytes 1572864 | tf_op jit(solution)/shard_map/all_to_all | solution.py:411
  63.6 0.1 fusion.3
  63.7 8.9 %all-gather.2 = f32[4,384,128]{2,1,0:T(8,128)S(1)} all-gather(f32[2,384,128]{2,1,0:T(8,128)S(1)} %get-tuple-element.30), channel_id=4, replica_groups={{0,64},{128,192},{256,320},{384,448},{1,65},{129,193},{257,321},{385,44..., dimensions={0}, use_global_device_ids=true | all-gather | bytes 1179648 | tf_op jit(solution)/shard_map/all_gather | solution.py:463
  72.6 2.4 %all-gather.1 = f32[4,384,128]{2,1,0:T(8,128)S(1)} all-gather(f32[2,384,128]{2,1,0:T(8,128)S(1)} %get-tuple-element.31), channel_id=3, replica_groups={{0,64},{128,192},{256,320},{384,448},{1,65},{129,193},{257,321},{385,44..., dimensions={0}, use_global_device_ids=true | all-gather | bytes 1179648 | tf_op jit(solution)/shard_map/all_gather | solution.py:463
  74.9 9.2 %level0.1 = (f32[64,256]{1,0:T(8,128)S(1)}, bf16[256,640]{1,0:T(8,128)(2,1)S(1)}) custom-call(s32[8]{0:T(128)S(1)} %stack.43.sc, s32[3,64]{1,0:T(4,128)S(1)} %pad_add_fusion.maps_s.maps_v, f32[2,2,384,128]{3,2,1,0:T(8,128)S(1)} %bitcast.34, f32[2,2,384,128]{3,2,1,0:T(8,128)S(1)} %bitcast.31, f32[3,128,128]{2,1,0:T(8,128)S(1)} %get-tuple-element.19.x), custom_call_target="tpu_custom_call" | custom-call | flops 1000000000 | bytes 4000000 | tf_op jit(solution)/shard_map/level0/pallas_call | solution.py:471
  84.1 2.2 %collective-permute-start = (bf16[256,640]{1,0:T(8,128)(2,1)S(1)}, bf16[256,640]{1,0:T(8,128)(2,1)S(1)}, u32[]{:S(2)}, u32[]{:S(2)}) collective-permute-start(bf16[256,640]{1,0:T(8,128)(2,1)S(1)} %get-tuple-element.20.v0), channel_id=1, source_target_pairs={{0,128},{64,192},{128,0},{192,64},{256,384},{320,448},{384,256},{4... | collective-permute-start | bytes 983048 | tf_op jit(solution)/shard_map/ppermute | solution.py:407
  86.3 8.6 %collective-permute-done.v0s = bf16[256,640]{1,0:T(8,128)(2,1)S(1)} collective-permute-done((bf16[256,640]{1,0:T(8,128)(2,1)S(1)}, bf16[256,640]{1,0:T(8,128)(2,1)S(1)}, u32[]{:S(2)}, u32[]{:S(2)}) %collective-permute-start) | collective-permute-done | bytes 327712 | tf_op jit(solution)/shard_map/ppermute | solution.py:407
  95.0 9.7 %level1.1 = (f32[64,256]{1,0:T(8,128)S(1)}, f32[256,512]{1,0:T(8,128)S(1)}, f32[128,512]{1,0:T(8,128)S(1)}) custom-call(s32[8]{0:T(128)S(1)} %stack.43.sc, s32[3,64]{1,0:T(4,128)S(1)} %pad_add_fusion.maps_s.maps_v, f32[2,2,384,128]{3,2,1,0:T(8,128)S(1)} %bitcast.35, f32[2,2,384,128]{3,2,1,0:T(8,128)S(1)} %bitcast.32, ...), custom_call_target="tpu_custom_call" | custom-call | flops 1000000000 | bytes 4000000 | tf_op jit(solution)/shard_map/level1/pallas_call | solution.py:480
  104.7 3.1 %collective-permute-start.1 = (f32[128,512]{1,0:T(8,128)S(1)}, f32[128,512]{1,0:T(8,128)S(1)}, u32[]{:S(2)}, u32[]{:S(2)}) collective-permute-start(f32[128,512]{1,0:T(8,128)S(1)} %get-tuple-element.22), channel_id=1, source_target_pairs={{0,256},{64,320},{128,384},{192,448},{256,0},{320,64},{384,128},{4... | collective-permute-start | bytes 786440 | tf_op jit(solution)/shard_map/ppermute | solution.py:407
  107.8 3.4 %collective-permute-start.2 = (f32[1024,128]{1,0:T(8,128)}, f32[1024,128]{1,0:T(8,128)}, u32[]{:S(2)}, u32[]{:S(2)}) collective-permute-start(f32[1024,128]{1,0:T(8,128)} %get-tuple-element.27), channel_id=1, source_target_pairs={{0,64},{64,0},{128,192},{192,128},{256,320},{320,256},{384,448},{4... | collective-permute-start | bytes 1572872 | tf_op jit(solution)/shard_map/ppermute | solution.py:407
  111.2 3.5 %collective-permute-done.1 = f32[128,512]{1,0:T(8,128)S(1)} collective-permute-done((f32[128,512]{1,0:T(8,128)S(1)}, f32[128,512]{1,0:T(8,128)S(1)}, u32[]{:S(2)}, u32[]{:S(2)}) %collective-permute-start.1) | collective-permute-done | bytes 262176 | tf_op jit(solution)/shard_map/ppermute | solution.py:407
  114.7 3.9 %all-gather.3 = f32[256,512]{1,0:T(8,128)S(1)} all-gather(f32[128,512]{1,0:T(8,128)S(1)} %collective-permute-done.1), channel_id=5, replica_groups={{0,64},{128,192},{256,320},{384,448},{1,65},{129,193},{257,321},{385,44..., dimensions={0}, use_global_device_ids=true | all-gather | bytes 786432 | tf_op jit(solution)/shard_map/all_gather | solution.py:488
  118.6 9.9 %level2.1 = (f32[3,64,256]{2,1,0:T(8,128)}, bf16[112,128]{1,0:T(8,128)(2,1)S(1)}, bf16[2,1792,128]{2,1,0:T(8,128)(2,1)S(1)}) custom-call(s32[8]{0:T(128)S(1)} %stack.43.sc, f32[2,2,384,128]{3,2,1,0:T(8,128)S(1)} %bitcast.36, f32[2,2,384,128]{3,2,1,0:T(8,128)S(1)} %bitcast.33, f32[3,128,128]{2,1,0:T(8,128)S(1)} %get-tuple-element.19.x, ...), custom_call_target="tpu_custom_call" | custom-call | flops 1000000000 | bytes 4000000 | tf_op jit(solution)/shard_map/level2/pallas_call | solution.py:489
  128.6 24.6 %all_gather.46 = bf16[1792,128]{1,0:T(8,128)(2,1)S(1)} all-gather(bf16[112,128]{1,0:T(8,128)(2,1)S(1)} %get-tuple-element.28), channel_id=1, replica_groups={{0,4,8,12,16,20,24,28,32,36,40,44,48,52,56,60},{1,5,9,13,17,21,25,29,33..., dimensions={0}, use_global_device_ids=true | all-gather | bytes 487424 | tf_op jit(solution)/shard_map/all_gather | solution.py:497
  153.2 1.5 broadcast_in_dim.20
  154.7 3.6 %all-to-all-start.2 = ((bf16[4,1792,128]{2,1,0:T(8,128)(2,1)}), bf16[4,1792,128]{2,1,0:T(8,128)(2,1)S(1)}, u32[]{:S(2)}, u32[]{:S(2)}) async-start(bf16[4,1792,128]{2,1,0:T(8,128)(2,1)} %broadcast_in_dim.20), calls=%async_computation.2 | async-start | bytes 3670016 | tf_op jit(solution)/shard_map/all_to_all | solution.py:411
  158.3 0.0 collective-permute-done.2
  158.3 1.1 add.54
  159.4 2.1 %collective-permute-start.3 = (f32[512,128]{1,0:T(8,128)S(1)}, f32[512,128]{1,0:T(8,128)S(1)}, u32[]{:S(2)}, u32[]{:S(2)}) collective-permute-start(f32[512,128]{1,0:T(8,128)S(1)} %slice.41), channel_id=1, source_target_pairs={{0,128},{64,192},{128,0},{192,64},{256,384},{320,448},{384,256},{4... | collective-permute-start | bytes 786440 | tf_op jit(solution)/shard_map/ppermute | solution.py:407
  161.6 5.0 %collective-permute-done.3 = f32[512,128]{1,0:T(8,128)S(1)} collective-permute-done((f32[512,128]{1,0:T(8,128)S(1)}, f32[512,128]{1,0:T(8,128)S(1)}, u32[]{:S(2)}, u32[]{:S(2)}) %collective-permute-start.3) | collective-permute-done | bytes 262176 | tf_op jit(solution)/shard_map/ppermute | solution.py:407
  166.6 3.3 %collective-permute-start.4 = (f32[256,128]{1,0:T(8,128)S(1)}, f32[256,128]{1,0:T(8,128)S(1)}, u32[]{:S(2)}, u32[]{:S(2)}) collective-permute-start(f32[256,128]{1,0:T(8,128)S(1)} %slice.43), channel_id=1, source_target_pairs={{0,256},{64,320},{128,384},{192,448},{256,0},{320,64},{384,128},{4... | collective-permute-start | bytes 393224 | tf_op jit(solution)/shard_map/ppermute | solution.py:407
  169.9 5.3 %collective-permute-done.4 = f32[256,128]{1,0:T(8,128)S(1)} collective-permute-done((f32[256,128]{1,0:T(8,128)S(1)}, f32[256,128]{1,0:T(8,128)S(1)}, u32[]{:S(2)}, u32[]{:S(2)}) %collective-permute-start.4) | collective-permute-done | bytes 131104 | tf_op jit(solution)/shard_map/ppermute | solution.py:407
  175.2 0.0 all-to-all-done.2
  175.2 0.7 top.1
  176.0 22.1 %all-gather.4 = f32[1984,128]{1,0:T(8,128)S(1)} all-gather(f32[248,128]{1,0:T(8,128)S(1)} %top.1), channel_id=6, replica_groups=mesh['cube'=8,'front'=64] {'cube'}, dimensions={0}, use_global_device_ids=true | all-gather | bytes 1142784 | tf_op jit(solution)/shard_map/all_gather | solution.py:507
  198.1 2.5 %last.1 = f32[60,3840]{1,0:T(8,128)} custom-call(f32[8,248,128]{2,1,0:T(8,128)S(1)} %bitcast.28), custom_call_target="tpu_custom_call" | custom-call | flops 100000000 | bytes 4000000 | tf_op jit(solution)/shard_map/last/pallas_call | solution.py:508
  (8 shorter events, 0.1 us)
Async XLA Ops:
  0.6 2.2 %copy-start = (f32[7,64,256]{2,1,0:T(8,128)S(1)}, f32[7,64,256]{2,1,0:T(8,128)}, u32[]{:S(2)}) copy-start(f32[7,64,256]{2,1,0:T(8,128)} %entries.1) | copy-start | bytes 1376260
  84.1 10.8 %collective-permute-start = (bf16[256,640]{1,0:T(8,128)(2,1)S(1)}, bf16[256,640]{1,0:T(8,128)(2,1)S(1)}, u32[]{:S(2)}, u32[]{:S(2)}) collective-permute-start(bf16[256,640]{1,0:T(8,128)(2,1)S(1)} %get-tuple-element.20.v0), channel_id=1, source_target_pairs={{0,128},{64,192},{128,0},{192,64},{256,384},{320,448},{384,256},{4... | collective-permute-start | bytes 983048 | tf_op jit(solution)/shard_map/ppermute | solution.py:407
  104.7 10.0 %collective-permute-start.1 = (f32[128,512]{1,0:T(8,128)S(1)}, f32[128,512]{1,0:T(8,128)S(1)}, u32[]{:S(2)}, u32[]{:S(2)}) collective-permute-start(f32[128,512]{1,0:T(8,128)S(1)} %get-tuple-element.22), channel_id=1, source_target_pairs={{0,256},{64,320},{128,384},{192,448},{256,0},{320,64},{384,128},{4... | collective-permute-start | bytes 786440 | tf_op jit(solution)/shard_map/ppermute | solution.py:407
  107.8 50.5 %collective-permute-start.2 = (f32[1024,128]{1,0:T(8,128)}, f32[1024,128]{1,0:T(8,128)}, u32[]{:S(2)}, u32[]{:S(2)}) collective-permute-start(f32[1024,128]{1,0:T(8,128)} %get-tuple-element.27), channel_id=1, source_target_pairs={{0,64},{64,0},{128,192},{192,128},{256,320},{320,256},{384,448},{4... | collective-permute-start | bytes 1572872 | tf_op jit(solution)/shard_map/ppermute | solution.py:407
  154.7 20.5 %all-to-all-start.2 = ((bf16[4,1792,128]{2,1,0:T(8,128)(2,1)}), bf16[4,1792,128]{2,1,0:T(8,128)(2,1)S(1)}, u32[]{:S(2)}, u32[]{:S(2)}) async-start(bf16[4,1792,128]{2,1,0:T(8,128)(2,1)} %broadcast_in_dim.20), calls=%async_computation.2 | async-start | bytes 3670016 | tf_op jit(solution)/shard_map/all_to_all | solution.py:411
  159.4 7.1 %collective-permute-start.3 = (f32[512,128]{1,0:T(8,128)S(1)}, f32[512,128]{1,0:T(8,128)S(1)}, u32[]{:S(2)}, u32[]{:S(2)}) collective-permute-start(f32[512,128]{1,0:T(8,128)S(1)} %slice.41), channel_id=1, source_target_pairs={{0,128},{64,192},{128,0},{192,64},{256,384},{320,448},{384,256},{4... | collective-permute-start | bytes 786440 | tf_op jit(solution)/shard_map/ppermute | solution.py:407
  166.6 8.6 %collective-permute-start.4 = (f32[256,128]{1,0:T(8,128)S(1)}, f32[256,128]{1,0:T(8,128)S(1)}, u32[]{:S(2)}, u32[]{:S(2)}) collective-permute-start(f32[256,128]{1,0:T(8,128)S(1)} %slice.43), channel_id=1, source_target_pairs={{0,256},{64,320},{128,384},{192,448},{256,0},{320,64},{384,128},{4... | collective-permute-start | bytes 393224 | tf_op jit(solution)/shard_map/ppermute | solution.py:407

commit v3 on v2

--- a/solution.py
+++ b/solution.py
@@ -12,14 +12,14 @@
 HIGH = lax.Precision.HIGHEST
 
 N = 64
-Z, Y = 16, 4
+FAR, NEAR = 8, 8
 WIDTH = 64
 KEEP = 60
 PAN = 256
 BLK = 32
 
-Z_GROUPS = [[Y * z + y for z in range(Z)] for y in range(Y)]
-Y_GROUPS = [[Y * z + y for y in range(Y)] for z in range(Z)]
+FAR_GROUPS = [[NEAR * far + near for far in range(FAR)] for near in range(NEAR)]
+NEAR_GROUPS = [[NEAR * far + near for near in range(NEAR)] for far in range(FAR)]
 CORE_GROUPS = [[0, 1], [2, 3], [4, 5], [6, 7]]
 X_GROUPS = [[0, 2, 4, 6], [1, 3, 5, 7]]
 
@@ -132,10 +132,10 @@
 
 def rows_of(g_ref, part, first, count, out_ref):
     for r in range(count):
-        for y in range(Y):
+        for near in range(NEAR):
             for half in range(2):
-                out_ref[half, pl.ds(r * N + y, Z, stride=Y), :] = g_ref[y // 2][
-                    part, y % 2, pl.ds(half * 12 + first + r, Z, stride=24), :
+                out_ref[half, pl.ds(r * N + near, FAR, stride=NEAR), :] = g_ref[near // 4][
+                    part, near % 4, pl.ds(half * 12 + first + r, FAR, stride=24), :
                 ]
 
 
@@ -255,11 +255,13 @@
         z = z + (dot(table, h, NT) + dot(table, m, NT) + dot(table, l, NT))
     rows = jnp.concatenate([z[0:4], z[8:12], z[16:20]], axis=0)
     rows = jnp.concatenate([rows[:, :128], rows[:, 128:]], axis=0)
-    for k in range(Z):
+    for k in range(FAR):
         send_ref[k] = rows
 
 
-def level0_kernel(sc, maps_v, ga, gb, x, f_ref, v_ref, a, r):
+def level0_kernel(sc, maps_v, ga, gb, x, ta, tr, f_ref, v_ref, tk_ref, ts_ref, a, r):
+    tk_ref[...] = ta[0:512, :] + tr[0:512, :]
+    ts_ref[...] = ta[512:1024, :] + tr[512:1024, :]
     rows_of((ga, gb), 0, 0, 12, r)
     a[:, 0:256] = symmetric(joined(r, 0, 256))
     a[:, 256:768] = jnp.transpose(joined(r, 256, 768))
@@ -306,7 +308,11 @@
     half_ref[...] = d_ref[pl.ds(first, 128), :]
 
 
-def level2_kernel(sc, ga, gb, x, d, ds, f0, f1, f_ref, send_ref, vw_ref, a, r):
+def level2_kernel(
+    sc, ga, gb, x, d, ds, f0, f1, tk, tr, f_ref, send_ref, vw_ref, tk_ref, ts_ref, a, r
+):
+    tk_ref[...] = tk[0:256, :] + tr[0:256, :]
+    ts_ref[...] = tk[256:512, :] + tr[256:512, :]
     rows_of((ga, gb), 1, 8, 4, r)
     sib = jnp.concatenate([ds[0], ds[1]], axis=0)
     mine = d[...]
@@ -330,7 +336,8 @@
     pick = (iota((8, WIDTH), 0) + first == iota((8, WIDTH), 1)).astype(BF16)
     thick = jnp.concatenate([dot(pick, v, NT) for v in pieces], axis=0)
     thick = jnp.concatenate([thick[:, :128], thick[:, 128:]], axis=0).astype(BF16)
-    send_ref[...] = thick
+    for k in range(FAR):
+        send_ref[k] = thick
     src = iota((WIDTH, 128), 0)
     dst = iota((WIDTH, 128), 1)
     low = (src == dst + 4).astype(BF16)
@@ -341,11 +348,11 @@
         vw_ref[1, n * PAN : (n + 1) * PAN, :] = dot(v, high, NN).astype(BF16)
 
 
-def top_kernel(t_raw, got, vw, out, big):
-    for y in range(Y):
-        for z in range(Z):
-            block = got[y, z].astype(F32)
-            d = z * Y + y
+def top_kernel(tk, tr, got, vw, out, big):
+    for near in range(NEAR):
+        for far in range(FAR):
+            block = got[near, far].astype(F32)
+            d = far * NEAR + near
             for n in range(7):
                 for half in range(2):
                     first = half * 56 + n * 8
@@ -354,7 +361,7 @@
                     )
     low = dot(big[0:256, :].astype(BF16), vw[0], NN)
     high = dot(big[256:512, :].astype(BF16), vw[1], NN)
-    piece = t_raw[...] - (low + high)
+    piece = tk[...] + tr[...] - (low + high)
     last = piece[248:256, :]
     lane = iota((8, 128), 1)
     for t in range(31):
@@ -413,9 +420,10 @@
 
 def gather_front(sent, rows):
     lanes = sent.shape[-1]
-    got = spread(sent.reshape(Z * rows, lanes), Z_GROUPS)
-    copies = jnp.broadcast_to(got[None], (Y, Z * rows, lanes)).reshape(Y * Z * rows, lanes)
-    return spread(copies, Y_GROUPS).reshape(Y, Z * rows, lanes)
+    got = spread(sent.reshape(FAR * rows, lanes), FAR_GROUPS)
+    copies = jnp.broadcast_to(got[None], (NEAR, FAR * rows, lanes))
+    got = spread(copies.reshape(NEAR * FAR * rows, lanes), NEAR_GROUPS)
+    return got.reshape(NEAR, FAR * rows, lanes)
 
 
 def on_device(leaf_blocks, front_entries, child_maps):
@@ -455,28 +463,26 @@
     x, sent = call(
         pick_kernel,
         [SMEM] + [VMEM] * 4,
-        [((3, 128, 128), F32), ((Z, 24, 128), F32)],
+        [((3, 128, 128), F32), ((FAR, 24, 128), F32)],
         name="pick",
     )(sc, maps, both, quad, ent)
     g = gather_front(sent, 24)
     ga, gb = [
         lax.all_gather(part, "cube", axis_index_groups=CORE_GROUPS, axis=0)
-        for part in (g[:2], g[2:])
+        for part in (g[:4], g[4:])
     ]
 
-    t_raw = ta + crossed(tb, 1)
-    t_raw = t_raw[:512] + crossed(t_raw[512:], 2)
-    t_raw = t_raw[:256] + crossed(t_raw[256:], 4)
-
-    f0, v0 = call(
+    tr = crossed(tb, 1)
+    f0, v0, tk, ts = call(
         level0_kernel,
-        [SMEM] + [VMEM] * 4,
-        [((WIDTH, PAN), F32), ((PAN, 640), BF16)],
+        [SMEM] + [VMEM] * 6,
+        [((WIDTH, PAN), F32), ((PAN, 640), BF16), ((512, 128), F32), ((512, 128), F32)],
         [pltpu.VMEM((PAN, 896), F32), pltpu.VMEM((2, 768, 128), F32)],
         flops=10**9,
         name="level0",
-    )(sc, maps, ga, gb, x)
-    v0s = crossed(v0, 2)
+    )(sc, maps, ga, gb, x, ta, tr)
+    v0s, ts = lax.optimization_barrier((crossed(v0, 2), ts))
+    tr = crossed(ts, 2)
     f1, d1, half = call(
         level1_kernel,
         [SMEM] + [VMEM] * 6,
@@ -485,25 +491,31 @@
         flops=10**9,
         name="level1",
     )(sc, maps, ga, gb, x, v0, v0s)
+    half, tr = lax.optimization_barrier((half, tr))
     d1s = lax.all_gather(crossed(half, 4), "cube", axis_index_groups=CORE_GROUPS, axis=0)
-    factors, thick, vw = call(
+    factors, thick, vw, tk, ts = call(
         level2_kernel,
-        [SMEM] + [VMEM] * 7,
-        [((3, WIDTH, PAN), F32), ((112, 128), BF16), ((2, 7 * PAN, 128), BF16)],
+        [SMEM] + [VMEM] * 9,
+        [
+            ((3, WIDTH, PAN), F32),
+            ((FAR, 112, 128), BF16),
+            ((2, 7 * PAN, 128), BF16),
+            ((256, 128), F32),
+            ((256, 128), F32),
+        ],
         [pltpu.VMEM((PAN, 384), F32), pltpu.VMEM((2, 256, 128), F32)],
         flops=10**9,
         name="level2",
-    )(sc, ga, gb, x, d1, d1s, f0, f1)
-    thick = lax.all_gather(thick, "front", axis_index_groups=Z_GROUPS, axis=0, tiled=True)
-    copies = jnp.broadcast_to(thick[None], (Y, Z * 112, 128)).reshape(Y * Z * 112, 128)
-    thick = spread(copies, Y_GROUPS).reshape(Y, Z, 112, 128)
+    )(sc, ga, gb, x, d1, d1s, f0, f1, tk, tr)
+    tr = crossed(ts, 4)
+    thick = gather_front(thick, 112).reshape(NEAR, FAR, 112, 128)
     (piece,) = call(
         top_kernel,
-        [VMEM] * 3,
+        [VMEM] * 4,
         [((248, 128), F32)],
         [pltpu.VMEM((512, 7 * PAN), F32)],
         name="top",
-    )(t_raw, thick, vw)
+    )(tk, tr, thick, vw)
     pieces = lax.all_gather(piece, "cube", axis=0)
     (top,) = call(last_kernel, [VMEM], [((KEEP, KEEP * N), F32)], name="last")(pieces)
     return factors[None], top

time: 201 us -> 198 us (0.985)
  blocking collectives: 116 us -> 92 us
  starting transfers between devices: 17.7 us -> 29.2 us
  waiting for transfers between devices: 22.4 us -> 32 us
    all_gather x1 -> x0, blocking collectives: 24.6 us -> none  [on_device(): lax.all_gather(thick, 'front', axis_index_groups=Z_GROUPS, axis=0, tiled=...]
    all_to_all x1 -> x2, waiting for transfers between devices: 0.01 us -> 16.2 us  [spread(): lax.all_to_all(value, 'front', 0, 0, axis_index_groups=axis_groups, tiled...]
    all_to_all x2, blocking collectives: 35.3 us -> 42.9 us  [spread(): lax.all_to_all(value, 'front', 0, 0, axis_index_groups=axis_groups, tiled...]
    ppermute x5, starting transfers between devices: 14.1 us -> 21.4 us  [crossed(): return lax.ppermute(value, 'cube', [(c, c ^ mask) for c in range(8)])]
    ppermute x5, waiting for transfers between devices: 22.4 us -> 15.8 us  [crossed(): return lax.ppermute(value, 'cube', [(c, c ^ mask) for c in range(8)])]
    all_gather x1, blocking collectives: 22.1 us -> 16.8 us  [on_device(): pieces = lax.all_gather(piece, 'cube', axis=0)]
    all_to_all x1 -> x2, starting transfers between devices: 3.58 us -> 7.81 us  [spread(): lax.all_to_all(value, 'front', 0, 0, axis_index_groups=axis_groups, tiled...]
  transfers between devices with their start and end apart: 6 -> 7, of which waited for: 4 -> 5; matrix products, arithmetic and copies ran while one was open for 1% -> 0% of each run, Pallas kernels for 5% -> 5%
where the time goes in v3:
time: 198 us; the launch traced here: 197 us
  blocking collectives  92 us (46%)
  Pallas kernels  38.7 us (20%)
  waiting for transfers between devices  32 us (16%)
  starting transfers between devices  29.2 us (15%)
  local copies, waits for them, and re-layouts  4.67 us (2%)
    all_to_all x2, blocking collectives, spread(): lax.all_to_all(value, 'front', 0, 0, axis_index_groups=axis_groups, tiled...  42.9 us
    ppermute x5, starting transfers between devices, crossed(): return lax.ppermute(value, 'cube', [(c, c ^ mask) for c in range(8)])  21.4 us
    all_gather x1, blocking collectives, on_device(): pieces = lax.all_gather(piece, 'cube', axis=0)  16.8 us
    all_to_all x2, waiting for transfers between devices, spread(): lax.all_to_all(value, 'front', 0, 0, axis_index_groups=axis_groups, tiled...  16.2 us
    ppermute x5, waiting for transfers between devices, crossed(): return lax.ppermute(value, 'cube', [(c, c ^ mask) for c in range(8)])  15.8 us
    pallas_call x1, Pallas kernels, on_device(): call(level2_kernel, [SMEM] + [VMEM] * 9, [((3, WIDTH, PAN), F32), ((FAR,...  9.92 us
    all_gather x1, blocking collectives, on_device(): quad = lax.all_gather(pair, 'cube', axis_index_groups=X_GROUPS, axis=0)  9.9 us
    pallas_call x1, Pallas kernels, on_device(): call(level1_kernel, [SMEM] + [VMEM] * 6, [((WIDTH, PAN), F32), ((PAN, 512...  9.71 us
  transfers between devices with their start and end apart: 7, of which 5 were waited for; matrix products, arithmetic and copies ran while one was open for 0% of the time, Pallas kernels for 5%

profile of v3, /device:TPU:1, one launch (start us, length us, event | category | flops | bytes accessed | tf_op | source)
XLA Modules:
  0.0 197.3 jit_solution(1011659964247711933)
XLA Ops:
  0.6 0.0 copy-start
  0.7 0.8 reshape.37
  1.4 1.3 copy.6.leaf
  2.7 0.1 pad_bitcast_fusion
  2.8 0.1 stack.43.sc
  2.9 0.0 copy-done
  2.9 5.7 %leaf.2 = (f32[3,128,128]{2,1,0:T(8,128)S(1)}, f32[3,128,128]{2,1,0:T(8,128)S(1)}, f32[1024,128]{1,0:T(8,128)S(1)}, f32[1024,128]{1,0:T(8,128)S(1)}) custom-call(s32[8]{0:T(128)S(1)} %stack.43.sc, s32[3,64]{1,0:T(4,128)S(1)} %pad_add_fusion.maps_s.maps_v, s32[3,64]{1,0:T(4,128)S(1)} %pad_add_fusion.maps_s.maps_v, f32[1,60,3840]{2,1,0:T(8,128)S(1)} %copy.6.leaf, ...), custom_call_target="tpu_custom_call" | custom-call | flops 100000000 | bytes 4000000 | tf_op jit(solution)/shard_map/leaf/pallas_call | solution.py:452
  8.6 8.6 %all-gather = f32[6,128,128]{2,1,0:T(8,128)S(1)} all-gather(f32[3,128,128]{2,1,0:T(8,128)S(1)} %get-tuple-element.24), channel_id=2, replica_groups={{0,64},{128,192},{256,320},{384,448},{1,65},{129,193},{257,321},{385,44..., dimensions={0}, use_global_device_ids=true | all-gather | bytes 589824 | tf_op jit(solution)/shard_map/all_gather | solution.py:460
  17.2 9.9 %all_gather.36.e12 = f32[4,2,128,128]{3,2,1,0:T(8,128)S(1)} all-gather(f32[1,2,128,128]{3,2,1,0:T(8,128)S(1)} %slice_add_fusion), channel_id=1, replica_groups={{0,128,256,384},{64,192,320,448},{1,129,257,385},{65,193,321,449},{2,13..., dimensions={0}, use_global_device_ids=true | all-gather | bytes 655360 | tf_op jit(solution)/shard_map/all_gather | solution.py:462
  27.1 0.9 pick.1
  28.1 23.4 %all_to_all.24 = f32[8,24,128]{2,1,0:T(8,128)S(1)} all-to-all(f32[8,24,128]{2,1,0:T(8,128)S(1)} %get-tuple-element.26), channel_id=1, replica_groups={{0,8,16,24,32,40,48,56},{1,9,17,25,33,41,49,57},{2,10,18,26,34,42,50,58..., dimensions={0} | all-to-all | bytes 196608 | tf_op jit(solution)/shard_map/all_to_all | solution.py:418
  51.5 0.9 broadcast_in_dim.20
  52.4 4.2 %all-to-all-start.1 = ((f32[8,192,128]{2,1,0:T(8,128)}), f32[8,192,128]{2,1,0:T(8,128)S(1)}, u32[]{:S(2)}, u32[]{:S(2)}) async-start(f32[8,192,128]{2,1,0:T(8,128)} %broadcast_in_dim.20), calls=%async_computation.1 | async-start | bytes 1572864 | tf_op jit(solution)/shard_map/all_to_all | solution.py:418
  56.6 5.9 %collective-permute-start = (f32[1024,128]{1,0:T(8,128)S(1)}, f32[1024,128]{1,0:T(8,128)S(1)}, u32[]{:S(2)}, u32[]{:S(2)}) collective-permute-start(f32[1024,128]{1,0:T(8,128)S(1)} %get-tuple-element.29), channel_id=1, source_target_pairs={{0,64},{64,0},{128,192},{192,128},{256,320},{320,256},{384,448},{4... | collective-permute-start | bytes 1572872 | tf_op jit(solution)/shard_map/ppermute | solution.py:414
  62.6 2.4 %all-to-all-done.1 = f32[8,192,128]{2,1,0:T(8,128)S(1)} async-done(((f32[8,192,128]{2,1,0:T(8,128)}), f32[8,192,128]{2,1,0:T(8,128)S(1)}, u32[]{:S(2)}, u32[]{:S(2)}) %all-to-all-start.1) | async-done | bytes 786464 | tf_op jit(solution)/shard_map/all_to_all | solution.py:418
  65.0 0.1 fusion.3
  65.0 7.2 %all-gather.2 = f32[8,192,128]{2,1,0:T(8,128)S(1)} all-gather(f32[4,192,128]{2,1,0:T(8,128)S(1)} %get-tuple-element.46), channel_id=4, replica_groups={{0,64},{128,192},{256,320},{384,448},{1,65},{129,193},{257,321},{385,44..., dimensions={0}, use_global_device_ids=true | all-gather | bytes 1179648 | tf_op jit(solution)/shard_map/all_gather | solution.py:471
  72.2 2.4 %all-gather.1 = f32[8,192,128]{2,1,0:T(8,128)S(1)} all-gather(f32[4,192,128]{2,1,0:T(8,128)S(1)} %get-tuple-element.47), channel_id=3, replica_groups={{0,64},{128,192},{256,320},{384,448},{1,65},{129,193},{257,321},{385,44..., dimensions={0}, use_global_device_ids=true | all-gather | bytes 1179648 | tf_op jit(solution)/shard_map/all_gather | solution.py:471
  74.6 0.0 collective-permute-done.tr
  74.6 9.2 %level0.1 = (f32[64,256]{1,0:T(8,128)S(1)}, bf16[256,640]{1,0:T(8,128)(2,1)S(1)}, f32[512,128]{1,0:T(8,128)S(1)}, f32[512,128]{1,0:T(8,128)S(1)}) custom-call(s32[8]{0:T(128)S(1)} %stack.43.sc, s32[3,64]{1,0:T(4,128)S(1)} %pad_add_fusion.maps_s.maps_v, f32[2,4,192,128]{3,2,1,0:T(8,128)S(1)} %bitcast.35, f32[2,4,192,128]{3,2,1,0:T(8,128)S(1)} %bitcast.32, ...), custom_call_target="tpu_custom_call" | custom-call | flops 1000000000 | bytes 4000000 | tf_op jit(solution)/shard_map/level0/pallas_call | solution.py:476
  83.8 3.3 %collective-permute-start.1 = (bf16[256,640]{1,0:T(8,128)(2,1)S(1)}, bf16[256,640]{1,0:T(8,128)(2,1)S(1)}, u32[]{:S(2)}, u32[]{:S(2)}) collective-permute-start(bf16[256,640]{1,0:T(8,128)(2,1)S(1)} %get-tuple-element.30.v0), channel_id=1, source_target_pairs={{0,128},{64,192},{128,0},{192,64},{256,384},{320,448},{384,256},{4... | collective-permute-start | bytes 983048 | tf_op jit(solution)/shard_map/ppermute | solution.py:414
  87.2 7.5 %collective-permute-done.1.v0s = bf16[256,640]{1,0:T(8,128)(2,1)S(1)} collective-permute-done((bf16[256,640]{1,0:T(8,128)(2,1)S(1)}, bf16[256,640]{1,0:T(8,128)(2,1)S(1)}, u32[]{:S(2)}, u32[]{:S(2)}) %collective-permute-start.1) | collective-permute-done | bytes 327712 | tf_op jit(solution)/shard_map/ppermute | solution.py:414
  94.7 3.5 %collective-permute-start.2 = (f32[512,128]{1,0:T(8,128)S(1)}, f32[512,128]{1,0:T(8,128)S(1)}, u32[]{:S(2)}, u32[]{:S(2)}) collective-permute-start(f32[512,128]{1,0:T(8,128)S(1)} %get-tuple-element.35), channel_id=1, source_target_pairs={{0,128},{64,192},{128,0},{192,64},{256,384},{320,448},{384,256},{4... | collective-permute-start | bytes 786440 | tf_op jit(solution)/shard_map/ppermute | solution.py:414
  98.1 9.7 %level1.1 = (f32[64,256]{1,0:T(8,128)S(1)}, f32[256,512]{1,0:T(8,128)S(1)}, f32[128,512]{1,0:T(8,128)S(1)}) custom-call(s32[8]{0:T(128)S(1)} %stack.43.sc, s32[3,64]{1,0:T(4,128)S(1)} %pad_add_fusion.maps_s.maps_v, f32[2,4,192,128]{3,2,1,0:T(8,128)S(1)} %bitcast.36, f32[2,4,192,128]{3,2,1,0:T(8,128)S(1)} %bitcast.33, ...), custom_call_target="tpu_custom_call" | custom-call | flops 1000000000 | bytes 4000000 | tf_op jit(solution)/shard_map/level1/pallas_call | solution.py:486
  107.9 0.0 collective-permute-done.2.tr
  107.9 4.3 %collective-permute-start.3 = (f32[128,512]{1,0:T(8,128)S(1)}, f32[128,512]{1,0:T(8,128)S(1)}, u32[]{:S(2)}, u32[]{:S(2)}) collective-permute-start(f32[128,512]{1,0:T(8,128)S(1)} %get-tuple-element.36), channel_id=1, source_target_pairs={{0,256},{64,320},{128,384},{192,448},{256,0},{320,64},{384,128},{4... | collective-permute-start | bytes 786440 | tf_op jit(solution)/shard_map/ppermute | solution.py:414
  112.2 5.4 %collective-permute-done.3 = f32[128,512]{1,0:T(8,128)S(1)} collective-permute-done((f32[128,512]{1,0:T(8,128)S(1)}, f32[128,512]{1,0:T(8,128)S(1)}, u32[]{:S(2)}, u32[]{:S(2)}) %collective-permute-start.3) | collective-permute-done | bytes 262176 | tf_op jit(solution)/shard_map/ppermute | solution.py:414
  117.6 4.2 %all-gather.3 = f32[256,512]{1,0:T(8,128)S(1)} all-gather(f32[128,512]{1,0:T(8,128)S(1)} %collective-permute-done.3), channel_id=5, replica_groups={{0,64},{128,192},{256,320},{384,448},{1,65},{129,193},{257,321},{385,44..., dimensions={0}, use_global_device_ids=true | all-gather | bytes 786432 | tf_op jit(solution)/shard_map/all_gather | solution.py:495
  121.8 9.9 %level2.1 = (f32[3,64,256]{2,1,0:T(8,128)}, bf16[8,112,128]{2,1,0:T(8,128)(2,1)S(1)}, bf16[2,1792,128]{2,1,0:T(8,128)(2,1)S(1)}, f32[256,128]{1,0:T(8,128)S(1)}, f32[256,128]{1,0:T(8,128)S(1)}) custom-call(s32[8]{0:T(128)S(1)} %stack.43.sc, f32[2,4,192,128]{3,2,1,0:T(8,128)S(1)} %bitcast.37, f32[2,4,192,128]{3,2,1,0:T(8,128)S(1)} %bitcast.34, ...), custom_call_target="tpu_custom_call" | custom-call | flops 1000000000 | bytes 4000000 | tf_op jit(solution)/shard_map/level2/pallas_call | solution.py:496
  131.7 19.5 %all_to_all.25 = bf16[8,112,128]{2,1,0:T(8,128)(2,1)S(1)} all-to-all(bf16[8,112,128]{2,1,0:T(8,128)(2,1)S(1)} %get-tuple-element.44), channel_id=1, replica_groups={{0,8,16,24,32,40,48,56},{1,9,17,25,33,41,49,57},{2,10,18,26,34,42,50,58..., dimensions={0} | all-to-all | bytes 458752 | tf_op jit(solution)/shard_map/all_to_all | solution.py:418
  151.2 1.5 broadcast_in_dim.23
  152.7 3.6 %all-to-all-start.3 = ((bf16[8,896,128]{2,1,0:T(8,128)(2,1)}), bf16[8,896,128]{2,1,0:T(8,128)(2,1)S(1)}, u32[]{:S(2)}, u32[]{:S(2)}) async-start(bf16[8,896,128]{2,1,0:T(8,128)(2,1)} %broadcast_in_dim.23), calls=%async_computation.3 | async-start | bytes 3670016 | tf_op jit(solution)/shard_map/all_to_all | solution.py:418
  156.3 4.3 %collective-permute-start.4 = (f32[256,128]{1,0:T(8,128)S(1)}, f32[256,128]{1,0:T(8,128)S(1)}, u32[]{:S(2)}, u32[]{:S(2)}) collective-permute-start(f32[256,128]{1,0:T(8,128)S(1)} %get-tuple-element.43), channel_id=1, source_target_pairs={{0,256},{64,320},{128,384},{192,448},{256,0},{320,64},{384,128},{4... | collective-permute-start | bytes 393224 | tf_op jit(solution)/shard_map/ppermute | solution.py:414
  160.6 2.9 %collective-permute-done.4.tr = f32[256,128]{1,0:T(8,128)S(1)} collective-permute-done((f32[256,128]{1,0:T(8,128)S(1)}, f32[256,128]{1,0:T(8,128)S(1)}, u32[]{:S(2)}, u32[]{:S(2)}) %collective-permute-start.4) | collective-permute-done | bytes 131104 | tf_op jit(solution)/shard_map/ppermute | solution.py:414
  163.5 13.8 %all-to-all-done.3 = bf16[8,896,128]{2,1,0:T(8,128)(2,1)S(1)} async-done(((bf16[8,896,128]{2,1,0:T(8,128)(2,1)}), bf16[8,896,128]{2,1,0:T(8,128)(2,1)S(1)}, u32[]{:S(2)}, u32[]{:S(2)}) %all-to-all-start.3) | async-done | bytes 1835040 | tf_op jit(solution)/shard_map/all_to_all | solution.py:418
  177.3 0.7 top.1
  178.1 16.8 %all-gather.4 = f32[1984,128]{1,0:T(8,128)S(1)} all-gather(f32[248,128]{1,0:T(8,128)S(1)} %top.1), channel_id=6, replica_groups=mesh['cube'=8,'front'=64] {'cube'}, dimensions={0}, use_global_device_ids=true | all-gather | bytes 1142784 | tf_op jit(solution)/shard_map/all_gather | solution.py:519
  194.9 2.5 %last.1 = f32[60,3840]{1,0:T(8,128)} custom-call(f32[8,248,128]{2,1,0:T(8,128)S(1)} %bitcast.29), custom_call_target="tpu_custom_call" | custom-call | flops 100000000 | bytes 4000000 | tf_op jit(solution)/shard_map/last/pallas_call | solution.py:520
  (4 shorter events, 0.0 us)
Async XLA Ops:
  0.6 2.2 %copy-start = (f32[7,64,256]{2,1,0:T(8,128)S(1)}, f32[7,64,256]{2,1,0:T(8,128)}, u32[]{:S(2)}) copy-start(f32[7,64,256]{2,1,0:T(8,128)} %entries.1) | copy-start | bytes 1376260
  52.4 12.6 %all-to-all-start.1 = ((f32[8,192,128]{2,1,0:T(8,128)}), f32[8,192,128]{2,1,0:T(8,128)S(1)}, u32[]{:S(2)}, u32[]{:S(2)}) async-start(f32[8,192,128]{2,1,0:T(8,128)} %broadcast_in_dim.20), calls=%async_computation.1 | async-start | bytes 1572864 | tf_op jit(solution)/shard_map/all_to_all | solution.py:418
  56.6 17.9 %collective-permute-start = (f32[1024,128]{1,0:T(8,128)S(1)}, f32[1024,128]{1,0:T(8,128)S(1)}, u32[]{:S(2)}, u32[]{:S(2)}) collective-permute-start(f32[1024,128]{1,0:T(8,128)S(1)} %get-tuple-element.29), channel_id=1, source_target_pairs={{0,64},{64,0},{128,192},{192,128},{256,320},{320,256},{384,448},{4... | collective-permute-start | bytes 1572872 | tf_op jit(solution)/shard_map/ppermute | solution.py:414
  83.8 10.8 %collective-permute-start.1 = (bf16[256,640]{1,0:T(8,128)(2,1)S(1)}, bf16[256,640]{1,0:T(8,128)(2,1)S(1)}, u32[]{:S(2)}, u32[]{:S(2)}) collective-permute-start(bf16[256,640]{1,0:T(8,128)(2,1)S(1)} %get-tuple-element.30.v0), channel_id=1, source_target_pairs={{0,128},{64,192},{128,0},{192,64},{256,384},{320,448},{384,256},{4... | collective-permute-start | bytes 983048 | tf_op jit(solution)/shard_map/ppermute | solution.py:414
  94.7 13.2 %collective-permute-start.2 = (f32[512,128]{1,0:T(8,128)S(1)}, f32[512,128]{1,0:T(8,128)S(1)}, u32[]{:S(2)}, u32[]{:S(2)}) collective-permute-start(f32[512,128]{1,0:T(8,128)S(1)} %get-tuple-element.35), channel_id=1, source_target_pairs={{0,128},{64,192},{128,0},{192,64},{256,384},{320,448},{384,256},{4... | collective-permute-start | bytes 786440 | tf_op jit(solution)/shard_map/ppermute | solution.py:414
  107.9 9.7 %collective-permute-start.3 = (f32[128,512]{1,0:T(8,128)S(1)}, f32[128,512]{1,0:T(8,128)S(1)}, u32[]{:S(2)}, u32[]{:S(2)}) collective-permute-start(f32[128,512]{1,0:T(8,128)S(1)} %get-tuple-element.36), channel_id=1, source_target_pairs={{0,256},{64,320},{128,384},{192,448},{256,0},{320,64},{384,128},{4... | collective-permute-start | bytes 786440 | tf_op jit(solution)/shard_map/ppermute | solution.py:414
  152.7 24.6 %all-to-all-start.3 = ((bf16[8,896,128]{2,1,0:T(8,128)(2,1)}), bf16[8,896,128]{2,1,0:T(8,128)(2,1)S(1)}, u32[]{:S(2)}, u32[]{:S(2)}) async-start(bf16[8,896,128]{2,1,0:T(8,128)(2,1)} %broadcast_in_dim.23), calls=%async_computation.3 | async-start | bytes 3670016 | tf_op jit(solution)/shard_map/all_to_all | solution.py:418
  156.3 7.2 %collective-permute-start.4 = (f32[256,128]{1,0:T(8,128)S(1)}, f32[256,128]{1,0:T(8,128)S(1)}, u32[]{:S(2)}, u32[]{:S(2)}) collective-permute-start(f32[256,128]{1,0:T(8,128)S(1)} %get-tuple-element.43), channel_id=1, source_target_pairs={{0,256},{64,320},{128,384},{192,448},{256,0},{320,64},{384,128},{4... | collective-permute-start | bytes 393224 | tf_op jit(solution)/shard_map/ppermute | solution.py:414

commit v4 on v3

--- a/solution.py
+++ b/solution.py
@@ -21,7 +21,6 @@
 FAR_GROUPS = [[NEAR * far + near for far in range(FAR)] for near in range(NEAR)]
 NEAR_GROUPS = [[NEAR * far + near for near in range(NEAR)] for far in range(FAR)]
 CORE_GROUPS = [[0, 1], [2, 3], [4, 5], [6, 7]]
-X_GROUPS = [[0, 2, 4, 6], [1, 3, 5, 7]]
 
 VMEM = pl.BlockSpec(memory_space=pltpu.VMEM)
 SMEM = pl.BlockSpec(memory_space=pltpu.SMEM)
@@ -130,13 +129,16 @@
     return jnp.transpose(kept)[:WIDTH, :]
 
 
-def rows_of(g_ref, part, first, count, out_ref):
+def rows_of(g_ref, part, first, count, out_ref, more=None):
     for r in range(count):
         for near in range(NEAR):
             for half in range(2):
-                out_ref[half, pl.ds(r * N + near, FAR, stride=NEAR), :] = g_ref[near // 4][
-                    part, near % 4, pl.ds(half * 12 + first + r, FAR, stride=24), :
-                ]
+                at = half * 12 + first + r
+                got = g_ref[near // 4][part, near % 4, pl.ds(at, FAR, stride=24), :]
+                if more is not None:
+                    at = at + near % 4 * FAR * 24
+                    got = got + more[near // 4, pl.ds(at, FAR, stride=24), :]
+                out_ref[half, pl.ds(r * N + near, FAR, stride=NEAR), :] = got
 
 
 def joined(r, first, last):
@@ -147,8 +149,18 @@
     return jnp.where(iota(g.shape, 1) >= iota(g.shape, 0), jnp.transpose(g), g)
 
 
-def leaf_kernel(sc, maps_s, maps_v, leaf, entries, e_ref, ent_ref, ta_ref, tb_ref, big, inv):
+def leaf_kernel(
+    sc, maps_s, maps_v, leaf, entries, e_ref, ent_ref, ta_ref, tb_ref, stage, big, inv, sems
+):
     cube = sc[3]
+    chunks = 3840 // 256
+
+    def fetch(j):
+        cols = pl.ds(j * 256, 256)
+        return pltpu.make_async_copy(leaf.at[0, :, cols], stage.at[:, cols], sems.at[j])
+
+    for j in range(chunks):
+        fetch(j).start()
 
     @pl.loop(0, 72)
     def _(k):
@@ -166,18 +178,19 @@
     t1 = compose(onehot_rows(maps_v[1:2, :]), t0)
     t2 = compose(onehot_rows(maps_v[2:3, :]), t1)
     tt = compose(tail_table(), t2)
-    table = jnp.concatenate([tt, tt, t0, t0, t1, t1, t2, t2], axis=0).astype(F32)
+    table = jnp.concatenate([tt, t0, t1, t2], axis=0).astype(F32)
     table = jnp.transpose(table).astype(BF16)
     table = jnp.concatenate([table, table, table], axis=0)
 
     pad = jnp.zeros((WIDTH - KEEP, 256), F32)
-    for j in range(3840 // 256):
-        block = leaf[0, :, j * 256 : (j + 1) * 256]
+    for j in range(chunks):
+        fetch(j).wait()
+        block = stage[:, j * 256 : (j + 1) * 256]
         block = jnp.concatenate([block, pad], axis=0)
         parts = jnp.concatenate(split3(block), axis=0)
         turned = dot(parts, table, TN)
-        for f in range(4):
-            big[f, j * 256 : (j + 1) * 256, :] = turned[:, f * 128 : (f + 1) * 128]
+        big[0, j * 256 : (j + 1) * 256, :] = turned[:, 0:128]
+        big[1, j * 256 : (j + 1) * 256, :] = turned[:, 128:256]
 
     lane = iota((N, 128), 1)
     for h in range(3):
@@ -185,7 +198,9 @@
             pieces = []
             for side in range(2):
                 v = inv[h * 4 + side * 2 + k]
-                got = big[1 + h, pl.ds(jnp.maximum(v, 0), N, stride=KEEP), :]
+                got = big[(h + 1) // 2, pl.ds(jnp.maximum(v, 0), N, stride=KEEP), :]
+                if (h + 1) % 2 != side:
+                    got = pltpu.roll(got, 64, 1)
                 pieces.append(jnp.where(v >= 0, got, 0.0))
             e_ref[h, k * N : (k + 1) * N, :] = jnp.where(lane < WIDTH, pieces[0], pieces[1])
 
@@ -200,7 +215,8 @@
                 start = jnp.maximum(v, 0)
                 low = big[0, pl.ds(start, N // 2, stride=KEEP), :]
                 high = big[0, pl.ds(start + KEEP * N // 2, N // 2, stride=KEEP), :]
-                got = jnp.where(v >= 0, jnp.where(half_lane < WIDTH, low, high), 0.0)
+                got = jnp.where(half_lane < WIDTH, low, pltpu.roll(high, 64, 1))
+                got = jnp.where(v >= 0, got, 0.0)
             else:
                 got = jnp.zeros((N // 2, 128), F32)
 
@@ -221,15 +237,14 @@
         ent_ref[h] = jnp.concatenate([placed[:128], placed[128:]], axis=1)
 
 
-def pick_kernel(sc, maps_v, e0, e12, ent, x_ref, send_ref):
+def pick_kernel(sc, maps_v, e, ent, x_ref, xp_ref, send_ref):
     core = sc[5]
-    pair = sc[6]
-    x0 = e0[0, 0] + e0[1, 0] + ent[0]
-    q = [e12[x] for x in range(4)]
-    low, high = q[0] + q[1], q[2] + q[3]
-    x1 = jnp.where(pair == 0, low[0], high[0]) + ent[1]
-    x2 = low[1] + high[1] + ent[2]
-    x_ref[0], x_ref[1], x_ref[2] = x0, x1, x2
+    x = jnp.right_shift(sc[3], 1)
+    x0 = e[0, 0] + e[1, 0] + ent[0]
+    x1 = e[0, 1] + e[1, 1] + jnp.where(jnp.bitwise_and(x, 1) == 0, ent[1], 0.0)
+    x2 = e[0, 2] + e[1, 2] + jnp.where(x == 0, ent[2], 0.0)
+    x_ref[...] = x0
+    xp_ref[0], xp_ref[1] = x1, x2
     m1 = onehot_rows(maps_v[1:2, :])
     m2 = onehot_rows(maps_v[2:3, :])
     m21 = compose(m2, m1)
@@ -265,7 +280,7 @@
     rows_of((ga, gb), 0, 0, 12, r)
     a[:, 0:256] = symmetric(joined(r, 0, 256))
     a[:, 256:768] = jnp.transpose(joined(r, 256, 768))
-    a[:, 768:896] = unpack(x[0])
+    a[:, 768:896] = unpack(x[...])
     factor(a, 896)
     own = a[:, 768:896]
     f_ref[...] = own_columns(own, sc[4])
@@ -275,11 +290,13 @@
     v_ref[:, 512:640] = jnp.concatenate([moved, jnp.zeros_like(moved)], axis=1).astype(BF16)
 
 
-def level1_kernel(sc, maps_v, ga, gb, x, v0, v0s, f_ref, d_ref, half_ref, a, r):
-    rows_of((ga, gb), 1, 0, 8, r)
+def level1_kernel(
+    sc, maps_v, ga, gb, xp, cross, more, v0, v0s, f_ref, d_ref, half_ref, a, r
+):
+    rows_of((ga, gb), 1, 0, 12, r, more)
     a[:, 0:256] = symmetric(joined(r, 0, 256))
     a[:, 256:512] = jnp.transpose(joined(r, 256, 512))
-    a[:, 512:640] = unpack(x[1])
+    a[:, 512:640] = unpack(xp[0] + cross[768:896, :])
     mine, other = v0[...], v0s[...]
     a[...] -= dot(mine[:, 0:256], mine, TN) + dot(other[:, 0:256], other, TN)
     factor(a, 640)
@@ -297,9 +314,11 @@
     total = jnp.zeros((PAN, 384), F32)
     for c, right in zip(cols, right0):
         total = total + dot(c, right.astype(BF16), TN)
-    d_ref[:, 0:256] = total[:, 0:256]
+    d_ref[:, 0:256] = total[:, 0:256] - symmetric(joined(r, 512, 768))
+    own2 = unpack(xp[1] + cross[896:1024, :])
+    total = total[:, 256:384] - own2
     d_ref[:, 256:384] = jnp.concatenate(
-        [total[:, 256 : 256 + WIDTH], moved[0].astype(F32)], axis=1
+        [total[:, :WIDTH], moved[0].astype(F32)], axis=1
     )
     d_ref[:, 384:512] = jnp.concatenate(
         [moved[1].astype(F32), moved[2].astype(F32)], axis=1
@@ -309,18 +328,15 @@
 
 
 def level2_kernel(
-    sc, ga, gb, x, d, ds, f0, f1, tk, tr, f_ref, send_ref, vw_ref, tk_ref, ts_ref, a, r
+    sc, d, ds, f0, f1, tk, tr, f_ref, send_ref, vw_ref, tk_ref, ts_ref, a
 ):
     tk_ref[...] = tk[0:256, :] + tr[0:256, :]
     ts_ref[...] = tk[256:512, :] + tr[256:512, :]
-    rows_of((ga, gb), 1, 8, 4, r)
     sib = jnp.concatenate([ds[0], ds[1]], axis=0)
     mine = d[...]
     sub = mine[:, 0:384] + sib[:, 0:384]
-    a[:, 0:256] = symmetric(joined(r, 0, 256)) - sub[:, 0:256]
-    a[:, 256:384] = jnp.where(
-        iota((PAN, 128), 1) < WIDTH, unpack(x[2]) - sub[:, 256:384], 0.0
-    )
+    a[:, 0:256] = -sub[:, 0:256]
+    a[:, 256:384] = jnp.where(iota((PAN, 128), 1) < WIDTH, -sub[:, 256:384], 0.0)
     factor(a, 384)
     own = a[:, 256:384]
     f_ref[0] = f0[...]
@@ -435,9 +451,8 @@
     sc = jnp.stack(
         [n - 1 for n in nodes] + [cube, position, core, jnp.right_shift(cube, 2), cube * 0]
     ).astype(jnp.int32)
-    flat = child_maps.reshape(14, KEEP)
     picked = [
-        lax.dynamic_index_in_dim(flat, 2 * (n - 1) + s, 0, keepdims=False)
+        lax.dynamic_slice(child_maps, (n - 1, s, 0), (1, 1, KEEP)).reshape(KEEP)
         for n, s in zip(nodes, sides)
     ]
     none = jnp.full((4,), -1, jnp.int32)
@@ -451,26 +466,32 @@
 
     e, ent, ta, tb = call(
         leaf_kernel,
-        [SMEM, SMEM, VMEM, VMEM, VMEM],
+        [SMEM, SMEM, VMEM, pl.BlockSpec(memory_space=pltpu.HBM), VMEM],
         [((3, 128, 128), F32), ((3, 128, 128), F32), ((1024, 128), F32), ((1024, 128), F32)],
-        [pltpu.VMEM((4, 3840, 128), F32), pltpu.SMEM((128,), jnp.int32)],
+        [
+            pltpu.VMEM((KEEP, 3840), F32),
+            pltpu.VMEM((2, 3840, 128), F32),
+            pltpu.SMEM((128,), jnp.int32),
+            pltpu.SemaphoreType.DMA((15,)),
+        ],
         name="leaf",
     )(sc, maps, maps, leaf_blocks, front_entries)
 
     both = lax.all_gather(e, "cube", axis_index_groups=CORE_GROUPS, axis=0)
-    pair = both[0, 1:] + both[1, 1:]
-    quad = lax.all_gather(pair, "cube", axis_index_groups=X_GROUPS, axis=0)
-    x, sent = call(
+    x, xp, sent = call(
         pick_kernel,
-        [SMEM] + [VMEM] * 4,
-        [((3, 128, 128), F32), ((FAR, 24, 128), F32)],
+        [SMEM] + [VMEM] * 3,
+        [((128, 128), F32), ((2, 128, 128), F32), ((FAR, 24, 128), F32)],
         name="pick",
-    )(sc, maps, both, quad, ent)
+    )(sc, maps, both, ent)
     g = gather_front(sent, 24)
     ga, gb = [
         lax.all_gather(part, "cube", axis_index_groups=CORE_GROUPS, axis=0)
         for part in (g[:4], g[4:])
     ]
+
+    mine = jnp.where(core == 0, ga[1], gb[1]).reshape(768, 128)
+    cross = crossed(jnp.concatenate([mine, xp.reshape(256, 128)], axis=0), 2)
 
     tr = crossed(tb, 1)
     f0, v0, tk, ts = call(
@@ -483,19 +504,20 @@
     )(sc, maps, ga, gb, x, ta, tr)
     v0s, ts = lax.optimization_barrier((crossed(v0, 2), ts))
     tr = crossed(ts, 2)
+    more = lax.all_gather(cross[:768], "cube", axis_index_groups=CORE_GROUPS, axis=0)
     f1, d1, half = call(
         level1_kernel,
-        [SMEM] + [VMEM] * 6,
+        [SMEM] + [VMEM] * 8,
         [((WIDTH, PAN), F32), ((PAN, 512), F32), ((128, 512), F32)],
-        [pltpu.VMEM((PAN, 640), F32), pltpu.VMEM((2, 512, 128), F32)],
+        [pltpu.VMEM((PAN, 640), F32), pltpu.VMEM((2, 768, 128), F32)],
         flops=10**9,
         name="level1",
-    )(sc, maps, ga, gb, x, v0, v0s)
+    )(sc, maps, ga, gb, xp, cross, more, v0, v0s)
     half, tr = lax.optimization_barrier((half, tr))
     d1s = lax.all_gather(crossed(half, 4), "cube", axis_index_groups=CORE_GROUPS, axis=0)
     factors, thick, vw, tk, ts = call(
         level2_kernel,
-        [SMEM] + [VMEM] * 9,
+        [SMEM] + [VMEM] * 6,
         [
             ((3, WIDTH, PAN), F32),
             ((FAR, 112, 128), BF16),
@@ -503,10 +525,10 @@
             ((256, 128), F32),
             ((256, 128), F32),
         ],
-        [pltpu.VMEM((PAN, 384), F32), pltpu.VMEM((2, 256, 128), F32)],
+        [pltpu.VMEM((PAN, 384), F32)],
         flops=10**9,
         name="level2",
-    )(sc, ga, gb, x, d1, d1s, f0, f1, tk, tr)
+    )(sc, d1, d1s, f0, f1, tk, tr)
     tr = crossed(ts, 4)
     thick = gather_front(thick, 112).reshape(NEAR, FAR, 112, 128)
     (piece,) = call(

time: 198 us -> 199 us (level)
  blocking collectives: 92 us -> 82.9 us
  Pallas kernels: 38.7 us -> 44.9 us
  waiting for transfers between devices: 32 us -> 35.5 us
    pallas_call x4, Pallas kernels: 26.3 us -> 32.4 us  [the longest x1 11.9 us: on_device(): call(leaf_kernel, [SMEM, SMEM, VMEM, pl.BlockSpec(memory_space=pltpu.HBM)...]
    all_gather x1, blocking collectives: 9.9 us -> 3.99 us  [on_device(): lax.all_gather(cross[:768], 'cube', axis_index_groups=CORE_GROUPS, axis=0)]
    ppermute x5 -> x6, waiting for transfers between devices: 15.8 us -> 17.4 us  [crossed(): return lax.ppermute(value, 'cube', [(c, c ^ mask) for c in range(8)])]
    ppermute x5 -> x6, starting transfers between devices: 21.4 us -> 21.8 us  [crossed(): return lax.ppermute(value, 'cube', [(c, c ^ mask) for c in range(8)])]
  transfers between devices with their start and end apart: 7 -> 8, of which waited for: 5 -> 5; matrix products, arithmetic and copies ran while one was open for 0% -> 0% of each run, Pallas kernels for 5% -> 10%
where the time goes in v4:
time: 199 us
  blocking collectives  82.9 us (42%)
  Pallas kernels  44.9 us (23%)
  waiting for transfers between devices  35.5 us (18%)
  starting transfers between devices  29.8 us (15%)
  local copies, waits for them, and re-layouts  4.7 us (2%)
    all_to_all x2, blocking collectives, spread(): lax.all_to_all(value, 'front', 0, 0, axis_index_groups=axis_groups, tiled...  42.4 us
    ppermute x6, starting transfers between devices, crossed(): return lax.ppermute(value, 'cube', [(c, c ^ mask) for c in range(8)])  21.8 us
    all_to_all x2, waiting for transfers between devices, spread(): lax.all_to_all(value, 'front', 0, 0, axis_index_groups=axis_groups, tiled...  18.1 us
    ppermute x6, waiting for transfers between devices, crossed(): return lax.ppermute(value, 'cube', [(c, c ^ mask) for c in range(8)])  17.4 us
    all_gather x1, blocking collectives, on_device(): pieces = lax.all_gather(piece, 'cube', axis=0)  15.7 us
    pallas_call x1, Pallas kernels, on_device(): call(leaf_kernel, [SMEM, SMEM, VMEM, pl.BlockSpec(memory_space=pltpu.HBM)...  11.9 us
    pallas_call x1, Pallas kernels, on_device(): call(level2_kernel, [SMEM] + [VMEM] * 6, [((3, WIDTH, PAN), F32), ((FAR,...  9.84 us
    pallas_call x1, Pallas kernels, on_device(): call(level1_kernel, [SMEM] + [VMEM] * 8, [((WIDTH, PAN), F32), ((PAN, 512...  9.76 us
  transfers between devices with their start and end apart: 8, of which 5 were waited for; matrix products, arithmetic and copies ran while one was open for 0% of the time, Pallas kernels for 10%

profile of v4, /device:TPU:1, one launch (start us, length us, event | category | flops | bytes accessed | tf_op | source)
XLA Modules:
  0.0 198.7 jit_solution(9492967134603343057)
XLA Ops:
  0.6 0.0 copy-start
  0.7 0.8 fusion
  1.4 1.2 copy.6.leaf
  2.7 0.1 pad_bitcast_fusion
  2.8 0.1 stack.43.sc
  2.9 0.0 copy-done
  2.9 11.9 %leaf.2 = (f32[3,128,128]{2,1,0:T(8,128)S(1)}, f32[3,128,128]{2,1,0:T(8,128)S(1)}, f32[1024,128]{1,0:T(8,128)S(1)}, f32[1024,128]{1,0:T(8,128)S(1)}) custom-call(s32[8]{0:T(128)S(1)} %stack.43.sc, s32[3,64]{1,0:T(4,128)S(1)} %pad_add_fusion.maps_s.maps_v, s32[3,64]{1,0:T(4,128)S(1)} %pad_add_fusion.maps_s.maps_v, f32[1,60,3840]{2,1,0:T(8,128)S(1)} %copy.6.leaf, ...), custom_call_target="tpu_custom_call" | custom-call | flops 100000000 | bytes 4000000 | tf_op jit(solution)/shard_map/leaf/pallas_call | solution.py:467
  14.8 8.6 %all-gather = f32[6,128,128]{2,1,0:T(8,128)S(1)} all-gather(f32[3,128,128]{2,1,0:T(8,128)S(1)} %get-tuple-element.25), channel_id=2, replica_groups={{0,64},{128,192},{256,320},{384,448},{1,65},{129,193},{257,321},{385,44..., dimensions={0}, use_global_device_ids=true | all-gather | bytes 589824 | tf_op jit(solution)/shard_map/all_gather | solution.py:480
  23.4 0.9 pick.1
  24.3 21.9 %all_to_all.24 = f32[8,24,128]{2,1,0:T(8,128)S(1)} all-to-all(f32[8,24,128]{2,1,0:T(8,128)S(1)} %get-tuple-element.27), channel_id=1, replica_groups={{0,8,16,24,32,40,48,56},{1,9,17,25,33,41,49,57},{2,10,18,26,34,42,50,58..., dimensions={0} | all-to-all | bytes 196608 | tf_op jit(solution)/shard_map/all_to_all | solution.py:434
  46.2 0.9 broadcast_in_dim.20
  47.1 4.4 %all-to-all-start.1 = ((f32[8,192,128]{2,1,0:T(8,128)}), f32[8,192,128]{2,1,0:T(8,128)S(1)}, u32[]{:S(2)}, u32[]{:S(2)}) async-start(f32[8,192,128]{2,1,0:T(8,128)} %broadcast_in_dim.20), calls=%async_computation.1 | async-start | bytes 1572864 | tf_op jit(solution)/shard_map/all_to_all | solution.py:434
  51.5 5.3 %collective-permute-start.1 = (f32[1024,128]{1,0:T(8,128)S(1)}, f32[1024,128]{1,0:T(8,128)S(1)}, u32[]{:S(2)}, u32[]{:S(2)}) collective-permute-start(f32[1024,128]{1,0:T(8,128)S(1)} %get-tuple-element.31), channel_id=1, source_target_pairs={{0,64},{64,0},{128,192},{192,128},{256,320},{320,256},{384,448},{4... | collective-permute-start | bytes 1572872 | tf_op jit(solution)/shard_map/ppermute | solution.py:430
  56.8 3.0 %all-to-all-done.1 = f32[8,192,128]{2,1,0:T(8,128)S(1)} async-done(((f32[8,192,128]{2,1,0:T(8,128)}), f32[8,192,128]{2,1,0:T(8,128)S(1)}, u32[]{:S(2)}, u32[]{:S(2)}) %all-to-all-start.1) | async-done | bytes 786464 | tf_op jit(solution)/shard_map/all_to_all | solution.py:434
  59.8 0.1 fusion.3
  59.9 6.9 %all-gather.2 = f32[8,192,128]{2,1,0:T(8,128)S(1)} all-gather(f32[4,192,128]{2,1,0:T(8,128)S(1)} %get-tuple-element.48), channel_id=4, replica_groups={{0,64},{128,192},{256,320},{384,448},{1,65},{129,193},{257,321},{385,44..., dimensions={0}, use_global_device_ids=true | all-gather | bytes 1179648 | tf_op jit(solution)/shard_map/all_gather | solution.py:489
  66.8 2.4 %all-gather.1 = f32[8,192,128]{2,1,0:T(8,128)S(1)} all-gather(f32[4,192,128]{2,1,0:T(8,128)S(1)} %get-tuple-element.49), channel_id=3, replica_groups={{0,64},{128,192},{256,320},{384,448},{1,65},{129,193},{257,321},{385,44..., dimensions={0}, use_global_device_ids=true | all-gather | bytes 1179648 | tf_op jit(solution)/shard_map/all_gather | solution.py:489
  69.3 3.2 %collective-permute-start = (f32[1024,128]{1,0:T(8,128)S(1)}, f32[1024,128]{1,0:T(8,128)S(1)}, u32[]{:S(2)}, u32[]{:S(2)}) collective-permute-start(f32[1024,128]{1,0:T(8,128)S(1)} %pad_maximum_fusion), channel_id=1, source_target_pairs={{0,128},{64,192},{128,0},{192,64},{256,384},{320,448},{384,256},{4... | collective-permute-start | bytes 1572872 | tf_op jit(solution)/shard_map/ppermute | solution.py:430
  72.4 0.0 collective-permute-done.1.tr
  72.4 9.2 %level0.1 = (f32[64,256]{1,0:T(8,128)S(1)}, bf16[256,640]{1,0:T(8,128)(2,1)S(1)}, f32[512,128]{1,0:T(8,128)S(1)}, f32[512,128]{1,0:T(8,128)S(1)}) custom-call(s32[8]{0:T(128)S(1)} %stack.43.sc, s32[3,64]{1,0:T(4,128)S(1)} %pad_add_fusion.maps_s.maps_v, f32[2,4,192,128]{3,2,1,0:T(8,128)S(1)} %bitcast.35, f32[2,4,192,128]{3,2,1,0:T(8,128)S(1)} %bitcast.33, ...), custom_call_target="tpu_custom_call" | custom-call | flops 1000000000 | bytes 4000000 | tf_op jit(solution)/shard_map/level0/pallas_call | solution.py:497
  81.7 2.2 %collective-permute-start.2 = (bf16[256,640]{1,0:T(8,128)(2,1)S(1)}, bf16[256,640]{1,0:T(8,128)(2,1)S(1)}, u32[]{:S(2)}, u32[]{:S(2)}) collective-permute-start(bf16[256,640]{1,0:T(8,128)(2,1)S(1)} %get-tuple-element.32.v0), channel_id=1, source_target_pairs={{0,128},{64,192},{128,0},{192,64},{256,384},{320,448},{384,256},{4... | collective-permute-start | bytes 983048 | tf_op jit(solution)/shard_map/ppermute | solution.py:430
  83.8 8.4 %collective-permute-done.2.v0s = bf16[256,640]{1,0:T(8,128)(2,1)S(1)} collective-permute-done((bf16[256,640]{1,0:T(8,128)(2,1)S(1)}, bf16[256,640]{1,0:T(8,128)(2,1)S(1)}, u32[]{:S(2)}, u32[]{:S(2)}) %collective-permute-start.2) | collective-permute-done | bytes 327712 | tf_op jit(solution)/shard_map/ppermute | solution.py:430
  92.2 2.1 %collective-permute-start.3 = (f32[512,128]{1,0:T(8,128)S(1)}, f32[512,128]{1,0:T(8,128)S(1)}, u32[]{:S(2)}, u32[]{:S(2)}) collective-permute-start(f32[512,128]{1,0:T(8,128)S(1)} %get-tuple-element.37), channel_id=1, source_target_pairs={{0,128},{64,192},{128,0},{192,64},{256,384},{320,448},{384,256},{4... | collective-permute-start | bytes 786440 | tf_op jit(solution)/shard_map/ppermute | solution.py:430
  94.3 0.0 collective-permute-done.cross
  94.4 4.0 %all-gather.3 = f32[1536,128]{1,0:T(8,128)S(1)} all-gather(f32[768,128]{1,0:T(8,128)S(1)} %slice.30), channel_id=5, replica_groups={{0,64},{128,192},{256,320},{384,448},{1,65},{129,193},{257,321},{385,44..., dimensions={0}, use_global_device_ids=true | all-gather | bytes 1179648 | tf_op jit(solution)/shard_map/all_gather | solution.py:507
  98.4 9.8 %level1.1 = (f32[64,256]{1,0:T(8,128)S(1)}, f32[256,512]{1,0:T(8,128)S(1)}, f32[128,512]{1,0:T(8,128)S(1)}) custom-call(s32[8]{0:T(128)S(1)} %stack.43.sc, s32[3,64]{1,0:T(4,128)S(1)} %pad_add_fusion.maps_s.maps_v, f32[2,4,192,128]{3,2,1,0:T(8,128)S(1)} %bitcast.36, f32[2,4,192,128]{3,2,1,0:T(8,128)S(1)} %bitcast.34, ...), custom_call_target="tpu_custom_call" | custom-call | flops 1000000000 | bytes 4000000 | tf_op jit(solution)/shard_map/level1/pallas_call | solution.py:508
  108.1 0.0 collective-permute-done.3.tr
  108.1 4.7 %collective-permute-start.4 = (f32[128,512]{1,0:T(8,128)S(1)}, f32[128,512]{1,0:T(8,128)S(1)}, u32[]{:S(2)}, u32[]{:S(2)}) collective-permute-start(f32[128,512]{1,0:T(8,128)S(1)} %get-tuple-element.38), channel_id=1, source_target_pairs={{0,256},{64,320},{128,384},{192,448},{256,0},{320,64},{384,128},{4... | collective-permute-start | bytes 786440 | tf_op jit(solution)/shard_map/ppermute | solution.py:430
  112.8 6.2 %collective-permute-done.4 = f32[128,512]{1,0:T(8,128)S(1)} collective-permute-done((f32[128,512]{1,0:T(8,128)S(1)}, f32[128,512]{1,0:T(8,128)S(1)}, u32[]{:S(2)}, u32[]{:S(2)}) %collective-permute-start.4) | collective-permute-done | bytes 262176 | tf_op jit(solution)/shard_map/ppermute | solution.py:430
  119.0 3.0 %all-gather.4 = f32[256,512]{1,0:T(8,128)S(1)} all-gather(f32[128,512]{1,0:T(8,128)S(1)} %collective-permute-done.4), channel_id=6, replica_groups={{0,64},{128,192},{256,320},{384,448},{1,65},{129,193},{257,321},{385,44..., dimensions={0}, use_global_device_ids=true | all-gather | bytes 786432 | tf_op jit(solution)/shard_map/all_gather | solution.py:517
  122.1 9.8 %level2.1 = (f32[3,64,256]{2,1,0:T(8,128)}, bf16[8,112,128]{2,1,0:T(8,128)(2,1)S(1)}, bf16[2,1792,128]{2,1,0:T(8,128)(2,1)S(1)}, f32[256,128]{1,0:T(8,128)S(1)}, f32[256,128]{1,0:T(8,128)S(1)}) custom-call(s32[8]{0:T(128)S(1)} %stack.43.sc, f32[256,512]{1,0:T(8,128)S(1)} %get-tuple-element.35.d, f32[2,128,512]{2,1,0:T(8,128)S(1)} %bitcast.39, ...), custom_call_target="tpu_custom_call" | custom-call | flops 1000000000 | bytes 4000000 | tf_op jit(solution)/shard_map/level2/pallas_call | solution.py:518
  131.9 20.5 %all_to_all.25 = bf16[8,112,128]{2,1,0:T(8,128)(2,1)S(1)} all-to-all(bf16[8,112,128]{2,1,0:T(8,128)(2,1)S(1)} %get-tuple-element.46), channel_id=1, replica_groups={{0,8,16,24,32,40,48,56},{1,9,17,25,33,41,49,57},{2,10,18,26,34,42,50,58..., dimensions={0} | all-to-all | bytes 458752 | tf_op jit(solution)/shard_map/all_to_all | solution.py:434
  152.4 1.5 broadcast_in_dim.23
  153.9 3.6 %all-to-all-start.3 = ((bf16[8,896,128]{2,1,0:T(8,128)(2,1)}), bf16[8,896,128]{2,1,0:T(8,128)(2,1)S(1)}, u32[]{:S(2)}, u32[]{:S(2)}) async-start(bf16[8,896,128]{2,1,0:T(8,128)(2,1)} %broadcast_in_dim.23), calls=%async_computation.3 | async-start | bytes 3670016 | tf_op jit(solution)/shard_map/all_to_all | solution.py:434
  157.5 4.4 %collective-permute-start.5 = (f32[256,128]{1,0:T(8,128)S(1)}, f32[256,128]{1,0:T(8,128)S(1)}, u32[]{:S(2)}, u32[]{:S(2)}) collective-permute-start(f32[256,128]{1,0:T(8,128)S(1)} %get-tuple-element.45), channel_id=1, source_target_pairs={{0,256},{64,320},{128,384},{192,448},{256,0},{320,64},{384,128},{4... | collective-permute-start | bytes 393224 | tf_op jit(solution)/shard_map/ppermute | solution.py:430
  161.9 2.8 %collective-permute-done.5.tr = f32[256,128]{1,0:T(8,128)S(1)} collective-permute-done((f32[256,128]{1,0:T(8,128)S(1)}, f32[256,128]{1,0:T(8,128)S(1)}, u32[]{:S(2)}, u32[]{:S(2)}) %collective-permute-start.5) | collective-permute-done | bytes 131104 | tf_op jit(solution)/shard_map/ppermute | solution.py:430
  164.7 15.1 %all-to-all-done.3 = bf16[8,896,128]{2,1,0:T(8,128)(2,1)S(1)} async-done(((bf16[8,896,128]{2,1,0:T(8,128)(2,1)}), bf16[8,896,128]{2,1,0:T(8,128)(2,1)S(1)}, u32[]{:S(2)}, u32[]{:S(2)}) %all-to-all-start.3) | async-done | bytes 1835040 | tf_op jit(solution)/shard_map/all_to_all | solution.py:434
  179.8 0.7 top.1
  180.5 15.7 %all-gather.5 = f32[1984,128]{1,0:T(8,128)S(1)} all-gather(f32[248,128]{1,0:T(8,128)S(1)} %top.1), channel_id=7, replica_groups=mesh['cube'=8,'front'=64] {'cube'}, dimensions={0}, use_global_device_ids=true | all-gather | bytes 1142784 | tf_op jit(solution)/shard_map/all_gather | solution.py:541
  196.2 2.5 %last.1 = f32[60,3840]{1,0:T(8,128)} custom-call(f32[8,248,128]{2,1,0:T(8,128)S(1)} %bitcast.32), custom_call_target="tpu_custom_call" | custom-call | flops 100000000 | bytes 4000000 | tf_op jit(solution)/shard_map/last/pallas_call | solution.py:542
  (5 shorter events, 0.1 us)
Async XLA Ops:
  0.6 2.2 %copy-start = (f32[7,64,256]{2,1,0:T(8,128)S(1)}, f32[7,64,256]{2,1,0:T(8,128)}, u32[]{:S(2)}) copy-start(f32[7,64,256]{2,1,0:T(8,128)} %entries.1) | copy-start | bytes 1376260
  47.1 12.7 %all-to-all-start.1 = ((f32[8,192,128]{2,1,0:T(8,128)}), f32[8,192,128]{2,1,0:T(8,128)S(1)}, u32[]{:S(2)}, u32[]{:S(2)}) async-start(f32[8,192,128]{2,1,0:T(8,128)} %broadcast_in_dim.20), calls=%async_computation.1 | async-start | bytes 1572864 | tf_op jit(solution)/shard_map/all_to_all | solution.py:434
  51.5 21.0 %collective-permute-start.1 = (f32[1024,128]{1,0:T(8,128)S(1)}, f32[1024,128]{1,0:T(8,128)S(1)}, u32[]{:S(2)}, u32[]{:S(2)}) collective-permute-start(f32[1024,128]{1,0:T(8,128)S(1)} %get-tuple-element.31), channel_id=1, source_target_pairs={{0,64},{64,0},{128,192},{192,128},{256,320},{320,256},{384,448},{4... | collective-permute-start | bytes 1572872 | tf_op jit(solution)/shard_map/ppermute | solution.py:430
  69.3 25.1 %collective-permute-start = (f32[1024,128]{1,0:T(8,128)S(1)}, f32[1024,128]{1,0:T(8,128)S(1)}, u32[]{:S(2)}, u32[]{:S(2)}) collective-permute-start(f32[1024,128]{1,0:T(8,128)S(1)} %pad_maximum_fusion), channel_id=1, source_target_pairs={{0,128},{64,192},{128,0},{192,64},{256,384},{320,448},{384,256},{4... | collective-permute-start | bytes 1572872 | tf_op jit(solution)/shard_map/ppermute | solution.py:430
  81.7 10.5 %collective-permute-start.2 = (bf16[256,640]{1,0:T(8,128)(2,1)S(1)}, bf16[256,640]{1,0:T(8,128)(2,1)S(1)}, u32[]{:S(2)}, u32[]{:S(2)}) collective-permute-start(bf16[256,640]{1,0:T(8,128)(2,1)S(1)} %get-tuple-element.32.v0), channel_id=1, source_target_pairs={{0,128},{64,192},{128,0},{192,64},{256,384},{320,448},{384,256},{4... | collective-permute-start | bytes 983048 | tf_op jit(solution)/shard_map/ppermute | solution.py:430
  92.2 15.9 %collective-permute-start.3 = (f32[512,128]{1,0:T(8,128)S(1)}, f32[512,128]{1,0:T(8,128)S(1)}, u32[]{:S(2)}, u32[]{:S(2)}) collective-permute-start(f32[512,128]{1,0:T(8,128)S(1)} %get-tuple-element.37), channel_id=1, source_target_pairs={{0,128},{64,192},{128,0},{192,64},{256,384},{320,448},{384,256},{4... | collective-permute-start | bytes 786440 | tf_op jit(solution)/shard_map/ppermute | solution.py:430
  108.1 10.9 %collective-permute-start.4 = (f32[128,512]{1,0:T(8,128)S(1)}, f32[128,512]{1,0:T(8,128)S(1)}, u32[]{:S(2)}, u32[]{:S(2)}) collective-permute-start(f32[128,512]{1,0:T(8,128)S(1)} %get-tuple-element.38), channel_id=1, source_target_pairs={{0,256},{64,320},{128,384},{192,448},{256,0},{320,64},{384,128},{4... | collective-permute-start | bytes 786440 | tf_op jit(solution)/shard_map/ppermute | solution.py:430
  153.9 25.9 %all-to-all-start.3 = ((bf16[8,896,128]{2,1,0:T(8,128)(2,1)}), bf16[8,896,128]{2,1,0:T(8,128)(2,1)S(1)}, u32[]{:S(2)}, u32[]{:S(2)}) async-start(bf16[8,896,128]{2,1,0:T(8,128)(2,1)} %broadcast_in_dim.23), calls=%async_computation.3 | async-start | bytes 3670016 | tf_op jit(solution)/shard_map/all_to_all | solution.py:434
  157.5 7.2 %collective-permute-start.5 = (f32[256,128]{1,0:T(8,128)S(1)}, f32[256,128]{1,0:T(8,128)S(1)}, u32[]{:S(2)}, u32[]{:S(2)}) collective-permute-start(f32[256,128]{1,0:T(8,128)S(1)} %get-tuple-element.45), channel_id=1, source_target_pairs={{0,256},{64,320},{128,384},{192,448},{256,0},{320,64},{384,128},{4... | collective-permute-start | bytes 393224 | tf_op jit(solution)/shard_map/ppermute | solution.py:430

commit v5 on v4

--- a/solution.py
+++ b/solution.py
@@ -150,23 +150,16 @@
 
 
 def leaf_kernel(
-    sc, maps_s, maps_v, leaf, entries, e_ref, ent_ref, ta_ref, tb_ref, stage, big, inv, sems
+    sc, maps_s, maps_v, leaf, entries, e_ref, ent_ref, t_ref, big, inv
 ):
     cube = sc[3]
     chunks = 3840 // 256
 
-    def fetch(j):
-        cols = pl.ds(j * 256, 256)
-        return pltpu.make_async_copy(leaf.at[0, :, cols], stage.at[:, cols], sems.at[j])
-
-    for j in range(chunks):
-        fetch(j).start()
-
     @pl.loop(0, 72)
     def _(k):
         inv[k] = -1
 
-    @pl.loop(0, KEEP)
+    @pl.loop(0, KEEP, unroll=12)
     def _(v):
         a0 = maps_s[0, v]
         a1 = maps_s[1, a0]
@@ -184,8 +177,7 @@
 
     pad = jnp.zeros((WIDTH - KEEP, 256), F32)
     for j in range(chunks):
-        fetch(j).wait()
-        block = stage[:, j * 256 : (j + 1) * 256]
+        block = leaf[0, :, j * 256 : (j + 1) * 256]
         block = jnp.concatenate([block, pad], axis=0)
         parts = jnp.concatenate(split3(block), axis=0)
         turned = dot(parts, table, TN)
@@ -207,7 +199,7 @@
     half_lane = iota((N // 2, 128), 1)
     for s in range(8):
         r = jnp.bitwise_xor(s, cube)
-        slot = jnp.bitwise_and(r, 2) + jnp.right_shift(r, 2)
+        slot = jnp.bitwise_and(r, 1) * 4 + jnp.bitwise_and(r, 2) + jnp.right_shift(r, 2)
         for i in range(8):
             dst = pl.ds(slot * 256 + i, N // 2, stride=8)
             if s * 8 + i < KEEP:
@@ -220,13 +212,7 @@
             else:
                 got = jnp.zeros((N // 2, 128), F32)
 
-            @pl.when(jnp.bitwise_and(r, 1) == 0)
-            def _():
-                ta_ref[dst, :] = got
-
-            @pl.when(jnp.bitwise_and(r, 1) == 1)
-            def _():
-                tb_ref[dst, :] = got
+            t_ref[dst, :] = got
 
     p = iota((PAN, PAN), 0)
     order = (iota((PAN, PAN), 1) == (p % N) * 4 + p // N).astype(BF16)
@@ -464,15 +450,13 @@
         ]
     )
 
-    e, ent, ta, tb = call(
+    e, ent, t = call(
         leaf_kernel,
-        [SMEM, SMEM, VMEM, pl.BlockSpec(memory_space=pltpu.HBM), VMEM],
-        [((3, 128, 128), F32), ((3, 128, 128), F32), ((1024, 128), F32), ((1024, 128), F32)],
+        [SMEM, SMEM, VMEM, VMEM, VMEM],
+        [((3, 128, 128), F32), ((3, 128, 128), F32), ((2048, 128), F32)],
         [
-            pltpu.VMEM((KEEP, 3840), F32),
             pltpu.VMEM((2, 3840, 128), F32),
             pltpu.SMEM((128,), jnp.int32),
-            pltpu.SemaphoreType.DMA((15,)),
         ],
         name="leaf",
     )(sc, maps, maps, leaf_blocks, front_entries)
@@ -493,7 +477,7 @@
     mine = jnp.where(core == 0, ga[1], gb[1]).reshape(768, 128)
     cross = crossed(jnp.concatenate([mine, xp.reshape(256, 128)], axis=0), 2)
 
-    tr = crossed(tb, 1)
+    tr = crossed(t[1024:], 1)
     f0, v0, tk, ts = call(
         level0_kernel,
         [SMEM] + [VMEM] * 6,
@@ -501,7 +485,7 @@
         [pltpu.VMEM((PAN, 896), F32), pltpu.VMEM((2, 768, 128), F32)],
         flops=10**9,
         name="level0",
-    )(sc, maps, ga, gb, x, ta, tr)
+    )(sc, maps, ga, gb, x, t, tr)
     v0s, ts = lax.optimization_barrier((crossed(v0, 2), ts))
     tr = crossed(ts, 2)
     more = lax.all_gather(cross[:768], "cube", axis_index_groups=CORE_GROUPS, axis=0)

time: 199 us -> 191 us (0.960)
  Pallas kernels: 44.9 us -> 36.1 us
    pallas_call x1, Pallas kernels: 11.9 us -> 3.17 us  [on_device(): call(leaf_kernel, [SMEM, SMEM, VMEM, VMEM, VMEM], [((3, 128, 128), F32),...]
where the time goes in v5:
time: 191 us; the launch traced here: 190 us
  blocking collectives  82.7 us (43%)
  Pallas kernels  36.1 us (19%)
  waiting for transfers between devices  35.7 us (19%)
  starting transfers between devices  29.8 us (16%)
  local copies, waits for them, and re-layouts  4.74 us (2%)
    all_to_all x2, blocking collectives, spread(): lax.all_to_all(value, 'front', 0, 0, axis_index_groups=axis_groups, tiled...  42.6 us
    ppermute x6, starting transfers between devices, crossed(): return lax.ppermute(value, 'cube', [(c, c ^ mask) for c in range(8)])  21.8 us
    all_to_all x2, waiting for transfers between devices, spread(): lax.all_to_all(value, 'front', 0, 0, axis_index_groups=axis_groups, tiled...  18.3 us
    ppermute x6, waiting for transfers between devices, crossed(): return lax.ppermute(value, 'cube', [(c, c ^ mask) for c in range(8)])  17.4 us
    all_gather x1, blocking collectives, on_device(): pieces = lax.all_gather(piece, 'cube', axis=0)  15.3 us
    pallas_call x1, Pallas kernels, on_device(): call(level2_kernel, [SMEM] + [VMEM] * 6, [((3, WIDTH, PAN), F32), ((FAR,...  9.85 us
    pallas_call x1, Pallas kernels, on_device(): call(level1_kernel, [SMEM] + [VMEM] * 8, [((WIDTH, PAN), F32), ((PAN, 512...  9.76 us
    all_gather x2, blocking collectives, on_device(): lax.all_gather(part, 'cube', axis_index_groups=CORE_GROUPS, axis=0)  9.29 us
  transfers between devices with their start and end apart: 8, of which 5 were waited for; matrix products, arithmetic and copies ran while one was open for 0% of the time, Pallas kernels for 10%

profile of v5, /device:TPU:1, one launch (start us, length us, event | category | flops | bytes accessed | tf_op | source)
XLA Modules:
  0.0 190.0 jit_solution(16122784910158810819)
XLA Ops:
  0.6 0.0 copy-start
  0.7 0.8 fusion
  1.4 1.2 copy.6.leaf
  2.7 0.1 pad_bitcast_fusion
  2.8 0.1 stack.43.sc
  2.9 0.0 copy-done
  2.9 3.2 %leaf.2 = (f32[3,128,128]{2,1,0:T(8,128)S(1)}, f32[3,128,128]{2,1,0:T(8,128)S(1)}, f32[2048,128]{1,0:T(8,128)S(1)}) custom-call(s32[8]{0:T(128)S(1)} %stack.43.sc, s32[3,64]{1,0:T(4,128)S(1)} %pad_add_fusion.maps_s.maps_v, s32[3,64]{1,0:T(4,128)S(1)} %pad_add_fusion.maps_s.maps_v, f32[1,60,3840]{2,1,0:T(8,128)S(1)} %copy.6.leaf, f32[7,64,256]{2,1,0:T(8,128)S(1)} %copy-done), custom_call_target="tpu_custom_call" | custom-call | flops 100000000 | bytes 4000000 | tf_op jit(solution)/shard_map/leaf/pallas_call | solution.py:453
  6.0 8.6 %all-gather = f32[6,128,128]{2,1,0:T(8,128)S(1)} all-gather(f32[3,128,128]{2,1,0:T(8,128)S(1)} %get-tuple-element.24), channel_id=2, replica_groups={{0,64},{128,192},{256,320},{384,448},{1,65},{129,193},{257,321},{385,44..., dimensions={0}, use_global_device_ids=true | all-gather | bytes 589824 | tf_op jit(solution)/shard_map/all_gather | solution.py:464
  14.6 0.9 pick.1
  15.6 21.9 %all_to_all.24 = f32[8,24,128]{2,1,0:T(8,128)S(1)} all-to-all(f32[8,24,128]{2,1,0:T(8,128)S(1)} %get-tuple-element.26), channel_id=1, replica_groups={{0,8,16,24,32,40,48,56},{1,9,17,25,33,41,49,57},{2,10,18,26,34,42,50,58..., dimensions={0} | all-to-all | bytes 196608 | tf_op jit(solution)/shard_map/all_to_all | solution.py:420
  37.4 0.9 broadcast_in_dim.20
  38.4 4.4 %all-to-all-start.1 = ((f32[8,192,128]{2,1,0:T(8,128)}), f32[8,192,128]{2,1,0:T(8,128)S(1)}, u32[]{:S(2)}, u32[]{:S(2)}) async-start(f32[8,192,128]{2,1,0:T(8,128)} %broadcast_in_dim.20), calls=%async_computation.1 | async-start | bytes 1572864 | tf_op jit(solution)/shard_map/all_to_all | solution.py:420
  42.8 5.3 %collective-permute-start.1 = (f32[1024,128]{1,0:T(8,128)S(1)}, f32[1024,128]{1,0:T(8,128)S(1)}, u32[]{:S(2)}, u32[]{:S(2)}) collective-permute-start(f32[1024,128]{1,0:T(8,128)S(1)} %slice.27), channel_id=1, source_target_pairs={{0,64},{64,0},{128,192},{192,128},{256,320},{320,256},{384,448},{4... | collective-permute-start | bytes 1572872 | tf_op jit(solution)/shard_map/ppermute | solution.py:416
  48.1 3.0 %all-to-all-done.1 = f32[8,192,128]{2,1,0:T(8,128)S(1)} async-done(((f32[8,192,128]{2,1,0:T(8,128)}), f32[8,192,128]{2,1,0:T(8,128)S(1)}, u32[]{:S(2)}, u32[]{:S(2)}) %all-to-all-start.1) | async-done | bytes 786464 | tf_op jit(solution)/shard_map/all_to_all | solution.py:420
  51.1 0.1 fusion.3
  51.2 6.9 %all-gather.2 = f32[8,192,128]{2,1,0:T(8,128)S(1)} all-gather(f32[4,192,128]{2,1,0:T(8,128)S(1)} %get-tuple-element.46), channel_id=4, replica_groups={{0,64},{128,192},{256,320},{384,448},{1,65},{129,193},{257,321},{385,44..., dimensions={0}, use_global_device_ids=true | all-gather | bytes 1179648 | tf_op jit(solution)/shard_map/all_gather | solution.py:473
  58.1 2.4 %all-gather.1 = f32[8,192,128]{2,1,0:T(8,128)S(1)} all-gather(f32[4,192,128]{2,1,0:T(8,128)S(1)} %get-tuple-element.47), channel_id=3, replica_groups={{0,64},{128,192},{256,320},{384,448},{1,65},{129,193},{257,321},{385,44..., dimensions={0}, use_global_device_ids=true | all-gather | bytes 1179648 | tf_op jit(solution)/shard_map/all_gather | solution.py:473
  60.5 3.1 %collective-permute-start = (f32[1024,128]{1,0:T(8,128)S(1)}, f32[1024,128]{1,0:T(8,128)S(1)}, u32[]{:S(2)}, u32[]{:S(2)}) collective-permute-start(f32[1024,128]{1,0:T(8,128)S(1)} %pad_maximum_fusion), channel_id=1, source_target_pairs={{0,128},{64,192},{128,0},{192,64},{256,384},{320,448},{384,256},{4... | collective-permute-start | bytes 1572872 | tf_op jit(solution)/shard_map/ppermute | solution.py:416
  63.7 0.0 collective-permute-done.1.tr
  63.7 9.2 %level0.1 = (f32[64,256]{1,0:T(8,128)S(1)}, bf16[256,640]{1,0:T(8,128)(2,1)S(1)}, f32[512,128]{1,0:T(8,128)S(1)}, f32[512,128]{1,0:T(8,128)S(1)}) custom-call(s32[8]{0:T(128)S(1)} %stack.43.sc, s32[3,64]{1,0:T(4,128)S(1)} %pad_add_fusion.maps_s.maps_v, f32[2,4,192,128]{3,2,1,0:T(8,128)S(1)} %bitcast.35, f32[2,4,192,128]{3,2,1,0:T(8,128)S(1)} %bitcast.33, ...), custom_call_target="tpu_custom_call" | custom-call | flops 1000000000 | bytes 4000000 | tf_op jit(solution)/shard_map/level0/pallas_call | solution.py:481
  72.9 2.2 %collective-permute-start.2 = (bf16[256,640]{1,0:T(8,128)(2,1)S(1)}, bf16[256,640]{1,0:T(8,128)(2,1)S(1)}, u32[]{:S(2)}, u32[]{:S(2)}) collective-permute-start(bf16[256,640]{1,0:T(8,128)(2,1)S(1)} %get-tuple-element.30.v0), channel_id=1, source_target_pairs={{0,128},{64,192},{128,0},{192,64},{256,384},{320,448},{384,256},{4... | collective-permute-start | bytes 983048 | tf_op jit(solution)/shard_map/ppermute | solution.py:416
  75.1 8.3 %collective-permute-done.2.v0s = bf16[256,640]{1,0:T(8,128)(2,1)S(1)} collective-permute-done((bf16[256,640]{1,0:T(8,128)(2,1)S(1)}, bf16[256,640]{1,0:T(8,128)(2,1)S(1)}, u32[]{:S(2)}, u32[]{:S(2)}) %collective-permute-start.2) | collective-permute-done | bytes 327712 | tf_op jit(solution)/shard_map/ppermute | solution.py:416
  83.5 2.1 %collective-permute-start.3 = (f32[512,128]{1,0:T(8,128)S(1)}, f32[512,128]{1,0:T(8,128)S(1)}, u32[]{:S(2)}, u32[]{:S(2)}) collective-permute-start(f32[512,128]{1,0:T(8,128)S(1)} %get-tuple-element.35), channel_id=1, source_target_pairs={{0,128},{64,192},{128,0},{192,64},{256,384},{320,448},{384,256},{4... | collective-permute-start | bytes 786440 | tf_op jit(solution)/shard_map/ppermute | solution.py:416
  85.6 0.0 collective-permute-done.cross
  85.7 4.0 %all-gather.3 = f32[1536,128]{1,0:T(8,128)S(1)} all-gather(f32[768,128]{1,0:T(8,128)S(1)} %slice.34), channel_id=5, replica_groups={{0,64},{128,192},{256,320},{384,448},{1,65},{129,193},{257,321},{385,44..., dimensions={0}, use_global_device_ids=true | all-gather | bytes 1179648 | tf_op jit(solution)/shard_map/all_gather | solution.py:491
  89.6 9.8 %level1.1 = (f32[64,256]{1,0:T(8,128)S(1)}, f32[256,512]{1,0:T(8,128)S(1)}, f32[128,512]{1,0:T(8,128)S(1)}) custom-call(s32[8]{0:T(128)S(1)} %stack.43.sc, s32[3,64]{1,0:T(4,128)S(1)} %pad_add_fusion.maps_s.maps_v, f32[2,4,192,128]{3,2,1,0:T(8,128)S(1)} %bitcast.36, f32[2,4,192,128]{3,2,1,0:T(8,128)S(1)} %bitcast.34, ...), custom_call_target="tpu_custom_call" | custom-call | flops 1000000000 | bytes 4000000 | tf_op jit(solution)/shard_map/level1/pallas_call | solution.py:492
  99.4 0.0 collective-permute-done.3.tr
  99.4 4.7 %collective-permute-start.4 = (f32[128,512]{1,0:T(8,128)S(1)}, f32[128,512]{1,0:T(8,128)S(1)}, u32[]{:S(2)}, u32[]{:S(2)}) collective-permute-start(f32[128,512]{1,0:T(8,128)S(1)} %get-tuple-element.36), channel_id=1, source_target_pairs={{0,256},{64,320},{128,384},{192,448},{256,0},{320,64},{384,128},{4... | collective-permute-start | bytes 786440 | tf_op jit(solution)/shard_map/ppermute | solution.py:416
  104.1 6.3 %collective-permute-done.4 = f32[128,512]{1,0:T(8,128)S(1)} collective-permute-done((f32[128,512]{1,0:T(8,128)S(1)}, f32[128,512]{1,0:T(8,128)S(1)}, u32[]{:S(2)}, u32[]{:S(2)}) %collective-permute-start.4) | collective-permute-done | bytes 262176 | tf_op jit(solution)/shard_map/ppermute | solution.py:416
  110.3 3.0 %all-gather.4 = f32[256,512]{1,0:T(8,128)S(1)} all-gather(f32[128,512]{1,0:T(8,128)S(1)} %collective-permute-done.4), channel_id=6, replica_groups={{0,64},{128,192},{256,320},{384,448},{1,65},{129,193},{257,321},{385,44..., dimensions={0}, use_global_device_ids=true | all-gather | bytes 786432 | tf_op jit(solution)/shard_map/all_gather | solution.py:501
  113.3 9.8 %level2.1 = (f32[3,64,256]{2,1,0:T(8,128)}, bf16[8,112,128]{2,1,0:T(8,128)(2,1)S(1)}, bf16[2,1792,128]{2,1,0:T(8,128)(2,1)S(1)}, f32[256,128]{1,0:T(8,128)S(1)}, f32[256,128]{1,0:T(8,128)S(1)}) custom-call(s32[8]{0:T(128)S(1)} %stack.43.sc, f32[256,512]{1,0:T(8,128)S(1)} %get-tuple-element.33.d, f32[2,128,512]{2,1,0:T(8,128)S(1)} %bitcast.39, ...), custom_call_target="tpu_custom_call" | custom-call | flops 1000000000 | bytes 4000000 | tf_op jit(solution)/shard_map/level2/pallas_call | solution.py:502
  123.2 20.7 %all_to_all.25 = bf16[8,112,128]{2,1,0:T(8,128)(2,1)S(1)} all-to-all(bf16[8,112,128]{2,1,0:T(8,128)(2,1)S(1)} %get-tuple-element.44), channel_id=1, replica_groups={{0,8,16,24,32,40,48,56},{1,9,17,25,33,41,49,57},{2,10,18,26,34,42,50,58..., dimensions={0} | all-to-all | bytes 458752 | tf_op jit(solution)/shard_map/all_to_all | solution.py:420
  143.9 1.5 broadcast_in_dim.23
  145.3 3.6 %all-to-all-start.3 = ((bf16[8,896,128]{2,1,0:T(8,128)(2,1)}), bf16[8,896,128]{2,1,0:T(8,128)(2,1)S(1)}, u32[]{:S(2)}, u32[]{:S(2)}) async-start(bf16[8,896,128]{2,1,0:T(8,128)(2,1)} %broadcast_in_dim.23), calls=%async_computation.3 | async-start | bytes 3670016 | tf_op jit(solution)/shard_map/all_to_all | solution.py:420
  148.9 4.4 %collective-permute-start.5 = (f32[256,128]{1,0:T(8,128)S(1)}, f32[256,128]{1,0:T(8,128)S(1)}, u32[]{:S(2)}, u32[]{:S(2)}) collective-permute-start(f32[256,128]{1,0:T(8,128)S(1)} %get-tuple-element.43), channel_id=1, source_target_pairs={{0,256},{64,320},{128,384},{192,448},{256,0},{320,64},{384,128},{4... | collective-permute-start | bytes 393224 | tf_op jit(solution)/shard_map/ppermute | solution.py:416
  153.4 2.8 %collective-permute-done.5.tr = f32[256,128]{1,0:T(8,128)S(1)} collective-permute-done((f32[256,128]{1,0:T(8,128)S(1)}, f32[256,128]{1,0:T(8,128)S(1)}, u32[]{:S(2)}, u32[]{:S(2)}) %collective-permute-start.5) | collective-permute-done | bytes 131104 | tf_op jit(solution)/shard_map/ppermute | solution.py:416
  156.2 15.3 %all-to-all-done.3 = bf16[8,896,128]{2,1,0:T(8,128)(2,1)S(1)} async-done(((bf16[8,896,128]{2,1,0:T(8,128)(2,1)}), bf16[8,896,128]{2,1,0:T(8,128)(2,1)S(1)}, u32[]{:S(2)}, u32[]{:S(2)}) %all-to-all-start.3) | async-done | bytes 1835040 | tf_op jit(solution)/shard_map/all_to_all | solution.py:420
  171.5 0.7 top.1
  172.2 15.3 %all-gather.5 = f32[1984,128]{1,0:T(8,128)S(1)} all-gather(f32[248,128]{1,0:T(8,128)S(1)} %top.1), channel_id=7, replica_groups=mesh['cube'=8,'front'=64] {'cube'}, dimensions={0}, use_global_device_ids=true | all-gather | bytes 1142784 | tf_op jit(solution)/shard_map/all_gather | solution.py:525
  187.5 2.5 %last.1 = f32[60,3840]{1,0:T(8,128)} custom-call(f32[8,248,128]{2,1,0:T(8,128)S(1)} %bitcast.32), custom_call_target="tpu_custom_call" | custom-call | flops 100000000 | bytes 4000000 | tf_op jit(solution)/shard_map/last/pallas_call | solution.py:526
  (6 shorter events, 0.2 us)
Async XLA Ops:
  0.6 2.2 %copy-start = (f32[7,64,256]{2,1,0:T(8,128)S(1)}, f32[7,64,256]{2,1,0:T(8,128)}, u32[]{:S(2)}) copy-start(f32[7,64,256]{2,1,0:T(8,128)} %entries.1) | copy-start | bytes 1376260
  38.4 12.7 %all-to-all-start.1 = ((f32[8,192,128]{2,1,0:T(8,128)}), f32[8,192,128]{2,1,0:T(8,128)S(1)}, u32[]{:S(2)}, u32[]{:S(2)}) async-start(f32[8,192,128]{2,1,0:T(8,128)} %broadcast_in_dim.20), calls=%async_computation.1 | async-start | bytes 1572864 | tf_op jit(solution)/shard_map/all_to_all | solution.py:420
  42.8 20.9 %collective-permute-start.1 = (f32[1024,128]{1,0:T(8,128)S(1)}, f32[1024,128]{1,0:T(8,128)S(1)}, u32[]{:S(2)}, u32[]{:S(2)}) collective-permute-start(f32[1024,128]{1,0:T(8,128)S(1)} %slice.27), channel_id=1, source_target_pairs={{0,64},{64,0},{128,192},{192,128},{256,320},{320,256},{384,448},{4... | collective-permute-start | bytes 1572872 | tf_op jit(solution)/shard_map/ppermute | solution.py:416
  60.5 25.1 %collective-permute-start = (f32[1024,128]{1,0:T(8,128)S(1)}, f32[1024,128]{1,0:T(8,128)S(1)}, u32[]{:S(2)}, u32[]{:S(2)}) collective-permute-start(f32[1024,128]{1,0:T(8,128)S(1)} %pad_maximum_fusion), channel_id=1, source_target_pairs={{0,128},{64,192},{128,0},{192,64},{256,384},{320,448},{384,256},{4... | collective-permute-start | bytes 1572872 | tf_op jit(solution)/shard_map/ppermute | solution.py:416
  72.9 10.5 %collective-permute-start.2 = (bf16[256,640]{1,0:T(8,128)(2,1)S(1)}, bf16[256,640]{1,0:T(8,128)(2,1)S(1)}, u32[]{:S(2)}, u32[]{:S(2)}) collective-permute-start(bf16[256,640]{1,0:T(8,128)(2,1)S(1)} %get-tuple-element.30.v0), channel_id=1, source_target_pairs={{0,128},{64,192},{128,0},{192,64},{256,384},{320,448},{384,256},{4... | collective-permute-start | bytes 983048 | tf_op jit(solution)/shard_map/ppermute | solution.py:416
  83.5 15.9 %collective-permute-start.3 = (f32[512,128]{1,0:T(8,128)S(1)}, f32[512,128]{1,0:T(8,128)S(1)}, u32[]{:S(2)}, u32[]{:S(2)}) collective-permute-start(f32[512,128]{1,0:T(8,128)S(1)} %get-tuple-element.35), channel_id=1, source_target_pairs={{0,128},{64,192},{128,0},{192,64},{256,384},{320,448},{384,256},{4... | collective-permute-start | bytes 786440 | tf_op jit(solution)/shard_map/ppermute | solution.py:416
  99.4 10.9 %collective-permute-start.4 = (f32[128,512]{1,0:T(8,128)S(1)}, f32[128,512]{1,0:T(8,128)S(1)}, u32[]{:S(2)}, u32[]{:S(2)}) collective-permute-start(f32[128,512]{1,0:T(8,128)S(1)} %get-tuple-element.36), channel_id=1, source_target_pairs={{0,256},{64,320},{128,384},{192,448},{256,0},{320,64},{384,128},{4... | collective-permute-start | bytes 786440 | tf_op jit(solution)/shard_map/ppermute | solution.py:416
  145.3 26.1 %all-to-all-start.3 = ((bf16[8,896,128]{2,1,0:T(8,128)(2,1)}), bf16[8,896,128]{2,1,0:T(8,128)(2,1)S(1)}, u32[]{:S(2)}, u32[]{:S(2)}) async-start(bf16[8,896,128]{2,1,0:T(8,128)(2,1)} %broadcast_in_dim.23), calls=%async_computation.3 | async-start | bytes 3670016 | tf_op jit(solution)/shard_map/all_to_all | solution.py:420
  148.9 7.2 %collective-permute-start.5 = (f32[256,128]{1,0:T(8,128)S(1)}, f32[256,128]{1,0:T(8,128)S(1)}, u32[]{:S(2)}, u32[]{:S(2)}) collective-permute-start(f32[256,128]{1,0:T(8,128)S(1)} %get-tuple-element.43), channel_id=1, source_target_pairs={{0,256},{64,320},{128,384},{192,448},{256,0},{320,64},{384,128},{4... | collective-permute-start | bytes 393224 | tf_op jit(solution)/shard_map/ppermute | solution.py:416

commit v6 on v5

--- a/solution.py
+++ b/solution.py
@@ -77,6 +77,7 @@
         lo = j0 // 128 * 128
         wide = width - lo
         tiles = [a_ref[j0 + 8 * t : j0 + 8 * t + 8, lo:width] for t in range(count)]
+        roots = []
         for g in range(count):
             c0 = j0 - lo + 8 * g
             cols = [
@@ -84,7 +85,11 @@
                 for k in range(8)
             ]
             for i in range(8):
-                inv = 1.0 / spread_over(cols[i][0][i : i + 1, :], tile)
+                pivot = spread_over(cols[i][0][i : i + 1, :], tile)
+                inv = 1.0 / pivot
+                r = lax.rsqrt(pivot)
+                r = r * (1.5 - 0.5 * pivot * r * r)
+                root = r if i == 0 else jnp.where(rid >= i, r, root)
                 scale = [c * inv for c in cols[i]]
                 scale[0] = jnp.where(rid > i, scale[0], 0.0)
                 for k in range(i + 1, 8):
@@ -100,16 +105,12 @@
                         ],
                         axis=1,
                     )
+            roots.append(root)
+        tiles = [
+            jnp.concatenate([x[:, q : q + 128] * r for q in range(0, wide, 128)], axis=1)
+            for x, r in zip(tiles, roots)
+        ]
         rows = jnp.concatenate(tiles, axis=0)
-        head = rows[:, 0:128]
-        diag = jnp.sum(
-            jnp.where(iota(head.shape, 1) == iota(head.shape, 0) + (j0 - lo), head, 0.0),
-            axis=1,
-            keepdims=True,
-        )
-        root = lax.rsqrt(diag)
-        root = root * (1.5 - 0.5 * diag * root * root)
-        rows = rows * root
         a_ref[j0 : j0 + BLK, lo:width] = rows
         r0 = j0 + BLK
         if r0 < PAN:
@@ -313,11 +314,7 @@
     half_ref[...] = d_ref[pl.ds(first, 128), :]
 
 
-def level2_kernel(
-    sc, d, ds, f0, f1, tk, tr, f_ref, send_ref, vw_ref, tk_ref, ts_ref, a
-):
-    tk_ref[...] = tk[0:256, :] + tr[0:256, :]
-    ts_ref[...] = tk[256:512, :] + tr[256:512, :]
+def level2_kernel(sc, d, ds, f0, f1, f_ref, send_ref, vw_ref, a):
     sib = jnp.concatenate([ds[0], ds[1]], axis=0)
     mine = d[...]
     sub = mine[:, 0:384] + sib[:, 0:384]
@@ -420,12 +417,21 @@
     return lax.all_to_all(value, "front", 0, 0, axis_index_groups=axis_groups, tiled=True)
 
 
+def far_gather(sent, rows):
+    return spread(sent.reshape(FAR * rows, sent.shape[-1]), FAR_GROUPS)
+
+
+def near_copies(got):
+    return jnp.broadcast_to(got[None], (NEAR,) + got.shape)
+
+
+def near_gather(copies):
+    shape = copies.shape
+    return spread(copies.reshape(shape[0] * shape[1], shape[2]), NEAR_GROUPS).reshape(shape)
+
+
 def gather_front(sent, rows):
-    lanes = sent.shape[-1]
-    got = spread(sent.reshape(FAR * rows, lanes), FAR_GROUPS)
-    copies = jnp.broadcast_to(got[None], (NEAR, FAR * rows, lanes))
-    got = spread(copies.reshape(NEAR * FAR * rows, lanes), NEAR_GROUPS)
-    return got.reshape(NEAR, FAR * rows, lanes)
+    return near_gather(near_copies(far_gather(sent, rows)))
 
 
 def on_device(leaf_blocks, front_entries, child_maps):
@@ -486,8 +492,7 @@
         flops=10**9,
         name="level0",
     )(sc, maps, ga, gb, x, t, tr)
-    v0s, ts = lax.optimization_barrier((crossed(v0, 2), ts))
-    tr = crossed(ts, 2)
+    v0s = crossed(v0, 2)
     more = lax.all_gather(cross[:768], "cube", axis_index_groups=CORE_GROUPS, axis=0)
     f1, d1, half = call(
         level1_kernel,
@@ -497,24 +502,25 @@
         flops=10**9,
         name="level1",
     )(sc, maps, ga, gb, xp, cross, more, v0, v0s)
-    half, tr = lax.optimization_barrier((half, tr))
     d1s = lax.all_gather(crossed(half, 4), "cube", axis_index_groups=CORE_GROUPS, axis=0)
-    factors, thick, vw, tk, ts = call(
+    factors, thick, vw = call(
         level2_kernel,
-        [SMEM] + [VMEM] * 6,
+        [SMEM] + [VMEM] * 4,
         [
             ((3, WIDTH, PAN), F32),
             ((FAR, 112, 128), BF16),
             ((2, 7 * PAN, 128), BF16),
-            ((256, 128), F32),
-            ((256, 128), F32),
         ],
         [pltpu.VMEM((PAN, 384), F32)],
         flops=10**9,
         name="level2",
-    )(sc, d1, d1s, f0, f1, tk, tr)
+    )(sc, d1, d1s, f0, f1)
+    thick = far_gather(thick, 112)
+    thick, ts = lax.optimization_barrier((near_copies(thick), ts))
+    thick = near_gather(thick).reshape(NEAR, FAR, 112, 128)
+    tr = crossed(ts, 2)
+    tk, ts = tk[:256] + tr[:256], tk[256:] + tr[256:]
     tr = crossed(ts, 4)
-    thick = gather_front(thick, 112).reshape(NEAR, FAR, 112, 128)
     (piece,) = call(
         top_kernel,
         [VMEM] * 4,

time: 191 us -> 182 us (0.953)
  waiting for transfers between devices: 35.7 us -> 27.4 us
    all_to_all x2, waiting for transfers between devices: 18.3 us -> 9.75 us  [spread(): lax.all_to_all(value, 'front', 0, 0, axis_index_groups=axis_groups, tiled...]
  transfers between devices with their start and end apart: 8 -> 8, of which waited for: 5 -> 7; matrix products, arithmetic and copies ran while one was open for 0% -> 0% of each run, Pallas kernels for 10% -> 5%
where the time goes in v6:
time: 182 us
  blocking collectives  84 us (46%)
  Pallas kernels  34.5 us (19%)
  starting transfers between devices  30.2 us (17%)
  waiting for transfers between devices  27.4 us (15%)
  local copies, waits for them, and re-layouts  4.73 us (3%)
    all_to_all x2, blocking collectives, spread(): lax.all_to_all(value, 'front', 0, 0, axis_index_groups=axis_groups, tiled...  42 us
    ppermute x6, starting transfers between devices, crossed(): return lax.ppermute(value, 'cube', [(c, c ^ mask) for c in range(8)])  22.1 us
    ppermute x6, waiting for transfers between devices, crossed(): return lax.ppermute(value, 'cube', [(c, c ^ mask) for c in range(8)])  17.7 us
    all_gather x1, blocking collectives, on_device(): pieces = lax.all_gather(piece, 'cube', axis=0)  16.5 us
    all_to_all x2, waiting for transfers between devices, spread(): lax.all_to_all(value, 'front', 0, 0, axis_index_groups=axis_groups, tiled...  9.75 us
    all_gather x2, blocking collectives, on_device(): lax.all_gather(part, 'cube', axis_index_groups=CORE_GROUPS, axis=0)  9.29 us
    pallas_call x1, Pallas kernels, on_device(): call(level2_kernel, [SMEM] + [VMEM] * 4, [((3, WIDTH, PAN), F32), ((FAR,...  9.28 us
    pallas_call x1, Pallas kernels, on_device(): call(level1_kernel, [SMEM] + [VMEM] * 8, [((WIDTH, PAN), F32), ((PAN, 512...  9.22 us
  transfers between devices with their start and end apart: 8, of which 7 were waited for; matrix products, arithmetic and copies ran while one was open for 0% of the time, Pallas kernels for 5%

profile of v6, /device:TPU:1, one launch (start us, length us, event | category | flops | bytes accessed | tf_op | source)
XLA Modules:
  0.0 181.8 jit_solution(6006952534357056582)
XLA Ops:
  0.6 0.0 copy-start
  0.7 0.8 fusion
  1.4 1.2 copy.6.leaf
  2.7 0.1 pad_bitcast_fusion
  2.8 0.1 stack.43.sc
  2.9 0.0 copy-done
  2.9 3.2 %leaf.2 = (f32[3,128,128]{2,1,0:T(8,128)S(1)}, f32[3,128,128]{2,1,0:T(8,128)S(1)}, f32[2048,128]{1,0:T(8,128)S(1)}) custom-call(s32[8]{0:T(128)S(1)} %stack.43.sc, s32[3,64]{1,0:T(4,128)S(1)} %pad_add_fusion.maps_s.maps_v, s32[3,64]{1,0:T(4,128)S(1)} %pad_add_fusion.maps_s.maps_v, f32[1,60,3840]{2,1,0:T(8,128)S(1)} %copy.6.leaf, f32[7,64,256]{2,1,0:T(8,128)S(1)} %copy-done), custom_call_target="tpu_custom_call" | custom-call | flops 100000000 | bytes 4000000 | tf_op jit(solution)/shard_map/leaf/pallas_call | solution.py:459
  6.0 8.6 %all-gather = f32[6,128,128]{2,1,0:T(8,128)S(1)} all-gather(f32[3,128,128]{2,1,0:T(8,128)S(1)} %get-tuple-element.20), channel_id=2, replica_groups={{0,64},{128,192},{256,320},{384,448},{1,65},{129,193},{257,321},{385,44..., dimensions={0}, use_global_device_ids=true | all-gather | bytes 589824 | tf_op jit(solution)/shard_map/all_gather | solution.py:470
  14.6 0.9 pick.1
  15.6 21.9 %all_to_all.24 = f32[8,24,128]{2,1,0:T(8,128)S(1)} all-to-all(f32[8,24,128]{2,1,0:T(8,128)S(1)} %get-tuple-element.22), channel_id=1, replica_groups={{0,8,16,24,32,40,48,56},{1,9,17,25,33,41,49,57},{2,10,18,26,34,42,50,58..., dimensions={0} | all-to-all | bytes 196608 | tf_op jit(solution)/shard_map/all_to_all | solution.py:417
  37.4 0.9 broadcast_in_dim.20
  38.4 4.4 %all-to-all-start.1 = ((f32[8,192,128]{2,1,0:T(8,128)}), f32[8,192,128]{2,1,0:T(8,128)S(1)}, u32[]{:S(2)}, u32[]{:S(2)}) async-start(f32[8,192,128]{2,1,0:T(8,128)} %broadcast_in_dim.20), calls=%async_computation.1 | async-start | bytes 1572864 | tf_op jit(solution)/shard_map/all_to_all | solution.py:417
  42.8 5.3 %collective-permute-start.1 = (f32[1024,128]{1,0:T(8,128)S(1)}, f32[1024,128]{1,0:T(8,128)S(1)}, u32[]{:S(2)}, u32[]{:S(2)}) collective-permute-start(f32[1024,128]{1,0:T(8,128)S(1)} %slice.39), channel_id=1, source_target_pairs={{0,64},{64,0},{128,192},{192,128},{256,320},{320,256},{384,448},{4... | collective-permute-start | bytes 1572872 | tf_op jit(solution)/shard_map/ppermute | solution.py:413
  48.1 3.0 %all-to-all-done.1 = f32[8,192,128]{2,1,0:T(8,128)S(1)} async-done(((f32[8,192,128]{2,1,0:T(8,128)}), f32[8,192,128]{2,1,0:T(8,128)S(1)}, u32[]{:S(2)}, u32[]{:S(2)}) %all-to-all-start.1) | async-done | bytes 786464 | tf_op jit(solution)/shard_map/all_to_all | solution.py:417
  51.1 0.1 fusion.3
  51.2 6.9 %all-gather.1 = f32[8,192,128]{2,1,0:T(8,128)S(1)} all-gather(f32[4,192,128]{2,1,0:T(8,128)S(1)} %get-tuple-element.39), channel_id=3, replica_groups={{0,64},{128,192},{256,320},{384,448},{1,65},{129,193},{257,321},{385,44..., dimensions={0}, use_global_device_ids=true | all-gather | bytes 1179648 | tf_op jit(solution)/shard_map/all_gather | solution.py:479
  58.1 2.4 %all-gather.2 = f32[8,192,128]{2,1,0:T(8,128)S(1)} all-gather(f32[4,192,128]{2,1,0:T(8,128)S(1)} %get-tuple-element.38), channel_id=4, replica_groups={{0,64},{128,192},{256,320},{384,448},{1,65},{129,193},{257,321},{385,44..., dimensions={0}, use_global_device_ids=true | all-gather | bytes 1179648 | tf_op jit(solution)/shard_map/all_gather | solution.py:479
  60.5 3.1 %collective-permute-start = (f32[1024,128]{1,0:T(8,128)S(1)}, f32[1024,128]{1,0:T(8,128)S(1)}, u32[]{:S(2)}, u32[]{:S(2)}) collective-permute-start(f32[1024,128]{1,0:T(8,128)S(1)} %pad_maximum_fusion), channel_id=1, source_target_pairs={{0,128},{64,192},{128,0},{192,64},{256,384},{320,448},{384,256},{4... | collective-permute-start | bytes 1572872 | tf_op jit(solution)/shard_map/ppermute | solution.py:413
  63.7 0.0 collective-permute-done.1.tr
  63.7 8.8 %level0.1 = (f32[64,256]{1,0:T(8,128)S(1)}, bf16[256,640]{1,0:T(8,128)(2,1)S(1)}, f32[512,128]{1,0:T(8,128)S(1)}, f32[512,128]{1,0:T(8,128)S(1)}) custom-call(s32[8]{0:T(128)S(1)} %stack.43.sc, s32[3,64]{1,0:T(4,128)S(1)} %pad_add_fusion.maps_s.maps_v, f32[2,4,192,128]{3,2,1,0:T(8,128)S(1)} %bitcast.33, f32[2,4,192,128]{3,2,1,0:T(8,128)S(1)} %bitcast.35, ...), custom_call_target="tpu_custom_call" | custom-call | flops 1000000000 | bytes 4000000 | tf_op jit(solution)/shard_map/level0/pallas_call | solution.py:487
  72.5 2.2 %collective-permute-start.2 = (bf16[256,640]{1,0:T(8,128)(2,1)S(1)}, bf16[256,640]{1,0:T(8,128)(2,1)S(1)}, u32[]{:S(2)}, u32[]{:S(2)}) collective-permute-start(bf16[256,640]{1,0:T(8,128)(2,1)S(1)} %get-tuple-element.26.v0), channel_id=1, source_target_pairs={{0,128},{64,192},{128,0},{192,64},{256,384},{320,448},{384,256},{4... | collective-permute-start | bytes 983048 | tf_op jit(solution)/shard_map/ppermute | solution.py:413
  74.6 0.9 collective-permute-done.cross
  75.6 3.4 %all-gather.3 = f32[1536,128]{1,0:T(8,128)S(1)} all-gather(f32[768,128]{1,0:T(8,128)S(1)} %slice.50), channel_id=5, replica_groups={{0,64},{128,192},{256,320},{384,448},{1,65},{129,193},{257,321},{385,44..., dimensions={0}, use_global_device_ids=true | all-gather | bytes 1179648 | tf_op jit(solution)/shard_map/all_gather | solution.py:496
  79.0 4.0 %collective-permute-done.2.v0s = bf16[256,640]{1,0:T(8,128)(2,1)S(1)} collective-permute-done((bf16[256,640]{1,0:T(8,128)(2,1)S(1)}, bf16[256,640]{1,0:T(8,128)(2,1)S(1)}, u32[]{:S(2)}, u32[]{:S(2)}) %collective-permute-start.2) | collective-permute-done | bytes 327712 | tf_op jit(solution)/shard_map/ppermute | solution.py:413
  83.0 9.2 %level1.1 = (f32[64,256]{1,0:T(8,128)S(1)}, f32[256,512]{1,0:T(8,128)S(1)}, f32[128,512]{1,0:T(8,128)S(1)}) custom-call(s32[8]{0:T(128)S(1)} %stack.43.sc, s32[3,64]{1,0:T(4,128)S(1)} %pad_add_fusion.maps_s.maps_v, f32[2,4,192,128]{3,2,1,0:T(8,128)S(1)} %bitcast.34, f32[2,4,192,128]{3,2,1,0:T(8,128)S(1)} %bitcast.36, ...), custom_call_target="tpu_custom_call" | custom-call | flops 1000000000 | bytes 4000000 | tf_op jit(solution)/shard_map/level1/pallas_call | solution.py:497
  92.2 4.3 %collective-permute-start.3 = (f32[128,512]{1,0:T(8,128)S(1)}, f32[128,512]{1,0:T(8,128)S(1)}, u32[]{:S(2)}, u32[]{:S(2)}) collective-permute-start(f32[128,512]{1,0:T(8,128)S(1)} %get-tuple-element.28), channel_id=1, source_target_pairs={{0,256},{64,320},{128,384},{192,448},{256,0},{320,64},{384,128},{4... | collective-permute-start | bytes 786440 | tf_op jit(solution)/shard_map/ppermute | solution.py:413
  96.6 5.3 %collective-permute-done.3 = f32[128,512]{1,0:T(8,128)S(1)} collective-permute-done((f32[128,512]{1,0:T(8,128)S(1)}, f32[128,512]{1,0:T(8,128)S(1)}, u32[]{:S(2)}, u32[]{:S(2)}) %collective-permute-start.3) | collective-permute-done | bytes 262176 | tf_op jit(solution)/shard_map/ppermute | solution.py:413
  101.9 4.2 %all-gather.4 = f32[256,512]{1,0:T(8,128)S(1)} all-gather(f32[128,512]{1,0:T(8,128)S(1)} %collective-permute-done.3), channel_id=6, replica_groups={{0,64},{128,192},{256,320},{384,448},{1,65},{129,193},{257,321},{385,44..., dimensions={0}, use_global_device_ids=true | all-gather | bytes 786432 | tf_op jit(solution)/shard_map/all_gather | solution.py:505
  106.1 9.3 %level2.1 = (f32[3,64,256]{2,1,0:T(8,128)}, bf16[8,112,128]{2,1,0:T(8,128)(2,1)S(1)}, bf16[2,1792,128]{2,1,0:T(8,128)(2,1)S(1)}) custom-call(s32[8]{0:T(128)S(1)} %stack.43.sc, f32[256,512]{1,0:T(8,128)S(1)} %get-tuple-element.27.d, f32[2,128,512]{2,1,0:T(8,128)S(1)} %bitcast.39, f32[64,256]{1,0:T(8,128)S(1)} %get-tuple-element.29.f0, ...), custom_call_target="tpu_custom_call" | custom-call | flops 1000000000 | bytes 4000000 | tf_op jit(solution)/shard_map/level2/pallas_call | solution.py:506
  115.4 20.1 %all_to_all.25 = bf16[8,112,128]{2,1,0:T(8,128)(2,1)S(1)} all-to-all(bf16[8,112,128]{2,1,0:T(8,128)(2,1)S(1)} %get-tuple-element.33), channel_id=1, replica_groups={{0,8,16,24,32,40,48,56},{1,9,17,25,33,41,49,57},{2,10,18,26,34,42,50,58..., dimensions={0} | all-to-all | bytes 458752 | tf_op jit(solution)/shard_map/all_to_all | solution.py:417
  135.5 1.5 broadcast_in_dim.23
  137.0 3.8 %all-to-all-start.3 = ((bf16[8,896,128]{2,1,0:T(8,128)(2,1)}), bf16[8,896,128]{2,1,0:T(8,128)(2,1)S(1)}, u32[]{:S(2)}, u32[]{:S(2)}) async-start(bf16[8,896,128]{2,1,0:T(8,128)(2,1)} %broadcast_in_dim.23), calls=%async_computation.3 | async-start | bytes 3670016 | tf_op jit(solution)/shard_map/all_to_all | solution.py:417
  140.8 2.7 %collective-permute-start.4 = (f32[512,128]{1,0:T(8,128)S(1)}, f32[512,128]{1,0:T(8,128)S(1)}, u32[]{:S(2)}, u32[]{:S(2)}) collective-permute-start(f32[512,128]{1,0:T(8,128)S(1)} %get-tuple-element.35), channel_id=1, source_target_pairs={{0,128},{64,192},{128,0},{192,64},{256,384},{320,448},{384,256},{4... | collective-permute-start | bytes 786440 | tf_op jit(solution)/shard_map/ppermute | solution.py:413
  143.4 4.4 %collective-permute-done.4 = f32[512,128]{1,0:T(8,128)S(1)} collective-permute-done((f32[512,128]{1,0:T(8,128)S(1)}, f32[512,128]{1,0:T(8,128)S(1)}, u32[]{:S(2)}, u32[]{:S(2)}) %collective-permute-start.4) | collective-permute-done | bytes 262176 | tf_op jit(solution)/shard_map/ppermute | solution.py:413
  147.9 4.5 %collective-permute-start.5 = (f32[256,128]{1,0:T(8,128)S(1)}, f32[256,128]{1,0:T(8,128)S(1)}, u32[]{:S(2)}, u32[]{:S(2)}) collective-permute-start(f32[256,128]{1,0:T(8,128)S(1)} %get-tuple-element.40), channel_id=1, source_target_pairs={{0,256},{64,320},{128,384},{192,448},{256,0},{320,64},{384,128},{4... | collective-permute-start | bytes 393224 | tf_op jit(solution)/shard_map/ppermute | solution.py:413
  152.4 3.0 %collective-permute-done.5.tr = f32[256,128]{1,0:T(8,128)S(1)} collective-permute-done((f32[256,128]{1,0:T(8,128)S(1)}, f32[256,128]{1,0:T(8,128)S(1)}, u32[]{:S(2)}, u32[]{:S(2)}) %collective-permute-start.5) | collective-permute-done | bytes 131104 | tf_op jit(solution)/shard_map/ppermute | solution.py:413
  155.4 6.7 %all-to-all-done.3 = bf16[8,896,128]{2,1,0:T(8,128)(2,1)S(1)} async-done(((bf16[8,896,128]{2,1,0:T(8,128)(2,1)}), bf16[8,896,128]{2,1,0:T(8,128)(2,1)S(1)}, u32[]{:S(2)}, u32[]{:S(2)}) %all-to-all-start.3) | async-done | bytes 1835040 | tf_op jit(solution)/shard_map/all_to_all | solution.py:417
  162.2 0.7 top.1
  162.9 16.5 %all-gather.5 = f32[1984,128]{1,0:T(8,128)S(1)} all-gather(f32[248,128]{1,0:T(8,128)S(1)} %top.1), channel_id=7, replica_groups=mesh['cube'=8,'front'=64] {'cube'}, dimensions={0}, use_global_device_ids=true | all-gather | bytes 1142784 | tf_op jit(solution)/shard_map/all_gather | solution.py:531
  179.4 2.5 %last.1 = f32[60,3840]{1,0:T(8,128)} custom-call(f32[8,248,128]{2,1,0:T(8,128)S(1)} %bitcast.32), custom_call_target="tpu_custom_call" | custom-call | flops 100000000 | bytes 4000000 | tf_op jit(solution)/shard_map/last/pallas_call | solution.py:532
  (7 shorter events, 0.2 us)
Async XLA Ops:
  0.6 2.2 %copy-start = (f32[7,64,256]{2,1,0:T(8,128)S(1)}, f32[7,64,256]{2,1,0:T(8,128)}, u32[]{:S(2)}) copy-start(f32[7,64,256]{2,1,0:T(8,128)} %entries.1) | copy-start | bytes 1376260
  38.4 12.7 %all-to-all-start.1 = ((f32[8,192,128]{2,1,0:T(8,128)}), f32[8,192,128]{2,1,0:T(8,128)S(1)}, u32[]{:S(2)}, u32[]{:S(2)}) async-start(f32[8,192,128]{2,1,0:T(8,128)} %broadcast_in_dim.20), calls=%async_computation.1 | async-start | bytes 1572864 | tf_op jit(solution)/shard_map/all_to_all | solution.py:417
  42.8 20.9 %collective-permute-start.1 = (f32[1024,128]{1,0:T(8,128)S(1)}, f32[1024,128]{1,0:T(8,128)S(1)}, u32[]{:S(2)}, u32[]{:S(2)}) collective-permute-start(f32[1024,128]{1,0:T(8,128)S(1)} %slice.39), channel_id=1, source_target_pairs={{0,64},{64,0},{128,192},{192,128},{256,320},{320,256},{384,448},{4... | collective-permute-start | bytes 1572872 | tf_op jit(solution)/shard_map/ppermute | solution.py:413
  60.5 15.0 %collective-permute-start = (f32[1024,128]{1,0:T(8,128)S(1)}, f32[1024,128]{1,0:T(8,128)S(1)}, u32[]{:S(2)}, u32[]{:S(2)}) collective-permute-start(f32[1024,128]{1,0:T(8,128)S(1)} %pad_maximum_fusion), channel_id=1, source_target_pairs={{0,128},{64,192},{128,0},{192,64},{256,384},{320,448},{384,256},{4... | collective-permute-start | bytes 1572872 | tf_op jit(solution)/shard_map/ppermute | solution.py:413
  72.5 10.5 %collective-permute-start.2 = (bf16[256,640]{1,0:T(8,128)(2,1)S(1)}, bf16[256,640]{1,0:T(8,128)(2,1)S(1)}, u32[]{:S(2)}, u32[]{:S(2)}) collective-permute-start(bf16[256,640]{1,0:T(8,128)(2,1)S(1)} %get-tuple-element.26.v0), channel_id=1, source_target_pairs={{0,128},{64,192},{128,0},{192,64},{256,384},{320,448},{384,256},{4... | collective-permute-start | bytes 983048 | tf_op jit(solution)/shard_map/ppermute | solution.py:413
  92.2 9.7 %collective-permute-start.3 = (f32[128,512]{1,0:T(8,128)S(1)}, f32[128,512]{1,0:T(8,128)S(1)}, u32[]{:S(2)}, u32[]{:S(2)}) collective-permute-start(f32[128,512]{1,0:T(8,128)S(1)} %get-tuple-element.28), channel_id=1, source_target_pairs={{0,256},{64,320},{128,384},{192,448},{256,0},{320,64},{384,128},{4... | collective-permute-start | bytes 786440 | tf_op jit(solution)/shard_map/ppermute | solution.py:413
  137.0 25.2 %all-to-all-start.3 = ((bf16[8,896,128]{2,1,0:T(8,128)(2,1)}), bf16[8,896,128]{2,1,0:T(8,128)(2,1)S(1)}, u32[]{:S(2)}, u32[]{:S(2)}) async-start(bf16[8,896,128]{2,1,0:T(8,128)(2,1)} %broadcast_in_dim.23), calls=%async_computation.3 | async-start | bytes 3670016 | tf_op jit(solution)/shard_map/all_to_all | solution.py:417
  140.8 7.1 %collective-permute-start.4 = (f32[512,128]{1,0:T(8,128)S(1)}, f32[512,128]{1,0:T(8,128)S(1)}, u32[]{:S(2)}, u32[]{:S(2)}) collective-permute-start(f32[512,128]{1,0:T(8,128)S(1)} %get-tuple-element.35), channel_id=1, source_target_pairs={{0,128},{64,192},{128,0},{192,64},{256,384},{320,448},{384,256},{4... | collective-permute-start | bytes 786440 | tf_op jit(solution)/shard_map/ppermute | solution.py:413
  147.9 7.5 %collective-permute-start.5 = (f32[256,128]{1,0:T(8,128)S(1)}, f32[256,128]{1,0:T(8,128)S(1)}, u32[]{:S(2)}, u32[]{:S(2)}) collective-permute-start(f32[256,128]{1,0:T(8,128)S(1)} %get-tuple-element.40), channel_id=1, source_target_pairs={{0,256},{64,320},{128,384},{192,448},{256,0},{320,64},{384,128},{4... | collective-permute-start | bytes 393224 | tf_op jit(solution)/shard_map/ppermute | solution.py:413

commit v7 on v6

--- a/solution.py
+++ b/solution.py
@@ -151,10 +151,11 @@
 
 
 def leaf_kernel(
-    sc, maps_s, maps_v, leaf, entries, e_ref, ent_ref, t_ref, big, inv
+    sc, child_s, child_v, leaf, entries, e_ref, ent_ref, t_ref, maps_ref, big, inv
 ):
     cube = sc[3]
     chunks = 3840 // 256
+    sides = [jnp.bitwise_and(jnp.right_shift(cube, h), 1) for h in range(3)]
 
     @pl.loop(0, 72)
     def _(k):
@@ -162,15 +163,22 @@
 
     @pl.loop(0, KEEP, unroll=12)
     def _(v):
-        a0 = maps_s[0, v]
-        a1 = maps_s[1, a0]
-        a2 = maps_s[2, jnp.maximum(a1, 0)]
+        a0 = child_s[sc[0], sides[0], v]
+        a1 = child_s[sc[1], sides[1], jnp.maximum(a0 - 4, 0)]
+        a2 = child_s[sc[2], sides[2], jnp.maximum(a1 - 4, 0)]
         code = jnp.where(a0 < 4, a0, jnp.where(a1 < 4, 4 + a1, 8 + a2))
         inv[code] = v
 
-    t0 = onehot_rows(maps_v[0:1, :])
-    t1 = compose(onehot_rows(maps_v[1:2, :]), t0)
-    t2 = compose(onehot_rows(maps_v[2:3, :]), t1)
+    none = jnp.full((1, 4), -1, jnp.int32)
+    rows = []
+    for h in range(3):
+        two = child_v[sc[h]]
+        row = jnp.where(sides[h] == 0, two[0:1, :], two[1:2, :])
+        rows.append(jnp.concatenate([row, none] if h == 0 else [none, row], axis=1))
+        maps_ref[h : h + 1, :] = rows[h]
+    t0 = onehot_rows(rows[0])
+    t1 = compose(onehot_rows(rows[1]), t0)
+    t2 = compose(onehot_rows(rows[2]), t1)
     tt = compose(tail_table(), t2)
     table = jnp.concatenate([tt, t0, t1, t2], axis=0).astype(F32)
     table = jnp.transpose(table).astype(BF16)
@@ -178,7 +186,9 @@
 
     pad = jnp.zeros((WIDTH - KEEP, 256), F32)
     for j in range(chunks):
-        block = leaf[0, :, j * 256 : (j + 1) * 256]
+        block = jnp.concatenate(
+            [leaf[pl.ds(2 * j + k, KEEP, stride=30), :] for k in range(2)], axis=1
+        )
         block = jnp.concatenate([block, pad], axis=0)
         parts = jnp.concatenate(split3(block), axis=0)
         turned = dot(parts, table, TN)
@@ -439,33 +449,24 @@
     cube = lax.axis_index("cube")
     core = cube & 1
     nodes = [jnp.right_shift(cube + 8, h + 1) for h in range(3)]
-    sides = [jnp.right_shift(cube, h) & 1 for h in range(3)]
     sc = jnp.stack(
         [n - 1 for n in nodes] + [cube, position, core, jnp.right_shift(cube, 2), cube * 0]
     ).astype(jnp.int32)
-    picked = [
-        lax.dynamic_slice(child_maps, (n - 1, s, 0), (1, 1, KEEP)).reshape(KEEP)
-        for n, s in zip(nodes, sides)
-    ]
-    none = jnp.full((4,), -1, jnp.int32)
-    maps = jnp.stack(
-        [
-            jnp.concatenate([picked[0], none]),
-            jnp.concatenate([none, picked[1]]),
-            jnp.concatenate([none, picked[2]]),
-        ]
-    )
-
-    e, ent, t = call(
+    e, ent, t, maps = call(
         leaf_kernel,
         [SMEM, SMEM, VMEM, VMEM, VMEM],
-        [((3, 128, 128), F32), ((3, 128, 128), F32), ((2048, 128), F32)],
+        [
+            ((3, 128, 128), F32),
+            ((3, 128, 128), F32),
+            ((2048, 128), F32),
+            ((3, WIDTH), jnp.int32),
+        ],
         [
             pltpu.VMEM((2, 3840, 128), F32),
             pltpu.SMEM((128,), jnp.int32),
         ],
         name="leaf",
-    )(sc, maps, maps, leaf_blocks, front_entries)
+    )(sc, child_maps, child_maps, leaf_blocks.reshape(KEEP * 30, 128), front_entries)
 
     both = lax.all_gather(e, "cube", axis_index_groups=CORE_GROUPS, axis=0)
     x, xp, sent = call(

time: 182 us -> 184 us (1.011)
  no operation moved by 1% of the time
where the time goes in v7:
time: 184 us; the launch traced here: 183 us
  blocking collectives  84.1 us (46%)
  Pallas kernels  34.9 us (19%)
  starting transfers between devices  30.7 us (17%)
  waiting for transfers between devices  26.8 us (15%)
  local copies, waits for them, and re-layouts  5.51 us (3%)
    all_to_all x2, blocking collectives, spread(): lax.all_to_all(value, 'front', 0, 0, axis_index_groups=axis_groups, tiled...  42 us
    ppermute x6, starting transfers between devices, crossed(): return lax.ppermute(value, 'cube', [(c, c ^ mask) for c in range(8)])  22.6 us
    ppermute x6, waiting for transfers between devices, crossed(): return lax.ppermute(value, 'cube', [(c, c ^ mask) for c in range(8)])  17.1 us
    all_gather x1, blocking collectives, on_device(): pieces = lax.all_gather(piece, 'cube', axis=0)  16.6 us
    all_to_all x2, waiting for transfers between devices, spread(): lax.all_to_all(value, 'front', 0, 0, axis_index_groups=axis_groups, tiled...  9.67 us
    all_gather x2, blocking collectives, on_device(): lax.all_gather(part, 'cube', axis_index_groups=CORE_GROUPS, axis=0)  9.29 us
    pallas_call x1, Pallas kernels, on_device(): call(level2_kernel, [SMEM] + [VMEM] * 4, [((3, WIDTH, PAN), F32), ((FAR,...  9.27 us
    pallas_call x1, Pallas kernels, on_device(): call(level1_kernel, [SMEM] + [VMEM] * 8, [((WIDTH, PAN), F32), ((PAN, 512...  9.23 us
  transfers between devices with their start and end apart: 8, of which 7 were waited for; matrix products, arithmetic and copies ran while one was open for 0% of the time, Pallas kernels for 5%

profile of v7, /device:TPU:1, one launch (start us, length us, event | category | flops | bytes accessed | tf_op | source)
XLA Modules:
  0.0 183.0 jit_solution(15152685574662765615)
XLA Ops:
  0.6 0.1 stack.31.sc
  0.7 0.0 copy-start
  0.7 1.2 copy-done
  1.9 0.0 copy-start.1
  1.9 1.0 copy-done.1
  2.9 0.0 copy-start.2
  2.9 0.7 copy-done.2
  3.6 3.5 %leaf.1 = (f32[3,128,128]{2,1,0:T(8,128)S(1)}, f32[3,128,128]{2,1,0:T(8,128)S(1)}, f32[2048,128]{1,0:T(8,128)S(1)}, s32[3,64]{1,0:T(4,128)S(1)}) custom-call(s32[8]{0:T(128)S(1)} %stack.31.sc, s32[7,2,60]{2,1,0:T(2,128)S(1)} %copy-done.2, s32[7,2,60]{2,1,0:T(2,128)S(1)} %copy-done.2, f32[1800,128]{1,0:T(8,128)S(1)} %bitcast.27, f32[7,64,256]{2,1,0:T(8,128)S(1)} %copy-done.1), custom_call_target="tpu_custom_call" | custom-call | flops 100000000 | bytes 4000000 | tf_op jit(solution)/shard_map/leaf/pallas_call | solution.py:455
  7.2 8.6 %all-gather = f32[6,128,128]{2,1,0:T(8,128)S(1)} all-gather(f32[3,128,128]{2,1,0:T(8,128)S(1)} %get-tuple-element.22), channel_id=2, replica_groups={{0,64},{128,192},{256,320},{384,448},{1,65},{129,193},{257,321},{385,44..., dimensions={0}, use_global_device_ids=true | all-gather | bytes 589824 | tf_op jit(solution)/shard_map/all_gather | solution.py:471
  15.8 0.9 pick.1
  16.7 21.9 %all_to_all.24 = f32[8,24,128]{2,1,0:T(8,128)S(1)} all-to-all(f32[8,24,128]{2,1,0:T(8,128)S(1)} %get-tuple-element.24), channel_id=1, replica_groups={{0,8,16,24,32,40,48,56},{1,9,17,25,33,41,49,57},{2,10,18,26,34,42,50,58..., dimensions={0} | all-to-all | bytes 196608 | tf_op jit(solution)/shard_map/all_to_all | solution.py:427
  38.6 0.9 broadcast_in_dim.20
  39.5 4.4 %all-to-all-start.1 = ((f32[8,192,128]{2,1,0:T(8,128)}), f32[8,192,128]{2,1,0:T(8,128)S(1)}, u32[]{:S(2)}, u32[]{:S(2)}) async-start(f32[8,192,128]{2,1,0:T(8,128)} %broadcast_in_dim.20), calls=%async_computation.1 | async-start | bytes 1572864 | tf_op jit(solution)/shard_map/all_to_all | solution.py:427
  43.9 5.3 %collective-permute-start.1 = (f32[1024,128]{1,0:T(8,128)S(1)}, f32[1024,128]{1,0:T(8,128)S(1)}, u32[]{:S(2)}, u32[]{:S(2)}) collective-permute-start(f32[1024,128]{1,0:T(8,128)S(1)} %slice.39), channel_id=1, source_target_pairs={{0,64},{64,0},{128,192},{192,128},{256,320},{320,256},{384,448},{4... | collective-permute-start | bytes 1572872 | tf_op jit(solution)/shard_map/ppermute | solution.py:423
  49.2 3.0 %all-to-all-done.1 = f32[8,192,128]{2,1,0:T(8,128)S(1)} async-done(((f32[8,192,128]{2,1,0:T(8,128)}), f32[8,192,128]{2,1,0:T(8,128)S(1)}, u32[]{:S(2)}, u32[]{:S(2)}) %all-to-all-start.1) | async-done | bytes 786464 | tf_op jit(solution)/shard_map/all_to_all | solution.py:427
  52.2 0.1 fusion
  52.3 6.9 %all-gather.1 = f32[8,192,128]{2,1,0:T(8,128)S(1)} all-gather(f32[4,192,128]{2,1,0:T(8,128)S(1)} %get-tuple-element.41), channel_id=3, replica_groups={{0,64},{128,192},{256,320},{384,448},{1,65},{129,193},{257,321},{385,44..., dimensions={0}, use_global_device_ids=true | all-gather | bytes 1179648 | tf_op jit(solution)/shard_map/all_gather | solution.py:480
  59.2 2.4 %all-gather.2 = f32[8,192,128]{2,1,0:T(8,128)S(1)} all-gather(f32[4,192,128]{2,1,0:T(8,128)S(1)} %get-tuple-element.40), channel_id=4, replica_groups={{0,64},{128,192},{256,320},{384,448},{1,65},{129,193},{257,321},{385,44..., dimensions={0}, use_global_device_ids=true | all-gather | bytes 1179648 | tf_op jit(solution)/shard_map/all_gather | solution.py:480
  61.7 3.1 %collective-permute-start = (f32[1024,128]{1,0:T(8,128)S(1)}, f32[1024,128]{1,0:T(8,128)S(1)}, u32[]{:S(2)}, u32[]{:S(2)}) collective-permute-start(f32[1024,128]{1,0:T(8,128)S(1)} %pad_maximum_fusion), channel_id=1, source_target_pairs={{0,128},{64,192},{128,0},{192,64},{256,384},{320,448},{384,256},{4... | collective-permute-start | bytes 1572872 | tf_op jit(solution)/shard_map/ppermute | solution.py:423
  64.8 0.0 collective-permute-done.1.tr
  64.8 8.8 %level0.1 = (f32[64,256]{1,0:T(8,128)S(1)}, bf16[256,640]{1,0:T(8,128)(2,1)S(1)}, f32[512,128]{1,0:T(8,128)S(1)}, f32[512,128]{1,0:T(8,128)S(1)}) custom-call(s32[8]{0:T(128)S(1)} %stack.31.sc, s32[3,64]{1,0:T(4,128)S(1)} %get-tuple-element.21.maps_v, f32[2,4,192,128]{3,2,1,0:T(8,128)S(1)} %bitcast.22, f32[2,4,192,128]{3,2,1,0:T(8,128)S(1)} %bitcast.24, ...), custom_call_target="tpu_custom_call" | custom-call | flops 1000000000 | bytes 4000000 | tf_op jit(solution)/shard_map/level0/pallas_call | solution.py:488
  73.6 2.2 %collective-permute-start.2 = (bf16[256,640]{1,0:T(8,128)(2,1)S(1)}, bf16[256,640]{1,0:T(8,128)(2,1)S(1)}, u32[]{:S(2)}, u32[]{:S(2)}) collective-permute-start(bf16[256,640]{1,0:T(8,128)(2,1)S(1)} %get-tuple-element.28.v0), channel_id=1, source_target_pairs={{0,128},{64,192},{128,0},{192,64},{256,384},{320,448},{384,256},{4... | collective-permute-start | bytes 983048 | tf_op jit(solution)/shard_map/ppermute | solution.py:423
  75.8 0.9 collective-permute-done.cross
  76.7 3.4 %all-gather.3 = f32[1536,128]{1,0:T(8,128)S(1)} all-gather(f32[768,128]{1,0:T(8,128)S(1)} %slice.50), channel_id=5, replica_groups={{0,64},{128,192},{256,320},{384,448},{1,65},{129,193},{257,321},{385,44..., dimensions={0}, use_global_device_ids=true | all-gather | bytes 1179648 | tf_op jit(solution)/shard_map/all_gather | solution.py:497
  80.1 4.0 %collective-permute-done.2.v0s = bf16[256,640]{1,0:T(8,128)(2,1)S(1)} collective-permute-done((bf16[256,640]{1,0:T(8,128)(2,1)S(1)}, bf16[256,640]{1,0:T(8,128)(2,1)S(1)}, u32[]{:S(2)}, u32[]{:S(2)}) %collective-permute-start.2) | collective-permute-done | bytes 327712 | tf_op jit(solution)/shard_map/ppermute | solution.py:423
  84.1 9.2 %level1.1 = (f32[64,256]{1,0:T(8,128)S(1)}, f32[256,512]{1,0:T(8,128)S(1)}, f32[128,512]{1,0:T(8,128)S(1)}) custom-call(s32[8]{0:T(128)S(1)} %stack.31.sc, s32[3,64]{1,0:T(4,128)S(1)} %get-tuple-element.21.maps_v, f32[2,4,192,128]{3,2,1,0:T(8,128)S(1)} %bitcast.23, f32[2,4,192,128]{3,2,1,0:T(8,128)S(1)} %bitcast.25, ...), custom_call_target="tpu_custom_call" | custom-call | flops 1000000000 | bytes 4000000 | tf_op jit(solution)/shard_map/level1/pallas_call | solution.py:498
  93.3 4.4 %collective-permute-start.3 = (f32[128,512]{1,0:T(8,128)S(1)}, f32[128,512]{1,0:T(8,128)S(1)}, u32[]{:S(2)}, u32[]{:S(2)}) collective-permute-start(f32[128,512]{1,0:T(8,128)S(1)} %get-tuple-element.30), channel_id=1, source_target_pairs={{0,256},{64,320},{128,384},{192,448},{256,0},{320,64},{384,128},{4... | collective-permute-start | bytes 786440 | tf_op jit(solution)/shard_map/ppermute | solution.py:423
  97.7 5.3 %collective-permute-done.3 = f32[128,512]{1,0:T(8,128)S(1)} collective-permute-done((f32[128,512]{1,0:T(8,128)S(1)}, f32[128,512]{1,0:T(8,128)S(1)}, u32[]{:S(2)}, u32[]{:S(2)}) %collective-permute-start.3) | collective-permute-done | bytes 262176 | tf_op jit(solution)/shard_map/ppermute | solution.py:423
  103.0 4.2 %all-gather.4 = f32[256,512]{1,0:T(8,128)S(1)} all-gather(f32[128,512]{1,0:T(8,128)S(1)} %collective-permute-done.3), channel_id=6, replica_groups={{0,64},{128,192},{256,320},{384,448},{1,65},{129,193},{257,321},{385,44..., dimensions={0}, use_global_device_ids=true | all-gather | bytes 786432 | tf_op jit(solution)/shard_map/all_gather | solution.py:506
  107.2 9.3 %level2.1 = (f32[3,64,256]{2,1,0:T(8,128)}, bf16[8,112,128]{2,1,0:T(8,128)(2,1)S(1)}, bf16[2,1792,128]{2,1,0:T(8,128)(2,1)S(1)}) custom-call(s32[8]{0:T(128)S(1)} %stack.31.sc, f32[256,512]{1,0:T(8,128)S(1)} %get-tuple-element.29.d, f32[2,128,512]{2,1,0:T(8,128)S(1)} %bitcast.29, f32[64,256]{1,0:T(8,128)S(1)} %get-tuple-element.31.f0, ...), custom_call_target="tpu_custom_call" | custom-call | flops 1000000000 | bytes 4000000 | tf_op jit(solution)/shard_map/level2/pallas_call | solution.py:507
  116.5 20.1 %all_to_all.25 = bf16[8,112,128]{2,1,0:T(8,128)(2,1)S(1)} all-to-all(bf16[8,112,128]{2,1,0:T(8,128)(2,1)S(1)} %get-tuple-element.35), channel_id=1, replica_groups={{0,8,16,24,32,40,48,56},{1,9,17,25,33,41,49,57},{2,10,18,26,34,42,50,58..., dimensions={0} | all-to-all | bytes 458752 | tf_op jit(solution)/shard_map/all_to_all | solution.py:427
  136.6 1.5 broadcast_in_dim.23
  138.1 3.7 %all-to-all-start.3 = ((bf16[8,896,128]{2,1,0:T(8,128)(2,1)}), bf16[8,896,128]{2,1,0:T(8,128)(2,1)S(1)}, u32[]{:S(2)}, u32[]{:S(2)}) async-start(bf16[8,896,128]{2,1,0:T(8,128)(2,1)} %broadcast_in_dim.23), calls=%async_computation.3 | async-start | bytes 3670016 | tf_op jit(solution)/shard_map/all_to_all | solution.py:427
  141.9 3.1 %collective-permute-start.4 = (f32[512,128]{1,0:T(8,128)S(1)}, f32[512,128]{1,0:T(8,128)S(1)}, u32[]{:S(2)}, u32[]{:S(2)}) collective-permute-start(f32[512,128]{1,0:T(8,128)S(1)} %get-tuple-element.37), channel_id=1, source_target_pairs={{0,128},{64,192},{128,0},{192,64},{256,384},{320,448},{384,256},{4... | collective-permute-start | bytes 786440 | tf_op jit(solution)/shard_map/ppermute | solution.py:423
  145.0 4.0 %collective-permute-done.4 = f32[512,128]{1,0:T(8,128)S(1)} collective-permute-done((f32[512,128]{1,0:T(8,128)S(1)}, f32[512,128]{1,0:T(8,128)S(1)}, u32[]{:S(2)}, u32[]{:S(2)}) %collective-permute-start.4) | collective-permute-done | bytes 262176 | tf_op jit(solution)/shard_map/ppermute | solution.py:423
  149.0 4.6 %collective-permute-start.5 = (f32[256,128]{1,0:T(8,128)S(1)}, f32[256,128]{1,0:T(8,128)S(1)}, u32[]{:S(2)}, u32[]{:S(2)}) collective-permute-start(f32[256,128]{1,0:T(8,128)S(1)} %get-tuple-element.42), channel_id=1, source_target_pairs={{0,256},{64,320},{128,384},{192,448},{256,0},{320,64},{384,128},{4... | collective-permute-start | bytes 393224 | tf_op jit(solution)/shard_map/ppermute | solution.py:423
  153.6 2.9 %collective-permute-done.5.tr = f32[256,128]{1,0:T(8,128)S(1)} collective-permute-done((f32[256,128]{1,0:T(8,128)S(1)}, f32[256,128]{1,0:T(8,128)S(1)}, u32[]{:S(2)}, u32[]{:S(2)}) %collective-permute-start.5) | collective-permute-done | bytes 131104 | tf_op jit(solution)/shard_map/ppermute | solution.py:423
  156.5 6.7 %all-to-all-done.3 = bf16[8,896,128]{2,1,0:T(8,128)(2,1)S(1)} async-done(((bf16[8,896,128]{2,1,0:T(8,128)(2,1)}), bf16[8,896,128]{2,1,0:T(8,128)(2,1)S(1)}, u32[]{:S(2)}, u32[]{:S(2)}) %all-to-all-start.3) | async-done | bytes 1835040 | tf_op jit(solution)/shard_map/all_to_all | solution.py:427
  163.2 0.7 top.1
  163.9 16.6 %all-gather.5 = f32[1984,128]{1,0:T(8,128)S(1)} all-gather(f32[248,128]{1,0:T(8,128)S(1)} %top.1), channel_id=7, replica_groups=mesh['cube'=8,'front'=64] {'cube'}, dimensions={0}, use_global_device_ids=true | all-gather | bytes 1142784 | tf_op jit(solution)/shard_map/all_gather | solution.py:532
  180.5 2.5 %last.1 = f32[60,3840]{1,0:T(8,128)} custom-call(f32[8,248,128]{2,1,0:T(8,128)S(1)} %bitcast.21), custom_call_target="tpu_custom_call" | custom-call | flops 100000000 | bytes 4000000 | tf_op jit(solution)/shard_map/last/pallas_call | solution.py:533
  (5 shorter events, 0.2 us)
Async XLA Ops:
  0.7 1.2 copy-start
  1.9 1.0 copy-start.1
  2.9 0.7 copy-start.2
  39.5 12.7 %all-to-all-start.1 = ((f32[8,192,128]{2,1,0:T(8,128)}), f32[8,192,128]{2,1,0:T(8,128)S(1)}, u32[]{:S(2)}, u32[]{:S(2)}) async-start(f32[8,192,128]{2,1,0:T(8,128)} %broadcast_in_dim.20), calls=%async_computation.1 | async-start | bytes 1572864 | tf_op jit(solution)/shard_map/all_to_all | solution.py:427
  43.9 20.9 %collective-permute-start.1 = (f32[1024,128]{1,0:T(8,128)S(1)}, f32[1024,128]{1,0:T(8,128)S(1)}, u32[]{:S(2)}, u32[]{:S(2)}) collective-permute-start(f32[1024,128]{1,0:T(8,128)S(1)} %slice.39), channel_id=1, source_target_pairs={{0,64},{64,0},{128,192},{192,128},{256,320},{320,256},{384,448},{4... | collective-permute-start | bytes 1572872 | tf_op jit(solution)/shard_map/ppermute | solution.py:423
  61.7 15.0 %collective-permute-start = (f32[1024,128]{1,0:T(8,128)S(1)}, f32[1024,128]{1,0:T(8,128)S(1)}, u32[]{:S(2)}, u32[]{:S(2)}) collective-permute-start(f32[1024,128]{1,0:T(8,128)S(1)} %pad_maximum_fusion), channel_id=1, source_target_pairs={{0,128},{64,192},{128,0},{192,64},{256,384},{320,448},{384,256},{4... | collective-permute-start | bytes 1572872 | tf_op jit(solution)/shard_map/ppermute | solution.py:423
  73.6 10.5 %collective-permute-start.2 = (bf16[256,640]{1,0:T(8,128)(2,1)S(1)}, bf16[256,640]{1,0:T(8,128)(2,1)S(1)}, u32[]{:S(2)}, u32[]{:S(2)}) collective-permute-start(bf16[256,640]{1,0:T(8,128)(2,1)S(1)} %get-tuple-element.28.v0), channel_id=1, source_target_pairs={{0,128},{64,192},{128,0},{192,64},{256,384},{320,448},{384,256},{4... | collective-permute-start | bytes 983048 | tf_op jit(solution)/shard_map/ppermute | solution.py:423
  93.3 9.7 %collective-permute-start.3 = (f32[128,512]{1,0:T(8,128)S(1)}, f32[128,512]{1,0:T(8,128)S(1)}, u32[]{:S(2)}, u32[]{:S(2)}) collective-permute-start(f32[128,512]{1,0:T(8,128)S(1)} %get-tuple-element.30), channel_id=1, source_target_pairs={{0,256},{64,320},{128,384},{192,448},{256,0},{320,64},{384,128},{4... | collective-permute-start | bytes 786440 | tf_op jit(solution)/shard_map/ppermute | solution.py:423
  138.1 25.1 %all-to-all-start.3 = ((bf16[8,896,128]{2,1,0:T(8,128)(2,1)}), bf16[8,896,128]{2,1,0:T(8,128)(2,1)S(1)}, u32[]{:S(2)}, u32[]{:S(2)}) async-start(bf16[8,896,128]{2,1,0:T(8,128)(2,1)} %broadcast_in_dim.23), calls=%async_computation.3 | async-start | bytes 3670016 | tf_op jit(solution)/shard_map/all_to_all | solution.py:427
  141.9 7.1 %collective-permute-start.4 = (f32[512,128]{1,0:T(8,128)S(1)}, f32[512,128]{1,0:T(8,128)S(1)}, u32[]{:S(2)}, u32[]{:S(2)}) collective-permute-start(f32[512,128]{1,0:T(8,128)S(1)} %get-tuple-element.37), channel_id=1, source_target_pairs={{0,128},{64,192},{128,0},{192,64},{256,384},{320,448},{384,256},{4... | collective-permute-start | bytes 786440 | tf_op jit(solution)/shard_map/ppermute | solution.py:423
  149.0 7.5 %collective-permute-start.5 = (f32[256,128]{1,0:T(8,128)S(1)}, f32[256,128]{1,0:T(8,128)S(1)}, u32[]{:S(2)}, u32[]{:S(2)}) collective-permute-start(f32[256,128]{1,0:T(8,128)S(1)} %get-tuple-element.42), channel_id=1, source_target_pairs={{0,256},{64,320},{128,384},{192,448},{256,0},{320,64},{384,128},{4... | collective-permute-start | bytes 393224 | tf_op jit(solution)/shard_map/ppermute | solution.py:423
